TPU v7x, 32 devices: a whole 2x2x4 slice. The times are simulated.
32 devices in a mesh: row: 2 (over x), col: 16 (over z, y, core).
Axes of the slice: x: 2, y: 2, z: 4, core: 2. Of those that a mesh axis runs over, the one named last changes fastest.
Arguments:
- tokens: bfloat16 [25216, 768], P(('row', 'col')), may hold values from -6 to 6
- keep_mask: int32 [128, 197], P(('row', 'col')), may hold values from 0 to 1, as said below
- w_qkv: bfloat16 [768, 2304], replicated, may hold values from -0.3125 to 0.3125
- w_out: bfloat16 [768, 768], replicated, may hold values from -0.3125 to 0.3125
- w_up: bfloat16 [768, 3072], replicated, may hold values from -0.4375 to 0.4375
- w_down: bfloat16 [3072, 768], replicated, may hold values from -0.109375 to 0.109375
- vectors: float32 [8, 768], replicated, may hold values from -3 to 3, as said below
- up_bias: float32 [3072], replicated, may hold values from -3 to 3
- w_proj: bfloat16 [768, 512], replicated, may hold values from -0.21875 to 0.21875
- texts: bfloat16 [128, 512], P(('row', 'col')), may hold values from -0.29882812 to 0.29882812
- pair_index: int32 [128], replicated, may hold values from 0 to 127, each once
- logit_scale: float32 [1], replicated, may hold values from 30 to 60
Outputs:
- loss: float32 [1], replicated
- token_grad: float32 [25216, 768], P(('row', 'col'))
- qkv_grad: float32 [768, 2304], P('col')
- out_grad: float32 [768, 768], P('col')
- up_grad: float32 [768, 3072], P('col')
- down_grad: float32 [3072, 768], P('col')
- vectors_grad: float32 [8, 768], P(None, 'col')
- up_bias_grad: float32 [3072], P('col')
- proj_grad: float32 [768, 512], P('col')
- text_grad: float32 [128, 512], P(('row', 'col'))
Inputs may be any that keep to these rules, and one draw needn't show every extreme that they name: `keep_mask`: column 0 of every row is 1; the number of kept tokens varies from image to image. `vectors`: rows 0 and 5 are gains, the others biases.
All inputs are finite; a program needn't handle non-finite values.
Results may differ from a plain program's by a relative error of at most 0.017.
Values may be sent and summed in bfloat16 or wider, within the bound.
A program may use at most 192 MiB of HBM per device.

v0:
```python
from functools import partial

import jax
import jax.numpy as jnp
from jax import lax
from jax.sharding import PartitionSpec as P

D = 768
HEADS = 12
HEAD_DIM = 64
SEQ = 197


HIGH = lax.Precision.HIGHEST


def norm_forward(values, gain, shift):
    mean_val = jnp.mean(values, axis=-1, keepdims=True)
    centred = values - mean_val
    inv_std = lax.rsqrt(jnp.mean(centred * centred, axis=-1, keepdims=True) + 1e-06)
    scaled = centred * inv_std
    return (scaled * gain + shift, scaled, inv_std)


def norm_backward(grad_in, scaled, inv_std, gain):
    weighted = grad_in * gain
    inner = weighted - jnp.mean(weighted, axis=-1, keepdims=True)
    inner = inner - scaled * jnp.mean(weighted * scaled, axis=-1, keepdims=True)
    return (inner * inv_std, jnp.sum(grad_in * scaled, axis=0), jnp.sum(grad_in, axis=0))


def per_device(
    tokens,
    keep_mask,
    w_qkv,
    w_out,
    w_up,
    w_down,
    vectors,
    up_bias,
    w_proj,
    texts,
    pair_index,
    logit_scale,
):
    images = keep_mask.shape[0]
    rows = tokens.shape[0]
    total_images = pair_index.shape[0]
    scale_qk = HEAD_DIM ** (-0.5)
    head_shape = (images, SEQ, HEADS, HEAD_DIM)
    inputs = tokens.astype(jnp.float32)
    keep_float = keep_mask.astype(jnp.float32)
    normed, scaled_one, inv_one = norm_forward(inputs, vectors[0], vectors[1])
    normed_b = normed.astype(jnp.bfloat16)
    projected = jnp.dot(normed_b, w_qkv, preferred_element_type=jnp.float32)
    queries = (projected[:, :D] + vectors[2]).astype(jnp.bfloat16).reshape(head_shape)
    key_rows = projected[:, D : 2 * D].astype(jnp.bfloat16).reshape(head_shape)
    value_rows = (projected[:, 2 * D :] + vectors[3]).astype(jnp.bfloat16).reshape(head_shape)
    raw = jnp.einsum("nqhd,nkhd->nhqk", queries, key_rows, preferred_element_type=jnp.float32)
    allowed = keep_mask[:, None, None, :] > 0
    scores = jnp.where(allowed, raw * scale_qk, -1e30)
    probs = jax.nn.softmax(scores, axis=-1)
    probs_b = probs.astype(jnp.bfloat16)
    attended = jnp.einsum(
        "nhqk,nkhd->nqhd", probs_b, value_rows, preferred_element_type=jnp.float32
    )
    attended = attended.reshape(rows, D).astype(jnp.bfloat16)
    resid = inputs + jnp.dot(attended, w_out, preferred_element_type=jnp.float32) + vectors[4]
    normed_two, scaled_two, inv_two = norm_forward(resid, vectors[5], vectors[6])
    normed_two_b = normed_two.astype(jnp.bfloat16)
    hidden = jnp.dot(normed_two_b, w_up, preferred_element_type=jnp.float32) + up_bias
    activ_b = jax.nn.gelu(hidden, approximate=False).astype(jnp.bfloat16)
    outputs = resid + jnp.dot(activ_b, w_down, preferred_element_type=jnp.float32) + vectors[7]
    counts = jnp.sum(keep_float, axis=1)
    pooled = (
        jnp.sum(outputs.reshape(images, SEQ, D) * keep_float[:, :, None], axis=1) / counts[:, None]
    )
    proj_float = w_proj.astype(jnp.float32)
    latent = jnp.dot(pooled, proj_float, precision=HIGH)
    inv_norm = lax.rsqrt(jnp.sum(latent * latent, axis=-1, keepdims=True) + 1e-06)
    embeds = latent * inv_norm
    embeds_b = embeds.astype(jnp.bfloat16)
    logit_mult = logit_scale[0]
    first_image = lax.axis_index(("row", "col")) * images
    local_ids = first_image + jnp.arange(images, dtype=jnp.int32)
    all_ids = jnp.arange(total_images, dtype=jnp.int32)
    local_pairs = lax.dynamic_slice_in_dim(pair_index, first_image, images)
    match_cols = (pair_index[:, None] == local_ids[None, :]).astype(jnp.float32)
    texts_float = texts.astype(jnp.float32)
    all_embeds, all_texts = (
        lax.all_gather(embeds_b, ("row", "col"), axis=0, tiled=True),
        lax.all_gather(texts, ("row", "col"), axis=0, tiled=True),
    )
    row_logits = logit_mult * jnp.dot(embeds_b, all_texts.T, preferred_element_type=jnp.float32)
    col_logits = logit_mult * jnp.dot(all_embeds, texts.T, preferred_element_type=jnp.float32)
    match_rows = (local_pairs[:, None] == all_ids[None, :]).astype(jnp.float32)
    row_lse = jax.nn.logsumexp(row_logits, axis=1)
    col_lse = jax.nn.logsumexp(col_logits, axis=0)
    partial_loss = 0.5 * (jnp.sum(row_lse) + jnp.sum(col_lse)) - jnp.sum(row_logits * match_rows)
    summed = lax.psum(partial_loss, ("row", "col"))
    row_grad = 0.5 * jnp.exp(row_logits - row_lse[:, None]) - 0.5 * match_rows
    col_grad = 0.5 * jnp.exp(col_logits - col_lse[None, :]) - 0.5 * match_cols
    embed_terms = logit_mult * jnp.dot(col_grad, texts_float, precision=HIGH)
    text_terms = logit_mult * jnp.dot(row_grad.T, embeds_b.astype(jnp.float32), precision=HIGH)
    embed_in, text_in = (
        lax.psum_scatter(embed_terms, ("row", "col"), scatter_dimension=0, tiled=True),
        lax.psum_scatter(text_terms, ("row", "col"), scatter_dimension=0, tiled=True),
    )
    embed_grad = (
        logit_mult * jnp.dot(row_grad, all_texts.astype(jnp.float32), precision=HIGH) + embed_in
    )
    text_grad = (
        logit_mult * jnp.dot(col_grad.T, all_embeds.astype(jnp.float32), precision=HIGH) + text_in
    )
    grad_latent = inv_norm * (
        embed_grad - embeds * jnp.sum(embeds * embed_grad, axis=-1, keepdims=True)
    )
    grad_proj = jnp.dot(pooled.T, grad_latent, precision=HIGH)
    grad_pooled = jnp.dot(grad_latent, proj_float.T, precision=HIGH)
    grad_outputs = (keep_float[:, :, None] * (grad_pooled / counts[:, None])[:, None, :]).reshape(
        rows, D
    )
    grad_mlp = grad_outputs.astype(jnp.bfloat16)
    grad_down = jnp.dot(activ_b.T, grad_mlp, preferred_element_type=jnp.float32)
    grad_down_bias = jnp.sum(grad_mlp.astype(jnp.float32), axis=0)
    grad_activ = jnp.dot(grad_mlp, w_down.T, preferred_element_type=jnp.float32)
    _, gelu_pull = jax.vjp(partial(jax.nn.gelu, approximate=False), hidden)
    grad_hidden = gelu_pull(grad_activ)[0].astype(jnp.bfloat16)
    grad_up = jnp.dot(normed_two_b.T, grad_hidden, preferred_element_type=jnp.float32)
    grad_up_bias = jnp.sum(grad_hidden.astype(jnp.float32), axis=0)
    grad_normed_two = jnp.dot(grad_hidden, w_up.T, preferred_element_type=jnp.float32)
    back_two, gain_two, shift_two = norm_backward(grad_normed_two, scaled_two, inv_two, vectors[5])
    grad_resid = grad_outputs + back_two
    grad_branch = grad_resid.astype(jnp.bfloat16)
    grad_out = jnp.dot(attended.T, grad_branch, preferred_element_type=jnp.float32)
    grad_out_bias = jnp.sum(grad_branch.astype(jnp.float32), axis=0)
    grad_attended = jnp.dot(grad_branch, w_out.T, preferred_element_type=jnp.float32)
    grad_attended = grad_attended.astype(jnp.bfloat16).reshape(head_shape)
    grad_values = jnp.einsum(
        "nhqk,nqhd->nkhd", probs_b, grad_attended, preferred_element_type=jnp.float32
    ).astype(jnp.bfloat16)
    grad_probs = jnp.einsum(
        "nqhd,nkhd->nhqk", grad_attended, value_rows, preferred_element_type=jnp.float32
    )
    grad_scores = probs * (grad_probs - jnp.sum(probs * grad_probs, axis=-1, keepdims=True))
    grad_scores = grad_scores.astype(jnp.bfloat16)
    grad_queries = jnp.einsum(
        "nhqk,nkhd->nqhd", grad_scores, key_rows, preferred_element_type=jnp.float32
    )
    grad_queries = (grad_queries * scale_qk).astype(jnp.bfloat16).reshape(rows, D)
    grad_keys = jnp.einsum(
        "nhqk,nqhd->nkhd", grad_scores, queries, preferred_element_type=jnp.float32
    )
    grad_keys = (grad_keys * scale_qk).astype(jnp.bfloat16).reshape(rows, D)
    grad_values = grad_values.reshape(rows, D)
    grad_projected = jnp.concatenate([grad_queries, grad_keys, grad_values], axis=1)
    grad_qkv = jnp.dot(normed_b.T, grad_projected, preferred_element_type=jnp.float32)
    grad_normed = jnp.dot(grad_projected, w_qkv.T, preferred_element_type=jnp.float32)
    back_one, gain_one, shift_one = norm_backward(grad_normed, scaled_one, inv_one, vectors[0])
    token_grad = grad_resid + back_one
    grad_vectors = jnp.stack(
        [
            gain_one,
            shift_one,
            jnp.sum(grad_queries.astype(jnp.float32), axis=0),
            jnp.sum(grad_values.astype(jnp.float32), axis=0),
            grad_out_bias,
            gain_two,
            shift_two,
            grad_down_bias,
        ],
        axis=1,
    )
    shares = (
        lax.psum_scatter(
            grad_qkv.astype(jnp.bfloat16), "col", scatter_dimension=0, tiled=True
        ).astype(jnp.float32),
        lax.psum_scatter(
            grad_out.astype(jnp.bfloat16), "col", scatter_dimension=0, tiled=True
        ).astype(jnp.float32),
        lax.psum_scatter(
            grad_up.astype(jnp.bfloat16), "col", scatter_dimension=0, tiled=True
        ).astype(jnp.float32),
        lax.psum_scatter(
            grad_down.astype(jnp.bfloat16), "col", scatter_dimension=0, tiled=True
        ).astype(jnp.float32),
        lax.psum_scatter(
            grad_vectors.astype(jnp.bfloat16), "col", scatter_dimension=0, tiled=True
        ).astype(jnp.float32),
        lax.psum_scatter(
            grad_up_bias.astype(jnp.bfloat16), "col", scatter_dimension=0, tiled=True
        ).astype(jnp.float32),
        lax.psum_scatter(
            grad_proj.astype(jnp.bfloat16), "col", scatter_dimension=0, tiled=True
        ).astype(jnp.float32),
    )
    shares = (
        lax.psum(shares[0].astype(jnp.bfloat16), "row").astype(jnp.float32),
        lax.psum(shares[1].astype(jnp.bfloat16), "row").astype(jnp.float32),
        lax.psum(shares[2].astype(jnp.bfloat16), "row").astype(jnp.float32),
        lax.psum(shares[3].astype(jnp.bfloat16), "row").astype(jnp.float32),
        lax.psum(shares[4].astype(jnp.bfloat16), "row").astype(jnp.float32),
        lax.psum(shares[5].astype(jnp.bfloat16), "row").astype(jnp.float32),
        lax.psum(shares[6].astype(jnp.bfloat16), "row").astype(jnp.float32),
    )
    loss = (summed / total_images).reshape(1)
    return (
        loss,
        token_grad,
        shares[0],
        shares[1],
        shares[2],
        shares[3],
        shares[4].T,
        shares[5],
        shares[6],
        text_grad,
    )


def solution(mesh):
    in_specs = (
        P(("row", "col"), None),
        P(("row", "col"), None),
        P(),
        P(),
        P(),
        P(),
        P(),
        P(),
        P(),
        P(("row", "col"), None),
        P(),
        P(),
    )
    out_specs = (
        P(),
        P(("row", "col"), None),
        P("col", None),
        P("col", None),
        P("col", None),
        P("col", None),
        P(None, "col"),
        P("col"),
        P("col", None),
        P(("row", "col"), None),
    )
    return jax.shard_map(
        per_device, mesh=mesh, in_specs=in_specs, out_specs=out_specs, check_vma=False
    )
```

profile of v0, /device:TPU:0, one launch (start us, length us, event | category | flops | bytes accessed | tf_op | source)
XLA Modules:
  0.0 872.7 jit_solution(9870229743030779231)
XLA Ops:
  16.5 46.2 %all-gather = bf16[32,4,512]{2,1,0:T(4,128)(2,1)} all-gather(bf16[1,4,512]{2,1,0:T(4,128)(2,1)S(1)} %bitcast.68), channel_id=1, replica_groups=mesh['row'=2,'col'=16] {'row','col'}, dimensions={0}, use_global_device_ids=true | all-gather | bytes 135168 | tf_op jit(solution)/shard_map/all_gather | solution.py:92
  64.3 4.5 fusion.58
  71.9 4.9 reshape.162
  76.8 4.9 copy.57
  81.7 4.8 reshape.163
  86.4 4.9 copy.58
  91.3 4.8 reshape.161
  96.0 4.8 copy.59
  100.9 10.2 %fusion.64 = (f32[4,12,197]{2,1,0:T(8,128)}, f32[4,12,197,197]{2,3,1,0:T(8,128)}) fusion(pred[4,197]{1,0:T(4,128)(4,1)S(1)} %copy-done.43, bf16[4,197,12,64]{1,3,2,0:T(8,128)(2,1)} %copy.57, bf16[4,197,12,64]{1,3,2,0:T(8,128)(2,1)} %copy.58), kind=kOutput, calls=%fused_computation.140 | convolution fusion | flops 245894016 | bytes 9910676 | tf_op jit(solution)/shard_map/sub | solution.py:62
  111.1 5.3 fusion.41
  118.8 4.4 convert_element_type.153
  123.2 3.6 fusion.65
  127.6 28.3 %multiply_convert_fusion.1 = (bf16[788,3072]{1,0:T(8,128)(2,1)S(1)}, f32[788,3072]{1,0:T(8,128)}, f32[788,3072]{1,0:T(8,128)}) fusion(f32[3072]{0:T(1024)S(1)} %copy-done.47, bf16[768,3072]{1,0:T(8,128)(2,1)} %param.16, f32[788,768]{1,0:T(8,128)S(1)} %get-tuple-element.50, f32[768]{0:T(1024)S(1)} %copy-done.35, f32[768]{0:T(1024)S(1)} %copy-done.26, ...), kind=kOutput, calls=%fused_computation.8 | convolution fusion | flops 3881044992 | bytes 31371424 | tf_op jit(solution)/shard_map/dot_general | solution.py:71
  158.0 5.5 add_add_fusion
  163.5 3.4 reshape.148
  171.0 39.6 %all-gather.1 = bf16[32,4,512]{2,1,0:T(4,128)(2,1)} all-gather(bf16[1,4,512]{2,1,0:T(4,128)(2,1)S(1)} %fusion.109), channel_id=1, replica_groups=mesh['row'=2,'col'=16] {'row','col'}, dimensions={0}, use_global_device_ids=true | all-gather | bytes 135168 | tf_op jit(solution)/shard_map/all_gather | solution.py:91
  223.8 125.0 %all-reduce.9.cloned.1.call-done = (f32[128,512]{1,0:T(8,128)}, f32[128,512]{1,0:T(8,128)}) async-done(((f32[128,512]{1,0:T(8,128)}, f32[128,512]{1,0:T(8,128)}), (f32[128,512]{1,0:T(8,128)}, f32[128,512]{1,0:T(8,128)})) %all-reduce.9.cloned.1.call-update) | async-done | bytes 524304
  354.7 3.4 mul.304
  358.1 13.7 %fusion.70 = (bf16[3072]{0:T(1024)(128)(2,1)}, bf16[788,3072]{1,0:T(8,128)(2,1)S(1)}) fusion(f32[788,3072]{1,0:T(8,128)} %get-tuple-element.44, bf16[3072,768]{1,0:T(8,128)(2,1)} %param.17, f32[788,768]{1,0:T(8,128)} %mul.304, f32[788]{0:T(1024)} %mul.289, f32[788,3072]{1,0:T(8,128)} %get-tuple-element.51, f32[3072]{0:T(1024)} %param.19), kind=kOutput, calls=%fused_computation.146 | convolution fusion | flops 3758189568 | bytes 31368272 | tf_op jit(solution)/shard_map/dot_general | solution.py:126
  371.9 9.1 %multiply_reduce_fusion.2 = (bf16[768]{0:T(1024)(128)(2,1)}, f32[788]{0:T(1024)S(1)}, f32[788]{0:T(1024)S(1)}, bf16[768]{0:T(1024)(128)(2,1)}, f32[788,768]{1,0:T(8,128)S(1)}) fusion(f32[788,768]{1,0:T(8,128)S(1)} %copy-done.4, f32[788]{0:T(1024)S(1)} %copy-done.30, f32[788]{0:T(1024)S(1)} %broadcast_multiply_fusion.4, f32[768]{0:T(1024)S(1)} %copy-done.27, ...), kind=kOutput, calls=%fused_computation.61 | convolution fusion | flops 3723694080 | bytes 14420288 | tf_op jit(solution)/shard_map/dot_general | solution.py:131
  384.3 2.4 convolution_convert_fusion.4
  386.7 4.2 convolution_convert_fusion.3
  390.9 4.7 reshape.164
  395.6 4.9 copy.63
  400.5 7.8 fusion.69
  408.3 7.9 multiply_reduce_fusion
  416.3 11.1 %multiply_convert_fusion = bf16[4,12,197,197]{2,3,1,0:T(8,128)(2,1)} fusion(f32[4,12,197,197]{2,3,1,0:T(8,128)} %get-tuple-element.62, f32[4,12,197]{2,1,0:T(8,128)} %get-tuple-element.61, f32[4,12,197,197]{2,3,1,0:T(8,128)} %get-tuple-element.48, f32[4,12,197]{2,1,0:T(8,128)} %get-tuple-element.47), kind=kLoop, calls=%fused_computation.2 | loop fusion | flops 7451328 | bytes 18703968 | tf_op jit(solution)/shard_map/convert_element_type | solution.py:146
  427.5 5.9 fusion.45
  433.4 2.4 copy.73
  435.8 4.2 reshape.153
  440.0 3.8 copy.70
  443.7 4.2 reshape.152
  447.9 4.7 fusion.68
  455.0 4.2 reshape.151
  463.6 6.0 convolution_convert_fusion.2
  469.7 9.7 %convolution_convert_fusion = bf16[3072,768]{1,0:T(8,128)(2,1)} fusion(bf16[788,3072]{1,0:T(8,128)(2,1)} %copy-done.49, f32[788,768]{1,0:T(8,128)} %mul.304, f32[788]{0:T(1024)} %mul.289), kind=kOutput, calls=%fused_computation.23 | convolution fusion | flops 3721820160 | bytes 11983952 | tf_op jit(solution)/shard_map/dot_general | solution.py:124
  479.5 9.9 %convolution_convert_fusion.1 = bf16[768,3072]{1,0:T(8,128)(2,1)} fusion(bf16[788,3072]{1,0:T(8,128)(2,1)} %copy-done.48, f32[788,768]{1,0:T(8,128)} %copy-done.3, f32[768]{0:T(1024)} %get-tuple-element.25, f32[768]{0:T(1024)} %get-tuple-element.19, f32[788]{0:T(1024)} %copy-done.29, f32[788]{0:T(1024)} %copy-done.20), kind=kOutput, calls=%fused_computation.24 | convolution fusion | flops 3723635712 | bytes 11993248 | tf_op jit(solution)/shard_map/dot_general | solution.py:129
  497.4 8.5 fusion.27
  510.1 3.1 convolution_convert_fusion.5
  515.2 39.6 %psum.56 = f32[]{:T(128)} all-reduce(f32[]{:T(128)S(6)} %sub.108), channel_id=1, replica_groups=mesh['row'=2,'col'=16] {'row','col'}, use_global_device_ids=true, to_apply=%region_16.17 | all-reduce | flops 1 | bytes 8 | tf_op jit(solution)/shard_map/psum | solution.py:100
  557.3 33.6 %all-reduce.1 = bf16[3072]{0:T(1024)(128)(2,1)S(1)} all-reduce(bf16[3072]{0:T(1024)(128)(2,1)} %get-tuple-element.68), channel_id=8, replica_groups=mesh['row'=2,'col'=16] {'col'}, use_global_device_ids=true, to_apply=%region_43.44.clone | all-reduce | flops 3072 | bytes 12288
  592.2 32.0 %reduce-scatter.15.cloned.1.call-done = bf16[192,768]{1,0:T(8,128)(2,1)} async-done(((bf16[3072,768]{1,0:T(8,128)(2,1)}), bf16[192,768]{1,0:T(8,128)(2,1)}) %reduce-scatter.15.cloned.1.call-update) | async-done | bytes 294928 | tf_op jit(solution)/shard_map/reduce_scatter | solution.py:184
  624.2 78.3 %reduce-scatter.13.cloned.1.call-done = bf16[48,3072]{1,0:T(8,128)(2,1)} async-done(((bf16[768,3072]{1,0:T(8,128)(2,1)}), bf16[48,3072]{1,0:T(8,128)(2,1)}) %reduce-scatter.13.cloned.1.call-update) | async-done | bytes 294928 | tf_op jit(solution)/shard_map/reduce_scatter | solution.py:181
  705.0 4.3 fusion.26
  709.3 50.2 %reduce-scatter.19.cloned.1.call-done = bf16[48,8]{1,0:T(8,128)(2,1)} async-done(((bf16[768,8]{1,0:T(8,128)(2,1)}), bf16[48,8]{1,0:T(8,128)(2,1)}) %reduce-scatter.19.cloned.1.call-update) | async-done | bytes 784
  760.2 58.8 %reduce-scatter.17.cloned.1.call-done = bf16[48,512]{1,0:T(8,128)(2,1)} async-done(((bf16[768,512]{1,0:T(8,128)(2,1)}), bf16[48,512]{1,0:T(8,128)(2,1)}) %reduce-scatter.17.cloned.1.call-update) | async-done | bytes 49168 | tf_op jit(solution)/shard_map/reduce_scatter | solution.py:193
  819.0 10.4 %all-reduce.4 = (bf16[8,48]{1,0:T(8,128)(2,1)S(1)}, bf16[192]{0:T(256)(128)(2,1)S(1)}, bf16[48,512]{1,0:T(8,128)(2,1)}) all-reduce(bf16[8,48]{1,0:T(8,128)(2,1)S(1)} %bitcast.69, bf16[192]{0:T(256)(128)(2,1)S(1)} %copy-done.44, bf16[48,512]{1,0:T(8,128)(2,1)} %reduce-scatter.17.cloned.1.call-done), channel_id=1, replica_groups=mesh['row'=2,'col'=16] {'row'}, use_global_device_ids=true, to_apply=%region_41.42 | all-reduce | flops 25152 | bytes 100608 | tf_op jit(solution)/shard_map/psum | solution.py:202
  832.1 25.5 %all-reduce.11.cloned.1.call-done = (bf16[48,2304]{1,0:T(8,128)(2,1)}, bf16[48,768]{1,0:T(8,128)(2,1)}, bf16[48,3072]{1,0:T(8,128)(2,1)}, bf16[192,768]{1,0:T(8,128)(2,1)}) async-done(((bf16[48,2304]{1,0:T(8,128)(2,1)}, bf16[48,768]{1,0:T(8,128)(2,1)}, bf16[48,3072]{1,0:T(8,128)(2,1)}, bf16[192,768]{1,0:T(8,128)(2,1)}), (bf16[48,2304]{1,0:T(8,128)(2,1)}, bf16[48,768]{1,0:T(8,128)(2,1)}, ...) | async-done | bytes 884752 | tf_op jit(solution)/shard_map/psum | solution.py:198
  (189 shorter events, 79.4 us)
Async XLA Ops:
  7.2 57.1 %copy-start = (bf16[768,2304]{1,0:T(8,128)(2,1)S(1)}, bf16[768,2304]{1,0:T(8,128)(2,1)}, u32[]{:S(2)}) copy-start(bf16[768,2304]{1,0:T(8,128)(2,1)} %param.14) | copy-start | bytes 10616836
  7.2 9.3 %copy-start.21 = (bf16[4,512]{1,0:T(4,128)(2,1)S(1)}, bf16[4,512]{1,0:T(4,128)(2,1)}, u32[]{:S(2)}) copy-start(bf16[4,512]{1,0:T(4,128)(2,1)} %param.21) | copy-start | bytes 12292
  7.2 341.6 %all-reduce.9.cloned.1.call-start = ((), (), s32[]{:S(2)}) async-start(), calls=%async_computation.12 | async-start | bytes 1048576
  11.2 4.6 copy-start.22
  13.4 55.4 %copy-start.18 = (f32[788]{0:T(1024)}, f32[788]{0:T(1024)S(1)}, u32[]{:S(2)}) copy-start(f32[788]{0:T(1024)S(1)} %broadcast_multiply_fusion.5) | copy-start | bytes 9460
  64.3 5.7 copy-start.24
  96.0 4.9 copy-start.43
  116.4 6.8 copy-start.38
  123.2 34.8 %slice-start = ((s8[4718592]{0:T(1024)(128)(4,1)}), s8[4194304]{0:T(1024)(128)(4,1)S(1)}, s32[]{:S(2)}) async-start(s8[4718592]{0:T(1024)(128)(4,1)} %bitcast.70), calls=%async_computation.14 | async-start | bytes 8388608
  126.8 29.1 %copy-start.3 = (f32[788,768]{1,0:T(8,128)}, f32[788,768]{1,0:T(8,128)S(1)}, u32[]{:S(2)}) copy-start(f32[788,768]{1,0:T(8,128)S(1)} %get-tuple-element.50) | copy-start | bytes 7262212
  126.8 254.2 %copy-start.20 = (f32[788]{0:T(1024)}, f32[788]{0:T(1024)S(1)}, u32[]{:S(2)}) copy-start(f32[788]{0:T(1024)S(1)} %broadcast_multiply_fusion.4) | copy-start | bytes 9460
  127.3 28.5 %copy-start.29 = (f32[788]{0:T(1024)}, f32[788]{0:T(1024)S(1)}, u32[]{:S(2)}) copy-start(f32[788]{0:T(1024)S(1)} %add_rsqrt_fusion) | copy-start | bytes 9460
  127.6 30.5 %copy-start.37 = (f32[768]{0:T(1024)S(1)}, f32[768]{0:T(1024)}, u32[]{:S(2)}) copy-start(f32[768]{0:T(1024)} %get-tuple-element.18) | copy-start | bytes 9220
  127.6 30.5 %slice-start.1 = ((s8[4718592]{0:T(1024)(128)(4,1)}), s8[524288]{0:T(1024)(128)(4,1)S(1)}, s32[]{:S(2)}) async-start(s8[4718592]{0:T(1024)(128)(4,1)} %bitcast.70), calls=%async_computation.15 | async-start | bytes 1048576
  155.8 2.2 copy-start.49
  166.9 2.0 copy-start.12
  166.9 2.1 copy-start.33
  166.9 2.7 copy-start.14
  215.7 3.7 copy-start.40
  219.4 1.8 copy-start.41
  219.4 1.8 copy-start.39
  223.0 369.1 %reduce-scatter.11.cloned.1.call-start = ((), (), s32[]{:S(2)}) async-start(), calls=%async_computation.7 | async-start | bytes 1253376 | tf_op jit(solution)/shard_map/reduce_scatter | solution.py:178
  358.1 13.7 %copy-start.4 = (f32[788,768]{1,0:T(8,128)S(1)}, f32[788,768]{1,0:T(8,128)}, u32[]{:S(2)}) copy-start(f32[788,768]{1,0:T(8,128)} %copy-done.3) | copy-start | bytes 7262212
  358.1 13.7 %copy-start.27 = (f32[768]{0:T(1024)S(1)}, f32[768]{0:T(1024)}, u32[]{:S(2)}) copy-start(f32[768]{0:T(1024)} %get-tuple-element.19) | copy-start | bytes 9220
  358.1 13.7 %copy-start.30 = (f32[788]{0:T(1024)S(1)}, f32[788]{0:T(1024)}, u32[]{:S(2)}) copy-start(f32[788]{0:T(1024)} %copy-done.29) | copy-start | bytes 9460
  371.8 9.2 %copy-start.48 = (bf16[788,3072]{1,0:T(8,128)(2,1)}, bf16[788,3072]{1,0:T(8,128)(2,1)S(1)}, u32[]{:S(2)}) copy-start(bf16[788,3072]{1,0:T(8,128)(2,1)S(1)} %get-tuple-element.69) | copy-start | bytes 14524420
  371.8 9.2 %copy-start.5 = (f32[788,768]{1,0:T(8,128)S(1)}, f32[788,768]{1,0:T(8,128)}, u32[]{:S(2)}) copy-start(f32[788,768]{1,0:T(8,128)} %mul.304) | copy-start | bytes 7262212
  371.9 9.2 %copy-start.31 = (f32[788]{0:T(1024)S(1)}, f32[788]{0:T(1024)}, u32[]{:S(2)}) copy-start(f32[788]{0:T(1024)} %mul.289) | copy-start | bytes 9460
  381.0 3.3 copy-start.11
  400.5 7.8 copy-start.9
  400.5 7.8 copy-start.10
  400.5 7.8 copy-start.16
  416.3 175.9 %reduce-scatter.9.cloned.1.call-start = ((), (), s32[]{:S(2)}) async-start(), calls=%async_computation.6 | async-start | bytes 3760128 | tf_op jit(solution)/shard_map/reduce_scatter | solution.py:175
  427.5 5.9 copy-start.8
  459.2 2.2 copy-start.6
  460.9 2.7 copy-start.1
  460.9 2.7 copy-start.19
  460.9 2.7 copy-start.25
  460.9 2.7 copy-start.28
  460.9 2.7 copy-start.36
  461.6 2.0 copy-start.13
  469.7 154.6 %reduce-scatter.15.cloned.1.call-start = ((), (), s32[]{:S(2)}) async-start(), calls=%async_computation.9 | async-start | bytes 5013504 | tf_op jit(solution)/shard_map/reduce_scatter | solution.py:184
  479.4 223.1 %reduce-scatter.13.cloned.1.call-start = ((), (), s32[]{:S(2)}) async-start(), calls=%async_computation.8 | async-start | bytes 5013504 | tf_op jit(solution)/shard_map/reduce_scatter | solution.py:181
  489.4 270.1 %reduce-scatter.19.cloned.1.call-start = ((), (), s32[]{:S(2)}) async-start(), calls=%async_computation.11 | async-start | bytes 208896
  505.9 197.3 %copy-start.23 = (f32[128,4]{0,1:T(4,128)S(1)}, f32[128,4]{0,1:T(4,128)}, u32[]{:S(2)}) copy-start(f32[128,4]{0,1:T(4,128)} %get-tuple-element.57) | copy-start | bytes 6148
  510.0 309.0 %reduce-scatter.17.cloned.1.call-start = ((), (), s32[]{:S(2)}) async-start(), calls=%async_computation.10 | async-start | bytes 835584 | tf_op jit(solution)/shard_map/reduce_scatter | solution.py:193
  513.3 344.3 %all-reduce.11.cloned.1.call-start = ((), (), s32[]{:S(2)}) async-start(), calls=%async_computation.13 | async-start | bytes 1769472 | tf_op jit(solution)/shard_map/psum | solution.py:198
  705.0 114.1 %copy-start.44 = (bf16[192]{0:T(256)(128)(2,1)S(1)}, bf16[192]{0:T(256)(128)(2,1)}, u32[]{:S(2)}) copy-start(bf16[192]{0:T(256)(128)(2,1)} %dynamic-slice.2) | copy-start | bytes 1156
  (12 other events, 10.8 us)
Sparse Core Ops, SparseCore 0:
  223.2 125.5 all-reduce.8
  416.4 57.0 reduce-scatter.10
  477.9 67.1 reduce-scatter.8
  549.4 74.8 reduce-scatter.14
  627.9 74.5 reduce-scatter.12
  706.8 52.5 reduce-scatter.18
  763.4 55.5 reduce-scatter.16
  821.5 36.0 all-reduce.10
where the time goes:
time: 879 us; the launch traced here: 873 us
  waiting for transfers between devices  370 us (42%)
  blocking collectives  169 us (19%)
  matrix products  162 us (18%)
  local copies, waits for them, and re-layouts  105 us (12%)
  other arithmetic  46 us (5%)
  between operations  19.7 us (2%)
    unnamed x10, waiting for transfers between devices  175 us
    reduce_scatter x1, waiting for transfers between devices, per_device(): lax.psum_scatter(grad_up.astype(jnp.bfloat16), 'col', scatter_dimension=0...  78.3 us
    reduce_scatter x1, waiting for transfers between devices, per_device(): lax.psum_scatter(grad_proj.astype(jnp.bfloat16), 'col', scatter_dimension...  58.8 us
    all_gather x1, blocking collectives, per_device(): lax.all_gather(texts, ('row', 'col'), axis=0, tiled=True)  46.2 us
    psum x1, blocking collectives, per_device(): summed = lax.psum(partial_loss, ('row', 'col'))  39.6 us
    all_gather x1, blocking collectives, per_device(): lax.all_gather(embeds_b, ('row', 'col'), axis=0, tiled=True)  39.6 us
    unnamed x1, blocking collectives  33.6 us
    reduce_scatter x1, waiting for transfers between devices, per_device(): lax.psum_scatter(grad_down.astype(jnp.bfloat16), 'col', scatter_dimension...  32 us
  transfers between devices with their start and end apart: 8, of which 6 were waited for; matrix products, arithmetic and copies ran while one was open for 12% of the time, Pallas kernels for 0%

commit v1 on v0

--- a/solution.py
+++ b/solution.py
@@ -70,60 +70,63 @@
     normed_two_b = normed_two.astype(jnp.bfloat16)
     hidden = jnp.dot(normed_two_b, w_up, preferred_element_type=jnp.float32) + up_bias
     activ_b = jax.nn.gelu(hidden, approximate=False).astype(jnp.bfloat16)
-    outputs = resid + jnp.dot(activ_b, w_down, preferred_element_type=jnp.float32) + vectors[7]
     counts = jnp.sum(keep_float, axis=1)
-    pooled = (
-        jnp.sum(outputs.reshape(images, SEQ, D) * keep_float[:, :, None], axis=1) / counts[:, None]
-    )
+    activ_sum = jnp.einsum(
+        "nsf,ns->nf",
+        activ_b.reshape(images, SEQ, -1),
+        keep_mask.astype(jnp.bfloat16),
+        preferred_element_type=jnp.float32,
+    )
+    resid_sum = jnp.sum(resid.reshape(images, SEQ, D) * keep_float[:, :, None], axis=1)
+    pooled_sum = resid_sum + jnp.dot(activ_sum, w_down.astype(jnp.float32), precision=HIGH)
+    pooled = pooled_sum / counts[:, None] + vectors[7]
+    sent = jnp.concatenate([pooled, jnp.broadcast_to(counts[:, None], (images, 128))], axis=1)
+    gathered = lax.all_gather(sent, ("row", "col"), axis=0, tiled=True)
+    all_texts = lax.all_gather(texts, ("row", "col"), axis=0, tiled=True).astype(jnp.float32)
+    pooled_all, counts_all = gathered[:, :D], gathered[:, D : D + 1]
     proj_float = w_proj.astype(jnp.float32)
-    latent = jnp.dot(pooled, proj_float, precision=HIGH)
+    latent = jnp.dot(pooled_all, proj_float, precision=HIGH)
     inv_norm = lax.rsqrt(jnp.sum(latent * latent, axis=-1, keepdims=True) + 1e-06)
     embeds = latent * inv_norm
-    embeds_b = embeds.astype(jnp.bfloat16)
+    embeds_f = embeds.astype(jnp.bfloat16).astype(jnp.float32)
     logit_mult = logit_scale[0]
     first_image = lax.axis_index(("row", "col")) * images
-    local_ids = first_image + jnp.arange(images, dtype=jnp.int32)
     all_ids = jnp.arange(total_images, dtype=jnp.int32)
-    local_pairs = lax.dynamic_slice_in_dim(pair_index, first_image, images)
-    match_cols = (pair_index[:, None] == local_ids[None, :]).astype(jnp.float32)
-    texts_float = texts.astype(jnp.float32)
-    all_embeds, all_texts = (
-        lax.all_gather(embeds_b, ("row", "col"), axis=0, tiled=True),
-        lax.all_gather(texts, ("row", "col"), axis=0, tiled=True),
-    )
-    row_logits = logit_mult * jnp.dot(embeds_b, all_texts.T, preferred_element_type=jnp.float32)
-    col_logits = logit_mult * jnp.dot(all_embeds, texts.T, preferred_element_type=jnp.float32)
-    match_rows = (local_pairs[:, None] == all_ids[None, :]).astype(jnp.float32)
-    row_lse = jax.nn.logsumexp(row_logits, axis=1)
-    col_lse = jax.nn.logsumexp(col_logits, axis=0)
-    partial_loss = 0.5 * (jnp.sum(row_lse) + jnp.sum(col_lse)) - jnp.sum(row_logits * match_rows)
-    summed = lax.psum(partial_loss, ("row", "col"))
-    row_grad = 0.5 * jnp.exp(row_logits - row_lse[:, None]) - 0.5 * match_rows
-    col_grad = 0.5 * jnp.exp(col_logits - col_lse[None, :]) - 0.5 * match_cols
-    embed_terms = logit_mult * jnp.dot(col_grad, texts_float, precision=HIGH)
-    text_terms = logit_mult * jnp.dot(row_grad.T, embeds_b.astype(jnp.float32), precision=HIGH)
-    embed_in, text_in = (
-        lax.psum_scatter(embed_terms, ("row", "col"), scatter_dimension=0, tiled=True),
-        lax.psum_scatter(text_terms, ("row", "col"), scatter_dimension=0, tiled=True),
-    )
-    embed_grad = (
-        logit_mult * jnp.dot(row_grad, all_texts.astype(jnp.float32), precision=HIGH) + embed_in
-    )
-    text_grad = (
-        logit_mult * jnp.dot(col_grad.T, all_embeds.astype(jnp.float32), precision=HIGH) + text_in
-    )
+    match = (pair_index[:, None] == all_ids[None, :]).astype(jnp.float32)
+    logits = logit_mult * jnp.dot(
+        embeds_f.astype(jnp.bfloat16), all_texts.astype(jnp.bfloat16).T,
+        preferred_element_type=jnp.float32,
+    )
+    row_lse = jax.nn.logsumexp(logits, axis=1)
+    col_lse = jax.nn.logsumexp(logits, axis=0)
+    summed = 0.5 * (jnp.sum(row_lse) + jnp.sum(col_lse)) - jnp.sum(logits * match)
+    grad_logits = (
+        0.5 * jnp.exp(logits - row_lse[:, None]) + 0.5 * jnp.exp(logits - col_lse[None, :]) - match
+    )
+    embed_grad = logit_mult * jnp.dot(grad_logits, all_texts, precision=HIGH)
+    own_cols = lax.dynamic_slice_in_dim(grad_logits, first_image, images, axis=1)
+    text_grad = logit_mult * jnp.dot(own_cols.T, embeds_f, precision=HIGH)
     grad_latent = inv_norm * (
         embed_grad - embeds * jnp.sum(embeds * embed_grad, axis=-1, keepdims=True)
     )
-    grad_proj = jnp.dot(pooled.T, grad_latent, precision=HIGH)
+    shards = lax.axis_size("col")
+    mine = lax.axis_index("col")
+    own_pooled = lax.dynamic_slice_in_dim(pooled_all, mine * (D // shards), D // shards, axis=1)
+    grad_proj = jnp.dot(own_pooled.T, grad_latent, precision=HIGH)
     grad_pooled = jnp.dot(grad_latent, proj_float.T, precision=HIGH)
-    grad_outputs = (keep_float[:, :, None] * (grad_pooled / counts[:, None])[:, None, :]).reshape(
-        rows, D
-    )
-    grad_mlp = grad_outputs.astype(jnp.bfloat16)
-    grad_down = jnp.dot(activ_b.T, grad_mlp, preferred_element_type=jnp.float32)
-    grad_down_bias = jnp.sum(grad_mlp.astype(jnp.float32), axis=0)
-    grad_activ = jnp.dot(grad_mlp, w_down.T, preferred_element_type=jnp.float32)
+    image_grads = (grad_pooled / counts_all).astype(jnp.bfloat16)
+    ff = w_up.shape[1]
+    pieces = activ_sum.reshape(images, shards, ff // shards).transpose(1, 0, 2)
+    pieces = lax.all_to_all(pieces, "col", split_axis=0, concat_axis=0, tiled=True)
+    pieces = pieces.reshape(images * shards, ff // shards)
+    pieces = lax.all_gather(pieces, "row", axis=0, tiled=True)
+    grad_down = jnp.dot(pieces.T, image_grads.astype(jnp.float32), precision=HIGH)
+    own_grads = lax.dynamic_slice_in_dim(grad_pooled / counts_all, first_image, images)
+    own_rounded = own_grads.astype(jnp.bfloat16)
+    grad_outputs = (keep_float[:, :, None] * own_grads[:, None, :]).reshape(rows, D)
+    grad_down_bias = jnp.sum(counts[:, None] * own_rounded.astype(jnp.float32), axis=0)
+    image_activ = jnp.dot(own_rounded, w_down.T, preferred_element_type=jnp.float32)
+    grad_activ = (keep_float[:, :, None] * image_activ[:, None, :]).reshape(rows, ff)
     _, gelu_pull = jax.vjp(partial(jax.nn.gelu, approximate=False), hidden)
     grad_hidden = gelu_pull(grad_activ)[0].astype(jnp.bfloat16)
     grad_up = jnp.dot(normed_two_b.T, grad_hidden, preferred_element_type=jnp.float32)
@@ -171,38 +174,13 @@
         ],
         axis=1,
     )
-    shares = (
-        lax.psum_scatter(
-            grad_qkv.astype(jnp.bfloat16), "col", scatter_dimension=0, tiled=True
-        ).astype(jnp.float32),
-        lax.psum_scatter(
-            grad_out.astype(jnp.bfloat16), "col", scatter_dimension=0, tiled=True
-        ).astype(jnp.float32),
-        lax.psum_scatter(
-            grad_up.astype(jnp.bfloat16), "col", scatter_dimension=0, tiled=True
-        ).astype(jnp.float32),
-        lax.psum_scatter(
-            grad_down.astype(jnp.bfloat16), "col", scatter_dimension=0, tiled=True
-        ).astype(jnp.float32),
-        lax.psum_scatter(
-            grad_vectors.astype(jnp.bfloat16), "col", scatter_dimension=0, tiled=True
-        ).astype(jnp.float32),
-        lax.psum_scatter(
-            grad_up_bias.astype(jnp.bfloat16), "col", scatter_dimension=0, tiled=True
-        ).astype(jnp.float32),
-        lax.psum_scatter(
-            grad_proj.astype(jnp.bfloat16), "col", scatter_dimension=0, tiled=True
-        ).astype(jnp.float32),
-    )
-    shares = (
-        lax.psum(shares[0].astype(jnp.bfloat16), "row").astype(jnp.float32),
-        lax.psum(shares[1].astype(jnp.bfloat16), "row").astype(jnp.float32),
-        lax.psum(shares[2].astype(jnp.bfloat16), "row").astype(jnp.float32),
-        lax.psum(shares[3].astype(jnp.bfloat16), "row").astype(jnp.float32),
-        lax.psum(shares[4].astype(jnp.bfloat16), "row").astype(jnp.float32),
-        lax.psum(shares[5].astype(jnp.bfloat16), "row").astype(jnp.float32),
-        lax.psum(shares[6].astype(jnp.bfloat16), "row").astype(jnp.float32),
-    )
+    wide = [grad_qkv, grad_out, grad_up, grad_vectors, grad_up_bias]
+    shares = []
+    for grad in wide:
+        part = lax.psum_scatter(
+            grad.astype(jnp.bfloat16), "col", scatter_dimension=0, tiled=True
+        )
+        shares.append(lax.psum(part, "row").astype(jnp.float32))
     loss = (summed / total_images).reshape(1)
     return (
         loss,
@@ -210,10 +188,10 @@
         shares[0],
         shares[1],
         shares[2],
-        shares[3],
-        shares[4].T,
-        shares[5],
-        shares[6],
+        grad_down,
+        shares[3].T,
+        shares[4],
+        grad_proj,
         text_grad,
     )
 

time: 879 us -> 633 us (0.72)
  waiting for transfers between devices: 370 us -> 132 us
  blocking collectives: 169 us -> 129 us
  local copies, waits for them, and re-layouts: 105 us -> 133 us
  other arithmetic: 46 us -> 61.3 us
  matrix products: 162 us -> 148 us
    unnamed x10 -> x6, waiting for transfers between devices: 175 us -> 17.6 us
    reduce_scatter x5 -> x3, waiting for transfers between devices: 169 us -> 99.4 us  [per_device(): lax.psum_scatter(grad.astype(jnp.bfloat16), 'col', scatter_dimension=0, t...]
    psum x2 -> x1, blocking collectives: 50 us -> 5.06 us  [per_device(): shares.append(lax.psum(part, 'row').astype(jnp.float32))]
    dot_general x11 -> x9, matrix products: 41.8 us -> 23 us  [the longest x1 4.29 us: per_device(): jnp.dot(activ_sum, w_down.astype(jnp.float32), precision=HIGH)]
    all_gather x1 -> x2, blocking collectives: 39.6 us -> 53.6 us  [the longest x1 47.1 us: per_device(): gathered = lax.all_gather(sent, ('row', 'col'), axis=0, tiled=True)]
    mul x3 -> x5, local copies, waits for them, and re-layouts: 5.65 us -> 19.2 us  [the longest x2 13.6 us: per_device(): keep_float[:, :, None] * image_activ[:, None, :]]
    reduce_sum x4, other arithmetic: 5.28 us -> 17.7 us  [the longest x1 12.7 us: per_device(): grad_up_bias = jnp.sum(grad_hidden.astype(jnp.float32), axis=0)]
    psum x1, waiting for transfers between devices: 25.5 us -> 15.3 us  [per_device(): shares.append(lax.psum(part, 'row').astype(jnp.float32))]
  transfers between devices with their start and end apart: 8 -> 6, of which waited for: 6 -> 4; matrix products, arithmetic and copies ran while one was open for 12% -> 21% of each run, Pallas kernels for 0% -> 0%
where the time goes in v1:
time: 633 us; the launch traced here: 627 us
  matrix products  148 us (23%)
  local copies, waits for them, and re-layouts  133 us (21%)
  waiting for transfers between devices  132 us (21%)
  blocking collectives  129 us (20%)
  other arithmetic  61.3 us (10%)
  between operations  19.1 us (3%)
    reduce_scatter x3, waiting for transfers between devices, per_device(): lax.psum_scatter(grad.astype(jnp.bfloat16), 'col', scatter_dimension=0, t...  99.4 us
    all_gather x1, blocking collectives, per_device(): gathered = lax.all_gather(sent, ('row', 'col'), axis=0, tiled=True)  47.1 us
    all_gather x1, blocking collectives, per_device(): lax.all_gather(texts, ('row', 'col'), axis=0, tiled=True)  39.7 us
    dot_general x1, matrix products, per_device(): jnp.dot(normed_two_b, w_up, preferred_element_type=jnp.float32) + up_bias  30.8 us
    unnamed x1, blocking collectives  30.5 us
    unnamed x6, waiting for transfers between devices  17.6 us
    unnamed x95, local copies, waits for them, and re-layouts  16.8 us
    psum x1, waiting for transfers between devices, per_device(): shares.append(lax.psum(part, 'row').astype(jnp.float32))  15.3 us
  transfers between devices with their start and end apart: 6, of which 4 were waited for; matrix products, arithmetic and copies ran while one was open for 21% of the time, Pallas kernels for 0%

profile of v1, /device:TPU:0, one launch (start us, length us, event | category | flops | bytes accessed | tf_op | source)
XLA Modules:
  0.0 626.8 jit_solution(11565985746575313331)
XLA Ops:
  15.8 4.5 fusion.68
  23.4 5.0 reshape.170
  28.3 4.9 copy.81
  33.2 4.8 reshape.171
  38.0 4.8 copy.82
  42.8 4.8 reshape.169
  47.6 4.8 copy.83
  52.4 10.2 %fusion.76 = (f32[4,12,197]{2,1,0:T(8,128)}, f32[4,12,197,197]{2,3,1,0:T(8,128)}) fusion(pred[4,197]{1,0:T(4,128)(4,1)} %broadcast_compare_fusion, bf16[4,197,12,64]{1,3,2,0:T(8,128)(2,1)} %copy.81, bf16[4,197,12,64]{1,3,2,0:T(8,128)(2,1)} %copy.82), kind=kOutput, calls=%fused_computation.147 | convolution fusion | flops 245894016 | bytes 9910676 | tf_op jit(solution)/shard_map/sub | solution.py:62
  62.6 5.3 fusion.41
  70.3 4.4 convert_element_type.132
  74.7 4.7 fusion.77
  79.4 3.4 reshape.151
  84.9 30.8 %multiply_convert_fusion.1 = (bf16[788,3072]{1,0:T(8,128)(2,1)}, f32[788,3072]{1,0:T(8,128)}, f32[788,3072]{1,0:T(8,128)}) fusion(f32[3072]{0:T(1024)} %param.19, bf16[768,3072]{1,0:T(8,128)(2,1)} %param.16, f32[788,768]{1,0:T(8,128)} %get-tuple-element.55, f32[768]{0:T(1024)} %get-tuple-element.30, f32[768]{0:T(1024)S(1)} %get-tuple-element.23, ...), kind=kOutput, calls=%fused_computation.8 | convolution fusion | flops 3881044992 | bytes 31371424 | tf_op jit(solution)/shard_map/dot_general | solution.py:71
  115.7 5.9 reshape.152
  128.1 4.3 fusion.47
  132.5 47.1 %all-gather = f32[32,4,896]{2,1,0:T(4,128)} all-gather(f32[1,4,896]{2,1,0:T(4,128)S(1)} %maximum_bitcast_fusion), channel_id=1, replica_groups=mesh['row'=2,'col'=16] {'row','col'}, dimensions={0}, use_global_device_ids=true | all-gather | bytes 473088 | tf_op jit(solution)/shard_map/all_gather | solution.py:84
  186.1 39.7 %all-gather.1 = bf16[32,4,512]{2,1,0:T(4,128)(2,1)} all-gather(bf16[1,4,512]{2,1,0:T(4,128)(2,1)S(1)} %bitcast.71), channel_id=1, replica_groups=mesh['row'=2,'col'=16] {'row','col'}, dimensions={0}, use_global_device_ids=true | all-gather | bytes 135168 | tf_op jit(solution)/shard_map/all_gather | solution.py:85
  242.8 3.6 fusion.56
  246.4 5.0 mul.300
  251.5 8.6 %mul.301 = f32[788,3072]{1,0:T(8,128)} reshape(f32[4,197,3072]{2,1,0:T(8,128)} %mul.300) | data formatting | bytes 19365888 | tf_op jit(solution)/shard_map/mul | solution.py:129
  260.1 12.7 %fusion.72 = (bf16[3072]{0:T(1024)(128)(2,1)}, bf16[788,3072]{1,0:T(8,128)(2,1)S(1)}) fusion(f32[788,3072]{1,0:T(8,128)} %get-tuple-element.47, f32[788,3072]{1,0:T(8,128)} %mul.301, f32[788]{0:T(1024)} %mul.285, f32[788,3072]{1,0:T(8,128)} %get-tuple-element.56, f32[3072]{0:T(1024)} %param.19), kind=kLoop, calls=%fused_computation.144 | loop fusion | flops 41149440 | bytes 33911888 | tf_op jit(solution)/shard_map/reduce_sum | solution.py:133
  272.8 10.5 %multiply_reduce_fusion.2 = (bf16[768]{0:T(1024)(128)(2,1)}, f32[788]{0:T(1024)S(1)}, f32[788]{0:T(1024)S(1)}, bf16[768]{0:T(1024)(128)(2,1)}, f32[788,768]{1,0:T(8,128)}) fusion(f32[788,768]{1,0:T(8,128)S(1)} %copy-done.1, f32[788]{0:T(1024)S(1)} %copy-done.32, f32[788]{0:T(1024)S(1)} %broadcast_multiply_fusion.4, f32[768]{0:T(1024)S(1)} %copy-done.26, ...), kind=kOutput, calls=%fused_computation.59 | convolution fusion | flops 3723694080 | bytes 14420288 | tf_op jit(solution)/shard_map/dot_general | solution.py:134
  286.1 3.4 mul.297
  289.5 4.3 convert_reduce_fusion.1
  297.8 4.2 convolution_convert_fusion.2
  302.0 4.9 reshape.172
  306.9 4.9 copy.88
  311.8 7.9 %fusion.79 = (bf16[12,64]{1,0:T(8,128)(2,1)}, bf16[4,197,12,64]{1,3,2,0:T(8,128)(2,1)}) fusion(bf16[4,197,12,64]{1,3,2,0:T(8,128)(2,1)} %copy.88, f32[4,12,197,197]{2,3,1,0:T(8,128)} %get-tuple-element.53, f32[4,12,197]{2,1,0:T(8,128)} %get-tuple-element.52), kind=kOutput, calls=%fused_computation.150 | convolution fusion | flops 243377760 | bytes 9911424 | tf_op jit(solution)/shard_map/nhqk,nqhd->nkhd/dot_general | solution.py:142
  319.7 7.8 %multiply_reduce_fusion = (f32[4,12,197]{2,1,0:T(8,128)}, f32[4,12,197,197]{2,3,1,0:T(8,128)}) fusion(f32[4,12,197,197]{2,3,1,0:T(8,128)} %get-tuple-element.53, f32[4,12,197]{2,1,0:T(8,128)S(1)} %copy-done.16, bf16[4,197,12,64]{1,3,2,0:T(8,128)(2,1)S(1)} %copy-done.10, bf16[4,197,12,64]{1,3,2,0:T(8,128)(2,1)S(1)} %copy-done.9), kind=kOutput, calls=%fused_computation.3 | convolution fusion | flops 244021536 | bytes 17399040 | tf_op jit(solution)/shard_map/nqhd,nkhd->nhqk/dot_general | solution.py:145
  327.6 11.1 %multiply_convert_fusion = bf16[4,12,197,197]{2,3,1,0:T(8,128)(2,1)} fusion(f32[4,12,197,197]{2,3,1,0:T(8,128)} %get-tuple-element.64, f32[4,12,197]{2,1,0:T(8,128)} %get-tuple-element.63, f32[4,12,197,197]{2,3,1,0:T(8,128)} %get-tuple-element.53, f32[4,12,197]{2,1,0:T(8,128)} %get-tuple-element.52), kind=kLoop, calls=%fused_computation.2 | loop fusion | flops 7451328 | bytes 18703968 | tf_op jit(solution)/shard_map/convert_element_type | solution.py:149
  338.7 5.9 fusion.45
  346.9 4.2 reshape.157
  351.2 3.8 copy.95
  355.0 4.4 reshape.156
  359.4 4.1 fusion.78
  365.9 4.2 reshape.155
  374.5 6.0 convolution_convert_fusion.1
  381.2 9.9 %convolution_convert_fusion = bf16[768,3072]{1,0:T(8,128)(2,1)} fusion(bf16[788,3072]{1,0:T(8,128)(2,1)} %copy-done.6, f32[788,768]{1,0:T(8,128)} %get-tuple-element.55, f32[768]{0:T(1024)} %get-tuple-element.30, f32[768]{0:T(1024)} %copy-done.25, f32[788]{0:T(1024)} %copy-done.31, f32[788]{0:T(1024)S(1)} %copy-done.20), kind=kOutput, calls=%fused_computation.23 | convolution fusion | flops 3723635712 | bytes 11993248 | tf_op jit(solution)/shard_map/dot_general | solution.py:132
  395.6 4.2 all-to-all-start
  400.1 8.5 %fusion.27 = (bf16[768]{0:T(1024)(128)(2,1)S(1)}, f32[788]{0:T(1024)}, f32[788]{0:T(1024)}, bf16[768]{0:T(1024)(128)(2,1)S(1)}, f32[788,768]{1,0:T(8,128)}) fusion(bf16[788,768]{1,0:T(8,128)(2,1)} %param.12, f32[788]{0:T(1024)S(1)} %copy-done.30, f32[788]{0:T(1024)S(1)} %copy-done.18, f32[768]{0:T(1024)S(1)} %copy-done.24, ...), kind=kOutput, calls=%fused_computation.51 | convolution fusion | flops 2794736640 | bytes 10819904 | tf_op jit(solution)/shard_map/dot_general | solution.py:161
  419.9 4.4 fusion.26
  425.1 21.1 %reduce-scatter.7.cloned.1.call-done = bf16[48,2304]{1,0:T(8,128)(2,1)} async-done(((bf16[768,2304]{1,0:T(8,128)(2,1)}), bf16[48,2304]{1,0:T(8,128)(2,1)}) %reduce-scatter.7.cloned.1.call-update) | async-done | bytes 221200 | tf_op jit(solution)/shard_map/reduce_scatter | solution.py:180
  446.3 78.3 %reduce-scatter.11.cloned.1.call-done = bf16[48,3072]{1,0:T(8,128)(2,1)} async-done(((bf16[768,3072]{1,0:T(8,128)(2,1)}), bf16[48,3072]{1,0:T(8,128)(2,1)}) %reduce-scatter.11.cloned.1.call-update) | async-done | bytes 294928 | tf_op jit(solution)/shard_map/reduce_scatter | solution.py:180
  530.4 30.5 %all-reduce = bf16[3072]{0:T(1024)(128)(2,1)S(1)} all-reduce(bf16[3072]{0:T(1024)(128)(2,1)S(1)} %copy-done.22), channel_id=6, replica_groups=mesh['row'=2,'col'=16] {'col'}, use_global_device_ids=true, to_apply=%region_39.40.clone | all-reduce | flops 3072 | bytes 12288
  563.5 17.5 %reduce-scatter.13.cloned.1.call-done = bf16[48,8]{1,0:T(8,128)(2,1)} async-done(((bf16[768,8]{1,0:T(8,128)(2,1)}), bf16[48,8]{1,0:T(8,128)(2,1)}) %reduce-scatter.13.cloned.1.call-update) | async-done | bytes 784
  581.8 5.1 all-reduce.1
  589.5 6.5 %all_gather.11 = f32[128,192]{1,0:T(8,128)S(1)} all-gather(f32[64,192]{1,0:T(8,128)} %reshape.159), channel_id=1, replica_groups=mesh['row'=2,'col'=16] {'row'}, dimensions={0}, use_global_device_ids=true | all-gather | bytes 147456 | tf_op jit(solution)/shard_map/all_gather | solution.py:122
  598.3 15.3 %all-reduce.5.cloned.1.call-done = (bf16[48,2304]{1,0:T(8,128)(2,1)}, bf16[48,768]{1,0:T(8,128)(2,1)}, bf16[48,3072]{1,0:T(8,128)(2,1)}) async-done(((bf16[48,2304]{1,0:T(8,128)(2,1)}, bf16[48,768]{1,0:T(8,128)(2,1)}, bf16[48,3072]{1,0:T(8,128)(2,1)}), (bf16[48,2304]{1,0:T(8,128)(2,1)}, bf16[48,768]{1,0:T(8,128)(2,1)}, bf16[48,3072]{1,0:T(8,128)(2,1)})) %all-reduce.5.cloned.1.call-update) | async-done | bytes 589840 | tf_op jit(solution)/shard_map/psum | solution.py:183
  (169 shorter events, 95.4 us)
Async XLA Ops:
  7.2 8.6 %copy-start = (bf16[768,2304]{1,0:T(8,128)(2,1)S(1)}, bf16[768,2304]{1,0:T(8,128)(2,1)}, u32[]{:S(2)}) copy-start(bf16[768,2304]{1,0:T(8,128)(2,1)} %param.14) | copy-start | bytes 10616836
  7.2 417.9 %reduce-scatter.9.cloned.1.call-start = ((), (), s32[]{:S(2)}) async-start(), calls=%async_computation.6 | async-start | bytes 1253376 | tf_op jit(solution)/shard_map/reduce_scatter | solution.py:180
  12.4 7.9 %copy-start.23 = (f32[768]{0:T(1024)}, f32[768]{0:T(1024)S(1)}, u32[]{:S(2)}) copy-start(f32[768]{0:T(1024)S(1)} %get-tuple-element.28) | copy-start | bytes 9220
  12.4 7.9 %copy-start.37 = (f32[768]{0:T(1024)}, f32[768]{0:T(1024)S(1)}, u32[]{:S(2)}) copy-start(f32[768]{0:T(1024)S(1)} %get-tuple-element.27) | copy-start | bytes 9220
  12.4 72.5 %copy-start.25 = (f32[768]{0:T(1024)}, f32[768]{0:T(1024)S(1)}, u32[]{:S(2)}) copy-start(f32[768]{0:T(1024)S(1)} %get-tuple-element.23) | copy-start | bytes 9220
  14.0 6.4 %copy-start.17 = (f32[788]{0:T(1024)}, f32[788]{0:T(1024)S(1)}, u32[]{:S(2)}) copy-start(f32[788]{0:T(1024)S(1)} %broadcast_multiply_fusion.5) | copy-start | bytes 9460
  15.8 4.6 copy-start.28
  79.4 210.0 %copy-start.19 = (f32[788]{0:T(1024)}, f32[788]{0:T(1024)S(1)}, u32[]{:S(2)}) copy-start(f32[788]{0:T(1024)S(1)} %broadcast_multiply_fusion.4) | copy-start | bytes 9460
  84.9 30.8 %copy-start.31 = (f32[788]{0:T(1024)}, f32[788]{0:T(1024)S(1)}, u32[]{:S(2)}) copy-start(f32[788]{0:T(1024)S(1)} %add_rsqrt_fusion) | copy-start | bytes 9460
  122.3 5.8 copy-start.34
  122.3 5.8 copy-start.36
  127.5 0.6 copy-start.14
  128.1 58.0 %copy-start.39 = (bf16[4,512]{1,0:T(4,128)(2,1)S(1)}, bf16[4,512]{1,0:T(4,128)(2,1)}, u32[]{:S(2)}) copy-start(bf16[4,512]{1,0:T(4,128)(2,1)} %param.21) | copy-start | bytes 12292
  132.4 99.5 %copy-start.40 = (s32[128]{0:T(128)S(1)}, s32[128]{0:T(128)}, u32[]{:S(2)}) copy-start(s32[128]{0:T(128)} %param.22) | copy-start | bytes 1540
  185.4 52.5 %copy-start.35 = (f32[128]{0:T(128)}, f32[128]{0:T(128)S(1)}, u32[]{:S(2)}) copy-start(f32[128]{0:T(128)S(1)} %add_rsqrt_fusion.2) | copy-start | bytes 1540
  237.9 0.7 copy-start.12
  237.9 0.7 copy-start.41
  240.7 0.7 copy-start.15
  260.1 12.7 %copy-start.1 = (f32[788,768]{1,0:T(8,128)S(1)}, f32[788,768]{1,0:T(8,128)}, u32[]{:S(2)}) copy-start(f32[788,768]{1,0:T(8,128)} %get-tuple-element.55) | copy-start | bytes 7262212
  260.1 12.7 %copy-start.26 = (f32[768]{0:T(1024)S(1)}, f32[768]{0:T(1024)}, u32[]{:S(2)}) copy-start(f32[768]{0:T(1024)} %copy-done.25) | copy-start | bytes 9220
  260.1 12.7 %copy-start.32 = (f32[788]{0:T(1024)S(1)}, f32[788]{0:T(1024)}, u32[]{:S(2)}) copy-start(f32[788]{0:T(1024)} %copy-done.31) | copy-start | bytes 9460
  272.8 10.5 %copy-start.6 = (bf16[788,3072]{1,0:T(8,128)(2,1)}, bf16[788,3072]{1,0:T(8,128)(2,1)S(1)}, u32[]{:S(2)}) copy-start(bf16[788,3072]{1,0:T(8,128)(2,1)S(1)} %get-tuple-element.37) | copy-start | bytes 14524420
  286.1 3.4 copy-start.21
  286.1 3.4 copy-start.27
  286.1 3.4 copy-start.33
  289.5 5.8 copy-start.11
  293.8 1.4 copy-start.3
  297.7 148.5 %reduce-scatter.7.cloned.1.call-start = ((), (), s32[]{:S(2)}) async-start(), calls=%async_computation.5 | async-start | bytes 3760128 | tf_op jit(solution)/shard_map/reduce_scatter | solution.py:180
  311.8 7.9 %copy-start.9 = (bf16[4,197,12,64]{1,3,2,0:T(8,128)(2,1)S(1)}, bf16[4,197,12,64]{1,3,2,0:T(8,128)(2,1)}, u32[]{:S(2)}) copy-start(bf16[4,197,12,64]{1,3,2,0:T(8,128)(2,1)} %copy.83) | copy-start | bytes 3631108
  311.8 7.9 %copy-start.10 = (bf16[4,197,12,64]{1,3,2,0:T(8,128)(2,1)S(1)}, bf16[4,197,12,64]{1,3,2,0:T(8,128)(2,1)}, u32[]{:S(2)}) copy-start(bf16[4,197,12,64]{1,3,2,0:T(8,128)(2,1)} %copy.88) | copy-start | bytes 3631108
  311.8 7.9 %copy-start.16 = (f32[4,12,197]{2,1,0:T(8,128)S(1)}, f32[4,12,197]{2,1,0:T(8,128)}, u32[]{:S(2)}) copy-start(f32[4,12,197]{2,1,0:T(8,128)} %get-tuple-element.52) | copy-start | bytes 113476
  338.7 5.9 copy-start.8
  370.1 1.8 copy-start.5
  370.1 2.2 copy-start.4
  371.8 2.6 copy-start.2
  371.8 2.6 copy-start.18
  371.8 2.6 copy-start.24
  371.8 2.6 copy-start.29
  371.8 2.6 copy-start.38
  372.5 2.0 copy-start.13
  380.5 0.7 copy-start.20
  380.5 144.0 %reduce-scatter.11.cloned.1.call-start = ((), (), s32[]{:S(2)}) async-start(), calls=%async_computation.7 | async-start | bytes 5013504 | tf_op jit(solution)/shard_map/reduce_scatter | solution.py:180
  391.1 9.0 %copy-start.30 = (f32[788]{0:T(1024)S(1)}, f32[788]{0:T(1024)}, u32[]{:S(2)}) copy-start(f32[788]{0:T(1024)} %copy-done.28) | copy-start | bytes 9460
  395.6 192.4 %all-to-all-start = ((f32[16,4,192]{2,1,0:T(4,128)}), f32[16,4,192]{2,1,0:T(4,128)}, u32[]{:S(2)}, u32[]{:S(2)}) async-start(f32[16,4,192]{2,1,0:T(4,128)} %copy.99), calls=%async_computation.3 | async-start | bytes 131072 | tf_op jit(solution)/shard_map/all_to_all | solution.py:120
  399.8 181.2 %reduce-scatter.13.cloned.1.call-start = ((), (), s32[]{:S(2)}) async-start(), calls=%async_computation.8 | async-start | bytes 208896
  418.5 195.1 %all-reduce.5.cloned.1.call-start = ((), (), s32[]{:S(2)}) async-start(), calls=%async_computation.9 | async-start | bytes 1179648 | tf_op jit(solution)/shard_map/psum | solution.py:183
  419.9 4.4 copy-start.7
  419.9 110.5 %copy-start.22 = (bf16[3072]{0:T(1024)(128)(2,1)S(1)}, bf16[3072]{0:T(1024)(128)(2,1)}, u32[]{:S(2)}) copy-start(bf16[3072]{0:T(1024)(128)(2,1)} %get-tuple-element.36) | copy-start | bytes 18436
  (1 other events, 0.6 us)
Sparse Core Ops, SparseCore 0:
  297.9 55.5 reduce-scatter.8
  380.6 65.5 reduce-scatter.6
  450.1 74.4 reduce-scatter.10
  528.3 52.6 reduce-scatter.12
  583.4 30.1 all-reduce.4

commit v2 on v1

v2 whole, which is shorter than its diff:
```python
import functools

import jax
import jax.numpy as jnp
from jax import lax
from jax.experimental import pallas as pl
from jax.experimental.pallas import tpu as pltpu
from jax.sharding import PartitionSpec as P

HIGH = lax.Precision.HIGHEST

D = 768
HEADS = 12
HEAD_DIM = 64
SEQ = 197
ROWS = 208
WIN = 256
TILE = 256
F32 = jnp.float32
BF = jnp.bfloat16
NT = (((1,), (1,)), ((), ()))
TN = (((0,), (0,)), ((), ()))


def mm(a, b, dims=(((1,), (0,)), ((), ()))):
    return lax.dot_general(a, b, dims, preferred_element_type=F32)


def head_masks():
    lane = lax.broadcasted_iota(jnp.int32, (1, TILE), 1) // HEAD_DIM
    return [(lane == h).astype(F32).astype(BF) for h in range(TILE // HEAD_DIM)]


def gelu_pair(u):
    z = jnp.abs(u)
    t = 1.0 / (1.0 + (0.3275911 * 0.7071067811865476) * z)
    e = jnp.exp(-0.5 * (u * u))
    poly = 0.5 * 1.061405429
    for c in (-1.453152027, 1.421413741, -0.284496736, 0.254829592):
        poly = poly * t + 0.5 * c
    tail = poly * t * e
    cdf = jnp.where(u >= 0.0, 1.0 - tail, tail)
    return u * cdf, cdf + (0.3989422804014327 * u) * e


def forward_kernel(
    images, ff,
    tok_ref, keep_ref, wqkv_h, wout_h, wup_h, wdown_h, vec_ref, upb_ref,
    h1_h, qkv_h, p_h, o_h, h2_h, xh2_h, rstd_h, gk_h, apool_ref, pooled_ref,
    wqkv, wout, wup, wdown, xs, h1, qkv, p_s, o_s, h2, xh2, rstd, gk, a_s, keep8, kmask, kcol, bias, acc,
    in_sem, out_sem,
):
    n_quads = D // TILE
    n_ff = ff // TILE
    loads = []
    for k, (src, dst) in enumerate(((wqkv_h, wqkv), (wout_h, wout), (wup_h, wup), (wdown_h, wdown))):
        c = pltpu.make_async_copy(src, dst, in_sem.at[k])
        c.start()
        loads.append(c)
    stores = []

    def send(k, src, dst):
        c = pltpu.make_async_copy(src, dst, out_sem.at[k])
        c.start()
        stores.append(c)

    total = images * SEQ
    last = total // 16 * 16
    xs[last:, :] = jnp.zeros_like(xs[last:, :])
    xs[0:last, :] = tok_ref[0:last, :].astype(F32)
    if last < total:
        xs[last:total, :] = tok_ref[last:total, :].astype(F32)
    keep8[...] = jnp.zeros_like(keep8)
    keep8[0:images, 0:SEQ] = keep_ref[...].astype(F32)
    kb = keep8[...]
    rid = lax.broadcasted_iota(jnp.int32, kb.shape, 0)
    for i in range(images):
        kmask[i] = jnp.where(rid == i, kb, 0.0).astype(BF)
        one = jnp.ones((kb.shape[0], 128), F32).astype(BF)
        kcol[i * ROWS:(i + 1) * ROWS, :] = mm(kmask[i], one, TN)[0:ROWS]
    bias[0:1, 0:D] = vec_ref[2:3, :]
    bias[0:1, D:2 * D] = jnp.zeros((1, D), F32)
    bias[0:1, 2 * D:] = vec_ref[3:4, :]
    for i in range(images):
        x = xs[i * SEQ:i * SEQ + ROWS, :]
        cen = x - jnp.mean(x, axis=1, keepdims=True)
        inv = lax.rsqrt(jnp.mean(cen * cen, axis=1, keepdims=True) + 1e-6)
        h1[i * ROWS:(i + 1) * ROWS, :] = (cen * inv * vec_ref[0:1, :] + vec_ref[1:2, :]).astype(BF)
    send(0, h1, h1_h)
    loads[0].wait()
    span = images * ROWS
    pad = qkv.shape[1] - span
    for t in range(3 * n_quads):
        qkv[t, span:, :] = jnp.zeros((pad, TILE), BF)

    def proj(t, _):
        col = pl.multiple_of(t * TILE, TILE)
        r = mm(h1[...], wqkv[:, pl.ds(col, TILE)]) + bias[0:1, pl.ds(col, TILE)]
        r = r * jnp.where(t < n_quads, HEAD_DIM ** -0.5, 1.0)
        qkv[t, 0:span, :] = r.astype(BF)
        return 0

    lax.fori_loop(0, 3 * n_quads, proj, 0)
    send(1, qkv, qkv_h)
    masks = head_masks()

    def attend(it, _):
        i = it // n_quads
        j = it % n_quads
        r0 = pl.multiple_of(i * ROWS, 16)
        q4 = qkv[j, pl.ds(r0, ROWS), :]
        k4 = qkv[n_quads + j, pl.ds(r0, WIN), :]
        v4 = qkv[2 * n_quads + j, pl.ds(r0, WIN), :]
        valid = keep8[pl.ds(i, 1), :] > 0.0
        out = jnp.zeros((ROWS, TILE), F32)
        for h, m in enumerate(masks):
            s = mm(q4 * m, k4, NT)
            s = jnp.where(valid, s, -1e30)
            e = jnp.exp(s - jnp.max(s, axis=1, keepdims=True))
            pb = (e * (1.0 / jnp.sum(e, axis=1, keepdims=True))).astype(BF)
            p_s[it, h * ROWS:(h + 1) * ROWS, :] = pb
            out = out + mm(pb, v4 * m)
        o_s[j, pl.ds(r0, ROWS), :] = out.astype(BF)
        return 0

    lax.fori_loop(0, images * n_quads, attend, 0)
    send(2, p_s, p_h)
    send(3, o_s, o_h)
    loads[1].wait()
    pooled_ref[...] = jnp.zeros_like(pooled_ref)
    for i in range(images):
        rows = slice(i * ROWS, (i + 1) * ROWS)
        x = xs[i * SEQ:i * SEQ + ROWS, :]
        y = x + vec_ref[4:5, :]
        for j in range(n_quads):
            y = y + mm(o_s[j, rows, :], wout[j * TILE:(j + 1) * TILE, :])
        kc = kcol[rows, 0:1]
        pooled_ref[i:i + 1, 0:D] = jnp.sum(y * kc, axis=0, keepdims=True)
        cen = y - jnp.mean(y, axis=1, keepdims=True)
        inv = lax.rsqrt(jnp.mean(cen * cen, axis=1, keepdims=True) + 1e-6)
        xh = cen * inv
        xh2[rows, :] = xh.astype(BF)
        rstd[rows, :] = jnp.broadcast_to(inv, (ROWS, 128))
        h2[rows, :] = (xh * vec_ref[5:6, :] + vec_ref[6:7, :]).astype(BF)
    send(4, h2, h2_h)
    send(5, xh2, xh2_h)
    send(6, rstd, rstd_h)
    loads[2].wait()
    loads[3].wait()
    acc[...] = jnp.zeros_like(acc)
    a_s[span:, :] = jnp.zeros((a_s.shape[0] - span, TILE), BF)

    def feed(t, _):
        col = pl.multiple_of(t * TILE, TILE)
        ub = upb_ref[0:1, pl.ds(col, TILE)]
        for i in range(images):
            rows = slice(i * ROWS, (i + 1) * ROWS)
            u = mm(h2[rows, :], wup[:, pl.ds(col, TILE)]) + ub
            a, g = gelu_pair(u)
            a_s[rows, :] = a.astype(BF)
            gk[t, rows, :] = (g * kcol[rows, 0:1]).astype(BF)
        ap = jnp.zeros((kmask.shape[1], TILE), F32)
        for i in range(images):
            ap = ap + mm(kmask[i], a_s[i * ROWS:i * ROWS + WIN, :])
        apool_ref[t] = ap
        hi = ap.astype(BF)
        lo = (ap - hi.astype(F32)).astype(BF)
        w = wdown[pl.ds(col, TILE), :]
        acc[...] += mm(hi, w) + mm(lo, w)
        pltpu.make_async_copy(gk.at[t], gk_h.at[t], out_sem.at[7]).start()
        return 0

    lax.fori_loop(0, n_ff, feed, 0)
    cnt = jnp.sum(kb, axis=1, keepdims=True)[0:8]
    inv = 1.0 / jnp.maximum(cnt, 1.0)
    pooled_ref[:, 0:D] = (pooled_ref[:, 0:D] + acc[0:8, :]) * inv + vec_ref[7:8, :]
    pooled_ref[:, D:] = jnp.broadcast_to(cnt, (8, 128))
    for c in stores:
        c.wait()
    for t in range(n_ff):
        pltpu.make_async_copy(gk.at[t], gk_h.at[t], out_sem.at[7]).wait()


def forward_call(images, ff, tokens, keep, wqkv, wout, wup, wdown, vec, upb):
    span = images * ROWS
    nq = D // TILE
    wide = span + WIN - ROWS
    outs = [
        ((span, D), BF), ((3 * nq, wide, TILE), BF), ((images * nq, 4 * ROWS, TILE), BF),
        ((nq, span, TILE), BF), ((span, D), BF), ((span, D), BF), ((span, 128), F32),
        ((ff // TILE, span, TILE), BF), ((ff // TILE, 16, TILE), F32), ((8, D + 128), F32),
    ]
    anyspec = pl.BlockSpec(memory_space=pl.ANY)
    vm = pl.BlockSpec(memory_space=pltpu.VMEM)
    scratch = [
        pltpu.VMEM((D, 3 * D), BF), pltpu.VMEM((D, D), BF), pltpu.VMEM((D, ff), BF), pltpu.VMEM((ff, D), BF),
        pltpu.VMEM(((images - 1) * SEQ + ROWS + 7 & -8, D), F32),
    ] + [pltpu.VMEM(*o) for o in outs[:8]] + [
        pltpu.VMEM((wide, TILE), BF), pltpu.VMEM((16, WIN), F32), pltpu.VMEM((images, 16, WIN), BF),
        pltpu.VMEM((span, 128), F32), pltpu.VMEM((1, 3 * D), F32), pltpu.VMEM((16, D), F32),
        pltpu.SemaphoreType.DMA((4,)), pltpu.SemaphoreType.DMA((8,)),
    ]
    return pl.pallas_call(
        functools.partial(forward_kernel, images, ff),
        out_shape=[jax.ShapeDtypeStruct(s, d) for s, d in outs],
        in_specs=[vm, vm] + [anyspec] * 4 + [vm, vm],
        out_specs=[anyspec] * 8 + [vm, vm],
        scratch_shapes=scratch,
        compiler_params=pltpu.CompilerParams(vmem_limit_bytes=60 * 2**20),
        name="block_forward",
    )(tokens, keep, wqkv, wout, wup, wdown, vec, upb)


def backward_kernel(
    images, ff,
    tok_ref, keep_ref, dy_ref, vec_ref,
    wqkv_h, wout_h, wup_h, wdown_h, h1_h, qkv_h, p_h, o_h, h2_h, xh2_h, rstd_h, gk_h,
    tg_ref, g_ref, vg_ref, ub_ref,
    wqkv, wout, wup, wdown, h1, qkv, p_s, o_s, h2, xh2, rstd, du,
    xs, dx, db, do_s, dp_s, h1t, h2t, keep8, kcol, da_s,
    in_sem, gk_sem, p_sem,
):
    n_quads = D // TILE
    n_ff = ff // TILE
    span = images * ROWS
    masks = head_masks()
    loads = {}
    for k, (name, src, dst) in enumerate((
        ("wdown", wdown_h, wdown), ("h2", h2_h, h2), ("wup", wup_h, wup), ("xh2", xh2_h, xh2),
        ("rstd", rstd_h, rstd), ("wout", wout_h, wout), ("o", o_h, o_s), ("qkv", qkv_h, qkv),
        ("h1", h1_h, h1), ("wqkv", wqkv_h, wqkv),
    )):
        loads[name] = pltpu.make_async_copy(src, dst, in_sem.at[k])
    for name in ("wdown", "h2"):
        loads[name].start()
    gks = []
    for t in range(n_ff):
        c = pltpu.make_async_copy(gk_h.at[t], du.at[:, t * TILE:(t + 1) * TILE], gk_sem.at[t])
        c.start()
        gks.append(c)
    for name in ("wup", "xh2", "rstd", "wout", "o", "qkv", "h1", "wqkv"):
        loads[name].start()

    def pcopy(i, j, slot):
        return pltpu.make_async_copy(p_h.at[i * n_quads + j], p_s.at[slot], p_sem.at[slot])

    pcopy(0, 0, 0).start()

    total = images * SEQ
    last = total // 16 * 16
    xs[last:, :] = jnp.zeros_like(xs[last:, :])
    xs[0:last, :] = tok_ref[0:last, :].astype(F32)
    if last < total:
        xs[last:total, :] = tok_ref[last:total, :].astype(F32)
    keep8[...] = jnp.zeros_like(keep8)
    keep8[0:images, 0:SEQ] = keep_ref[...].astype(F32)
    kb = keep8[...]
    rid = lax.broadcasted_iota(jnp.int32, kb.shape, 0)
    one = jnp.ones((kb.shape[0], 128), F32).astype(BF)
    for i in range(images):
        km = jnp.where(rid == i, kb, 0.0).astype(BF)
        kcol[i * ROWS:(i + 1) * ROWS, :] = mm(km, one, TN)[0:ROWS]

    dy = dy_ref[...]
    dyb = dy.astype(BF)
    cnt = jnp.sum(kb, axis=1, keepdims=True)[0:8]
    vg_ref[7:8, :] = jnp.sum(dyb.astype(F32) * cnt, axis=0, keepdims=True)
    dy16 = jnp.concatenate([dyb, jnp.zeros((8, D), BF)], axis=0)
    loads["wdown"].wait()

    def spread(t, _):
        col = pl.multiple_of(t * TILE, TILE)
        da_s[:, pl.ds(col, TILE)] = mm(dy16, wdown[pl.ds(col, TILE), :], NT)
        return 0

    lax.fori_loop(0, n_ff, spread, 0)
    loads["h2"].wait()
    h2t[...] = h2[...].T
    for c in gks:
        c.wait()

    def expand(t, _):
        col = pl.multiple_of(t * TILE, TILE)
        ub = jnp.zeros((1, TILE), F32)
        for i in range(images):
            rows = slice(i * ROWS, (i + 1) * ROWS)
            d = du[rows, pl.ds(col, TILE)].astype(F32) * da_s[i:i + 1, pl.ds(col, TILE)]
            ub = ub + jnp.sum(d, axis=0, keepdims=True)
            du[rows, pl.ds(col, TILE)] = d.astype(BF)
        ub_ref[:, pl.ds(col, TILE)] = ub
        part = mm(h2t[...], du[:, pl.ds(col, TILE)])
        c3 = pl.multiple_of((t % 3) * TILE, TILE)
        g_ref[t // 3, :, pl.ds(c3, TILE)] = part.astype(BF)
        return 0

    lax.fori_loop(0, n_ff, expand, 0)
    loads["wup"].wait()

    def down(n, _):
        col = pl.multiple_of(n * TILE, TILE)
        dx[:, pl.ds(col, TILE)] = mm(du[...], wup[pl.ds(col, TILE), :], NT)
        return 0

    lax.fori_loop(0, n_quads, down, 0)
    for name in ("xh2", "rstd", "wout", "o"):
        loads[name].wait()
    g2 = jnp.zeros((1, D), F32)
    b2 = jnp.zeros((1, D), F32)
    bo = jnp.zeros((1, D), F32)
    for i in range(images):
        rows = slice(i * ROWS, (i + 1) * ROWS)
        dh = dx[rows, :]
        xh = xh2[rows, :].astype(F32)
        g2 = g2 + jnp.sum(dh * xh, axis=0, keepdims=True)
        b2 = b2 + jnp.sum(dh, axis=0, keepdims=True)
        c = dh * vec_ref[5:6, :]
        m1 = jnp.mean(c, axis=1, keepdims=True)
        m2 = jnp.mean(c * xh, axis=1, keepdims=True)
        r = dy[i:i + 1, :] * kcol[rows, 0:1] + rstd[rows, 0:1] * (c - m1 - xh * m2)
        dx[rows, :] = r
        rb = r.astype(BF)
        db[rows, :] = rb
        bo = bo + jnp.sum(rb.astype(F32), axis=0, keepdims=True)
    vg_ref[5:6, :] = g2
    vg_ref[6:7, :] = b2
    vg_ref[4:5, :] = bo
    for j in range(n_quads):
        sl = slice(j * TILE, (j + 1) * TILE)
        do_s[j] = mm(db[...], wout[sl, :], NT).astype(BF)
        for n in range(n_quads):
            g_ref[4, sl, n * TILE:(n + 1) * TILE] = mm(
                o_s[j], db[:, n * TILE:(n + 1) * TILE], TN).astype(BF)
    for name in ("qkv", "h1"):
        loads[name].wait()
    h1t[...] = h1[...].T

    def quad(j, _):
        def attend(i, _):
            r0 = pl.multiple_of(i * ROWS, 16)
            step = j * images + i
            slot = step % 2
            nxt = step + 1

            @pl.when(nxt < n_quads * images)
            def _():
                pcopy(nxt % images, nxt // images, nxt % 2).start()

            pcopy(i, j, slot).wait()
            q4 = qkv[j, pl.ds(r0, ROWS), :]
            k4 = qkv[n_quads + j, pl.ds(r0, WIN), :]
            v4 = qkv[2 * n_quads + j, pl.ds(r0, WIN), :]
            d4 = do_s[j, pl.ds(r0, ROWS), :]
            dq = jnp.zeros((ROWS, TILE), F32)
            dk = jnp.zeros((WIN, TILE), F32)
            dv = jnp.zeros((WIN, TILE), F32)
            for h, m in enumerate(masks):
                pb = p_s[slot, h * ROWS:(h + 1) * ROWS, :]
                dm = d4 * m
                dv = dv + mm(pb, dm, TN)
                dpr = mm(dm, v4, NT)
                pf = pb.astype(F32)
                ds = (pf * (dpr - jnp.sum(pf * dpr, axis=1, keepdims=True))).astype(BF)
                dq = dq + mm(ds, k4 * m)
                dk = dk + mm(ds, q4 * m, TN)
            dq = dq * HEAD_DIM ** -0.5
            for s, val in enumerate((dq, dk[0:ROWS], dv[0:ROWS])):
                col = pl.multiple_of(s * D + j * TILE, TILE)
                dp_s[pl.ds(r0, ROWS), pl.ds(col, TILE)] = val.astype(BF)
            return 0

        lax.fori_loop(0, images, attend, 0)
        for s in range(3):
            col = pl.multiple_of(s * D + j * TILE, TILE)
            g_ref[5 + j, :, s * TILE:(s + 1) * TILE] = mm(h1t[...], dp_s[:, pl.ds(col, TILE)]).astype(BF)
        return 0

    lax.fori_loop(0, n_quads, quad, 0)
    vg_ref[2:3, :] = jnp.sum(dp_s[:, 0:D].astype(F32), axis=0, keepdims=True)
    vg_ref[3:4, :] = jnp.sum(dp_s[:, 2 * D:].astype(F32), axis=0, keepdims=True)
    loads["wqkv"].wait()
    g1 = jnp.zeros((1, D), F32)
    b1 = jnp.zeros((1, D), F32)
    for i in range(images):
        rows = slice(i * ROWS, (i + 1) * ROWS)
        dh = mm(dp_s[rows, :], wqkv[...], NT)
        x = xs[i * SEQ:i * SEQ + ROWS, :]
        cen = x - jnp.mean(x, axis=1, keepdims=True)
        inv = lax.rsqrt(jnp.mean(cen * cen, axis=1, keepdims=True) + 1e-6)
        xh = cen * inv
        g1 = g1 + jnp.sum(dh * xh, axis=0, keepdims=True)
        b1 = b1 + jnp.sum(dh, axis=0, keepdims=True)
        c = dh * vec_ref[0:1, :]
        m1 = jnp.mean(c, axis=1, keepdims=True)
        m2 = jnp.mean(c * xh, axis=1, keepdims=True)
        r = dx[rows, :] + inv * (c - m1 - xh * m2)
        tg_ref[i * SEQ:(i + 1) * SEQ, :] = r[0:SEQ]
    vg_ref[0:1, :] = g1
    vg_ref[1:2, :] = b1


def backward_call(images, ff, tokens, keep, dy, vec, wqkv, wout, wup, wdown, acts):
    span = images * ROWS
    nq = D // TILE
    wide = span + WIN - ROWS
    anyspec = pl.BlockSpec(memory_space=pl.ANY)
    vm = pl.BlockSpec(memory_space=pltpu.VMEM)
    outs = [((images * SEQ, D), F32), ((ff // D + 4, D, D), BF), ((8, D), F32), ((1, ff), F32)]
    scratch = [
        pltpu.VMEM((D, 3 * D), BF), pltpu.VMEM((D, D), BF), pltpu.VMEM((D, ff), BF), pltpu.VMEM((ff, D), BF),
        pltpu.VMEM((span, D), BF), pltpu.VMEM((3 * nq, wide, TILE), BF), pltpu.VMEM((2, 4 * ROWS, TILE), BF),
        pltpu.VMEM((nq, span, TILE), BF), pltpu.VMEM((span, D), BF), pltpu.VMEM((span, D), BF),
        pltpu.VMEM((span, 128), F32), pltpu.VMEM((span, ff), BF),
        pltpu.VMEM(((images - 1) * SEQ + ROWS + 7 & -8, D), F32), pltpu.VMEM((span, D), F32),
        pltpu.VMEM((span, D), BF), pltpu.VMEM((nq, span, TILE), BF), pltpu.VMEM((span, 3 * D), BF),
        pltpu.VMEM((D, span), BF), pltpu.VMEM((D, span), BF), pltpu.VMEM((16, WIN), F32),
        pltpu.VMEM((span, 128), F32), pltpu.VMEM((16, ff), F32),
        pltpu.SemaphoreType.DMA((10,)), pltpu.SemaphoreType.DMA((ff // TILE,)), pltpu.SemaphoreType.DMA((2,)),
    ]
    return pl.pallas_call(
        functools.partial(backward_kernel, images, ff),
        out_shape=[jax.ShapeDtypeStruct(s, d) for s, d in outs],
        in_specs=[vm] * 4 + [anyspec] * 12,
        out_specs=[vm] * 4,
        scratch_shapes=scratch,
        compiler_params=pltpu.CompilerParams(vmem_limit_bytes=62 * 2**20),
        name="block_backward",
    )(tokens, keep, dy, vec, wqkv, wout, wup, wdown, *acts)


def per_device(
    tokens,
    keep_mask,
    w_qkv,
    w_out,
    w_up,
    w_down,
    vectors,
    up_bias,
    w_proj,
    texts,
    pair_index,
    logit_scale,
):
    images = keep_mask.shape[0]
    rows = tokens.shape[0]
    total_images = pair_index.shape[0]
    ff = w_up.shape[1]
    acts = forward_call(
        images, ff, tokens, keep_mask, w_qkv, w_out, w_up, w_down, vectors, up_bias.reshape(1, ff)
    )
    activ_sum = acts[8].transpose(1, 0, 2).reshape(16, ff)[:images]
    sent = acts[9][:images]
    gathered = lax.all_gather(sent, ("row", "col"), axis=0, tiled=True)
    all_texts = lax.all_gather(texts, ("row", "col"), axis=0, tiled=True).astype(jnp.float32)
    pooled_all, counts_all = gathered[:, :D], gathered[:, D : D + 1]
    proj_float = w_proj.astype(jnp.float32)
    latent = jnp.dot(pooled_all, proj_float, precision=HIGH)
    inv_norm = lax.rsqrt(jnp.sum(latent * latent, axis=-1, keepdims=True) + 1e-06)
    embeds = latent * inv_norm
    embeds_f = embeds.astype(jnp.bfloat16).astype(jnp.float32)
    logit_mult = logit_scale[0]
    first_image = lax.axis_index(("row", "col")) * images
    all_ids = jnp.arange(total_images, dtype=jnp.int32)
    match = (pair_index[:, None] == all_ids[None, :]).astype(jnp.float32)
    logits = logit_mult * jnp.dot(
        embeds_f.astype(jnp.bfloat16), all_texts.astype(jnp.bfloat16).T,
        preferred_element_type=jnp.float32,
    )
    row_lse = jax.nn.logsumexp(logits, axis=1)
    col_lse = jax.nn.logsumexp(logits, axis=0)
    summed = 0.5 * (jnp.sum(row_lse) + jnp.sum(col_lse)) - jnp.sum(logits * match)
    grad_logits = (
        0.5 * jnp.exp(logits - row_lse[:, None]) + 0.5 * jnp.exp(logits - col_lse[None, :]) - match
    )
    embed_grad = logit_mult * jnp.dot(grad_logits, all_texts, precision=HIGH)
    own_cols = lax.dynamic_slice_in_dim(grad_logits, first_image, images, axis=1)
    text_grad = logit_mult * jnp.dot(own_cols.T, embeds_f, precision=HIGH)
    grad_latent = inv_norm * (
        embed_grad - embeds * jnp.sum(embeds * embed_grad, axis=-1, keepdims=True)
    )
    shards = lax.axis_size("col")
    mine = lax.axis_index("col")
    own_pooled = lax.dynamic_slice_in_dim(pooled_all, mine * (D // shards), D // shards, axis=1)
    grad_proj = jnp.dot(own_pooled.T, grad_latent, precision=HIGH)
    grad_pooled = jnp.dot(grad_latent, proj_float.T, precision=HIGH)
    image_grads = (grad_pooled / counts_all).astype(jnp.bfloat16)
    pieces = activ_sum.reshape(images, shards, ff // shards).transpose(1, 0, 2)
    pieces = lax.all_to_all(pieces, "col", split_axis=0, concat_axis=0, tiled=True)
    pieces = pieces.reshape(images * shards, ff // shards)
    pieces = lax.all_gather(pieces, "row", axis=0, tiled=True)
    grad_down = jnp.dot(pieces.T, image_grads.astype(jnp.float32), precision=HIGH)
    own_grads = lax.dynamic_slice_in_dim(grad_pooled / counts_all, first_image, images)
    dy = jnp.concatenate([own_grads, jnp.zeros((8 - images, D), jnp.float32)], axis=0)
    token_grad, grads, grad_vectors, grad_up_bias = backward_call(
        images, ff, tokens, keep_mask, dy, vectors, w_qkv, w_out, w_up, w_down, acts[:8]
    )
    part = lax.psum_scatter(grads, "col", scatter_dimension=1, tiled=True)
    part = lax.psum(part, "row").astype(jnp.float32)
    n_up = ff // D
    up_share = part[:n_up].transpose(1, 0, 2).reshape(-1, ff)
    out_share = part[n_up]
    qkv_share = part[n_up + 1 :].reshape(D // TILE, -1, 3, TILE).transpose(1, 2, 0, 3)
    qkv_share = qkv_share.reshape(-1, 3 * D)
    small = jnp.concatenate([grad_vectors, grad_up_bias.reshape(ff // D, D)], axis=0)
    small = lax.psum(small, ("row", "col"))
    vec_share = lax.dynamic_slice_in_dim(small[:8], mine * (D // shards), D // shards, axis=1)
    bias_share = lax.dynamic_slice_in_dim(small[8:].reshape(ff), mine * (ff // shards), ff // shards)
    loss = (summed / total_images).reshape(1)
    return (
        loss,
        token_grad,
        qkv_share,
        out_share,
        up_share,
        grad_down,
        vec_share,
        bias_share,
        grad_proj,
        text_grad,
    )


def solution(mesh):
    in_specs = (
        P(("row", "col"), None),
        P(("row", "col"), None),
        P(),
        P(),
        P(),
        P(),
        P(),
        P(),
        P(),
        P(("row", "col"), None),
        P(),
        P(),
    )
    out_specs = (
        P(),
        P(("row", "col"), None),
        P("col", None),
        P("col", None),
        P("col", None),
        P("col", None),
        P(None, "col"),
        P("col"),
        P("col", None),
        P(("row", "col"), None),
    )
    return jax.shard_map(
        per_device, mesh=mesh, in_specs=in_specs, out_specs=out_specs, check_vma=False
    )
```

time: 633 us -> 345 us (0.55)
  matrix products: 148 us -> 5.37 us
  local copies, waits for them, and re-layouts: 133 us -> 9.2 us
  Pallas kernels: 0 us -> 94.1 us
  other arithmetic: 61.3 us -> 3.26 us
  waiting for transfers between devices: 132 us -> 82.5 us
    dot_general x17 -> x0, matrix products: 124 us -> none  [the longest x1 30.8 us: per_device(): jnp.dot(normed_two_b, w_up, preferred_element_type=jnp.float32) + up_bias]
    pallas_call x0 -> x2, Pallas kernels: none -> 94.1 us  [the longest x1 55.2 us: backward_call(): pl.pallas_call(functools.partial(backward_kernel, images, ff), out_shape=...]
    reshape x13 -> x5, local copies, waits for them, and re-layouts: 61 us -> 2.19 us  [the longest x1 1.07 us: per_device(): qkv_share = qkv_share.reshape(-1, 3 * D)]
    reduce_scatter x3 -> x1, waiting for transfers between devices: 99.4 us -> 58 us  [per_device(): part = lax.psum_scatter(grads, 'col', scatter_dimension=1, tiled=True)]
    psum x1, blocking collectives: 5.06 us -> 41.1 us  [per_device(): small = lax.psum(small, ('row', 'col'))]
    unnamed x1 -> x0, blocking collectives: 30.5 us -> none
    reduce_sum x8 -> x0, other arithmetic: 27.1 us -> none  [the longest x1 12.7 us: per_device(): grad_up_bias = jnp.sum(grad_hidden.astype(jnp.float32), axis=0)]
    mul x5 -> x0, local copies, waits for them, and re-layouts: 19.2 us -> none  [the longest x2 13.6 us: per_device(): keep_float[:, :, None] * image_activ[:, None, :]]
  transfers between devices with their start and end apart: 6 -> 3, of which waited for: 4 -> 2; matrix products, arithmetic and copies ran while one was open for 21% -> 2% of each run, Pallas kernels for 0% -> 0%
where the time goes in v2:
time: 345 us; the launch traced here: 344 us
  blocking collectives  128 us (37%)
  Pallas kernels  94.1 us (27%)
  waiting for transfers between devices  82.5 us (24%)
  between operations  18.1 us (5%)
  local copies, waits for them, and re-layouts  9.2 us (3%)
  matrix products  5.37 us (2%)
  starting transfers between devices  3.58 us (1%)
    reduce_scatter x1, waiting for transfers between devices, per_device(): part = lax.psum_scatter(grads, 'col', scatter_dimension=1, tiled=True)  58 us
    pallas_call x1, Pallas kernels, backward_call(): pl.pallas_call(functools.partial(backward_kernel, images, ff), out_shape=...  55.2 us
    all_gather x1, blocking collectives, per_device(): lax.all_gather(texts, ('row', 'col'), axis=0, tiled=True)  43.8 us
    psum x1, blocking collectives, per_device(): small = lax.psum(small, ('row', 'col'))  41.1 us
    pallas_call x1, Pallas kernels, forward_call(): pl.pallas_call(functools.partial(forward_kernel, images, ff), out_shape=[...  38.9 us
    all_gather x1, blocking collectives, per_device(): gathered = lax.all_gather(sent, ('row', 'col'), axis=0, tiled=True)  38 us
    psum x1, waiting for transfers between devices, per_device(): part = lax.psum(part, 'row').astype(jnp.float32)  24.5 us
  transfers between devices with their start and end apart: 3, of which 2 were waited for; matrix products, arithmetic and copies ran while one was open for 2% of the time, Pallas kernels for 0%

profile of v2, /device:TPU:0, one launch (start us, length us, event | category | flops | bytes accessed | tf_op | source)
XLA Modules:
  0.0 344.0 jit_solution(7959181949994046322)
XLA Ops:
  7.2 0.0 copy-start
  7.2 0.0 reduce-scatter.2.cloned.1.call-start
  8.0 43.8 %all-gather.1 = bf16[32,4,512]{2,1,0:T(4,128)(2,1)S(1)} all-gather(bf16[1,4,512]{2,1,0:T(4,128)(2,1)} %bitcast.30), channel_id=1, replica_groups=mesh['row'=2,'col'=16] {'row','col'}, dimensions={0}, use_global_device_ids=true | all-gather | bytes 135168 | tf_op jit(solution)/shard_map/all_gather | solution.py:454
  51.8 38.9 %block_forward.1 = (bf16[832,768]{1,0:T(8,128)(2,1)}, bf16[9,880,256]{2,1,0:T(8,128)(2,1)}, bf16[12,832,256]{2,1,0:T(8,128)(2,1)}, bf16[3,832,256]{2,1,0:T(8,128...) custom-call(bf16[788,768]{1,0:T(8,128)(2,1)} %tok_ref.3, ...), custom_call_target="tpu_custom_call" | custom-call | tf_op jit(solution)/shard_map/block_forward/pallas_call | solution.py:203
  90.8 0.8 slice_bitcast_fusion.2
  91.5 38.0 %all-gather = f32[32,4,896]{2,1,0:T(4,128)S(1)} all-gather(f32[1,4,896]{2,1,0:T(4,128)S(1)} %slice_bitcast_fusion.2), channel_id=1, replica_groups=mesh['row'=2,'col'=16] {'row','col'}, dimensions={0}, use_global_device_ids=true | all-gather | bytes 473088 | tf_op jit(solution)/shard_map/all_gather | solution.py:453
  129.5 0.2 reshape.90
  129.7 0.0 copy-start.6
  129.7 0.1 copy.34
  129.8 0.0 copy-done
  129.8 0.6 multiply_reduce_fusion.1
  130.4 0.3 fusion.9
  130.8 0.6 select_reduce_fusion
  131.4 0.6 fusion.10
  132.0 0.1 convert_subtract_fusion
  132.1 0.4 multiply_reduce_fusion
  132.5 0.9 convolution_divide_fusion
  133.4 0.0 copy-start.2
  133.4 0.7 copy-done.2
  134.2 0.6 concatenate.6.dy_ref
  134.8 55.2 %block_backward.1 = (f32[788,768]{1,0:T(8,128)}, bf16[8,768,768]{2,1,0:T(8,128)(2,1)}, f32[8,768]{1,0:T(8,128)}, f32[1,3072]{1,0:T(1,128)}) custom-call(bf16[788,768]{1,0:T(8,128)(2,1)} %tok_ref.3, s32[4,197]{1,0:T(4,128)} %keep_ref.3, f32[8,768]{1,0:T(8,128)} %concatenate.6.dy_ref, f32[8,768]{1,0:T(8,128)} %vec_ref.3, bf16[768,2304]{1,0:T(8,128)(2,1)} %wqkv_h.3, ...), custom_call_target="tpu_custom_call" | custom-call | tf_op jit(solution)/shard_map/block_backward/pallas_call | solution.py:419
  190.0 0.0 reduce-scatter.2.cloned.1.call-update
  190.0 0.0 copy-start.5
  190.1 0.9 slice.42
  191.0 0.1 reshape.85
  191.1 0.7 copy.33
  191.7 3.5 %all-to-all-start = ((f32[16,4,192]{2,1,0:T(4,128)}), f32[16,4,192]{2,1,0:T(4,128)S(1)}, u32[]{:S(2)}, u32[]{:S(2)}) async-start(f32[16,4,192]{2,1,0:T(4,128)} %copy.33), calls=%async_computation.1 | async-start | bytes 131072 | tf_op jit(solution)/shard_map/all_to_all | solution.py:488
  195.3 0.0 all-reduce.3.cloned.1.call-start
  195.3 0.0 copy-start.3
  195.4 0.5 broadcast.47
  195.9 0.7 reduce.3
  196.6 41.1 %psum.15 = f32[12,768]{1,0:T(8,128)S(1)} all-reduce(f32[12,768]{1,0:T(8,128)S(1)} %pad_maximum_fusion), channel_id=1, replica_groups=mesh['row'=2,'col'=16] {'row','col'}, use_global_device_ids=true, to_apply=%region_11.0 | all-reduce | flops 9216 | bytes 73728 | tf_op jit(solution)/shard_map/psum | solution.py:505
  239.6 0.6 dynamic_slice.17
  240.3 1.0 fusion.2
  241.3 58.0 %reduce-scatter.2.cloned.1.call-done = bf16[8,48,768]{2,1,0:T(8,128)(2,1)} async-done(((bf16[8,768,768]{2,1,0:T(8,128)(2,1)}), bf16[8,48,768]{2,1,0:T(8,128)(2,1)}) %reduce-scatter.2.cloned.1.call-update) | async-done | bytes 589840 | tf_op jit(solution)/shard_map/reduce_scatter | solution.py:497
  299.3 0.0 all-reduce.3.cloned.1.call-update
  299.3 0.8 convolution_multiply_fusion.2
  300.2 0.7 constant_dynamic-slice_fusion
  300.8 0.0 all-to-all-done
  300.9 4.9 %all_gather.11 = f32[128,192]{1,0:T(8,128)S(1)} all-gather(f32[64,192]{1,0:T(8,128)S(1)} %reshape.86), channel_id=1, replica_groups=mesh['row'=2,'col'=16] {'row'}, dimensions={0}, use_global_device_ids=true | all-gather | bytes 147456 | tf_op jit(solution)/shard_map/all_gather | solution.py:490
  305.8 1.3 fusion
  307.1 24.5 %all-reduce.3.cloned.1.call-done = bf16[8,48,768]{2,1,0:T(8,128)(2,1)} async-done(((bf16[8,48,768]{2,1,0:T(8,128)(2,1)}), bf16[8,48,768]{2,1,0:T(8,128)(2,1)}) %all-reduce.3.cloned.1.call-update) | async-done | bytes 589840 | tf_op jit(solution)/shard_map/psum | solution.py:498
  331.5 1.2 convert_element_type.20
  332.8 0.7 slice_bitcast_fusion.1
  333.5 0.2 reshape.82
  333.8 0.3 copy.30
  334.1 1.1 reshape.83
  335.2 0.9 copy.35
  (23 shorter events, 0.2 us)
Async XLA Ops:
  7.2 122.6 %copy-start = (bf16[768,512]{1,0:T(8,128)(2,1)S(1)}, bf16[768,512]{1,0:T(8,128)(2,1)}, u32[]{:S(2)}) copy-start(bf16[768,512]{1,0:T(8,128)(2,1)} %param.20) | copy-start | bytes 2359300
  7.2 292.1 %reduce-scatter.2.cloned.1.call-start = ((), (), s32[]{:S(2)}) async-start(), calls=%async_computation.2 | async-start | bytes 10027008 | tf_op jit(solution)/shard_map/reduce_scatter | solution.py:497
  129.7 1.1 copy-start.6
  133.4 0.7 copy-start.2
  190.0 5.8 %copy-start.5 = (f32[1,3072]{1,0:T(1,128)S(1)}, f32[1,3072]{1,0:T(1,128)}, u32[]{:S(2)}) copy-start(f32[1,3072]{1,0:T(1,128)} %get-tuple-element.37) | copy-start | bytes 36868
  190.1 6.5 %copy-start.4 = (f32[8,768]{1,0:T(8,128)S(1)}, f32[8,768]{1,0:T(8,128)}, u32[]{:S(2)}) copy-start(f32[8,768]{1,0:T(8,128)} %get-tuple-element.36) | copy-start | bytes 73732
  191.7 109.1 %all-to-all-start = ((f32[16,4,192]{2,1,0:T(4,128)}), f32[16,4,192]{2,1,0:T(4,128)S(1)}, u32[]{:S(2)}, u32[]{:S(2)}) async-start(f32[16,4,192]{2,1,0:T(4,128)} %copy.33), calls=%async_computation.1 | async-start | bytes 131072 | tf_op jit(solution)/shard_map/all_to_all | solution.py:488
  195.3 136.3 %all-reduce.3.cloned.1.call-start = ((), (), s32[]{:S(2)}) async-start(), calls=%async_computation.3 | async-start | bytes 1179648 | tf_op jit(solution)/shard_map/psum | solution.py:498
  195.3 110.5 %copy-start.3 = (f32[128,768]{1,0:T(8,128)S(1)}, f32[128,768]{1,0:T(8,128)}, u32[]{:S(2)}) copy-start(f32[128,768]{1,0:T(8,128)} %copy-done.2) | copy-start | bytes 1179652
  331.5 2.0 copy-start.1
Sparse Core Ops, SparseCore 0:
  190.2 109.0 reduce-scatter.1
  301.7 29.7 all-reduce.2

commit v3 on v2

--- a/solution.py
+++ b/solution.py
@@ -7,12 +7,11 @@
 from jax.experimental.pallas import tpu as pltpu
 from jax.sharding import PartitionSpec as P
 
-HIGH = lax.Precision.HIGHEST
-
 D = 768
 HEADS = 12
 HEAD_DIM = 64
 SEQ = 197
+EMB = 512
 ROWS = 208
 WIN = 256
 TILE = 256
@@ -162,7 +161,8 @@
         ap = jnp.zeros((kmask.shape[1], TILE), F32)
         for i in range(images):
             ap = ap + mm(kmask[i], a_s[i * ROWS:i * ROWS + WIN, :])
-        apool_ref[t] = ap
+        at = pl.multiple_of((t % n_quads) * TILE, TILE)
+        apool_ref[t // n_quads, :, pl.ds(at, TILE)] = ap[0:8]
         hi = ap.astype(BF)
         lo = (ap - hi.astype(F32)).astype(BF)
         w = wdown[pl.ds(col, TILE), :]
@@ -188,7 +188,7 @@
     outs = [
         ((span, D), BF), ((3 * nq, wide, TILE), BF), ((images * nq, 4 * ROWS, TILE), BF),
         ((nq, span, TILE), BF), ((span, D), BF), ((span, D), BF), ((span, 128), F32),
-        ((ff // TILE, span, TILE), BF), ((ff // TILE, 16, TILE), F32), ((8, D + 128), F32),
+        ((ff // TILE, span, TILE), BF), ((ff // D, 8, D), F32), ((8, D + 128), F32),
     ]
     anyspec = pl.BlockSpec(memory_space=pl.ANY)
     vm = pl.BlockSpec(memory_space=pltpu.VMEM)
@@ -213,11 +213,11 @@
 
 def backward_kernel(
     images, ff,
-    tok_ref, keep_ref, dy_ref, vec_ref,
-    wqkv_h, wout_h, wup_h, wdown_h, h1_h, qkv_h, p_h, o_h, h2_h, xh2_h, rstd_h, gk_h,
+    tok_ref, keep_ref, dy_ref, da_s, vec_ref,
+    wqkv_h, wout_h, wup_h, h1_h, qkv_h, p_h, o_h, h2_h, xh2_h, rstd_h, gk_h,
     tg_ref, g_ref, vg_ref, ub_ref,
-    wqkv, wout, wup, wdown, h1, qkv, p_s, o_s, h2, xh2, rstd, du,
-    xs, dx, db, do_s, dp_s, h1t, h2t, keep8, kcol, da_s,
+    wqkv, wout, wup, h1, qkv, p_s, o_s, h2, xh2, rstd, du,
+    xs, dx, db, do_s, dp_s, h1t, h2t, keep8, kcol,
     in_sem, gk_sem, p_sem,
 ):
     n_quads = D // TILE
@@ -226,12 +226,12 @@
     masks = head_masks()
     loads = {}
     for k, (name, src, dst) in enumerate((
-        ("wdown", wdown_h, wdown), ("h2", h2_h, h2), ("wup", wup_h, wup), ("xh2", xh2_h, xh2),
+        ("h2", h2_h, h2), ("wup", wup_h, wup), ("xh2", xh2_h, xh2),
         ("rstd", rstd_h, rstd), ("wout", wout_h, wout), ("o", o_h, o_s), ("qkv", qkv_h, qkv),
         ("h1", h1_h, h1), ("wqkv", wqkv_h, wqkv),
     )):
         loads[name] = pltpu.make_async_copy(src, dst, in_sem.at[k])
-    for name in ("wdown", "h2"):
+    for name in ("h2",):
         loads[name].start()
     gks = []
     for t in range(n_ff):
@@ -265,15 +265,6 @@
     dyb = dy.astype(BF)
     cnt = jnp.sum(kb, axis=1, keepdims=True)[0:8]
     vg_ref[7:8, :] = jnp.sum(dyb.astype(F32) * cnt, axis=0, keepdims=True)
-    dy16 = jnp.concatenate([dyb, jnp.zeros((8, D), BF)], axis=0)
-    loads["wdown"].wait()
-
-    def spread(t, _):
-        col = pl.multiple_of(t * TILE, TILE)
-        da_s[:, pl.ds(col, TILE)] = mm(dy16, wdown[pl.ds(col, TILE), :], NT)
-        return 0
-
-    lax.fori_loop(0, n_ff, spread, 0)
     loads["h2"].wait()
     h2t[...] = h2[...].T
     for c in gks:
@@ -398,7 +389,7 @@
     vg_ref[1:2, :] = b1
 
 
-def backward_call(images, ff, tokens, keep, dy, vec, wqkv, wout, wup, wdown, acts):
+def backward_call(images, ff, tokens, keep, dy, da, vec, wqkv, wout, wup, acts):
     span = images * ROWS
     nq = D // TILE
     wide = span + WIN - ROWS
@@ -406,25 +397,220 @@
     vm = pl.BlockSpec(memory_space=pltpu.VMEM)
     outs = [((images * SEQ, D), F32), ((ff // D + 4, D, D), BF), ((8, D), F32), ((1, ff), F32)]
     scratch = [
-        pltpu.VMEM((D, 3 * D), BF), pltpu.VMEM((D, D), BF), pltpu.VMEM((D, ff), BF), pltpu.VMEM((ff, D), BF),
+        pltpu.VMEM((D, 3 * D), BF), pltpu.VMEM((D, D), BF), pltpu.VMEM((D, ff), BF),
         pltpu.VMEM((span, D), BF), pltpu.VMEM((3 * nq, wide, TILE), BF), pltpu.VMEM((2, 4 * ROWS, TILE), BF),
         pltpu.VMEM((nq, span, TILE), BF), pltpu.VMEM((span, D), BF), pltpu.VMEM((span, D), BF),
         pltpu.VMEM((span, 128), F32), pltpu.VMEM((span, ff), BF),
         pltpu.VMEM(((images - 1) * SEQ + ROWS + 7 & -8, D), F32), pltpu.VMEM((span, D), F32),
         pltpu.VMEM((span, D), BF), pltpu.VMEM((nq, span, TILE), BF), pltpu.VMEM((span, 3 * D), BF),
         pltpu.VMEM((D, span), BF), pltpu.VMEM((D, span), BF), pltpu.VMEM((16, WIN), F32),
-        pltpu.VMEM((span, 128), F32), pltpu.VMEM((16, ff), F32),
+        pltpu.VMEM((span, 128), F32),
         pltpu.SemaphoreType.DMA((10,)), pltpu.SemaphoreType.DMA((ff // TILE,)), pltpu.SemaphoreType.DMA((2,)),
     ]
     return pl.pallas_call(
         functools.partial(backward_kernel, images, ff),
         out_shape=[jax.ShapeDtypeStruct(s, d) for s, d in outs],
-        in_specs=[vm] * 4 + [anyspec] * 12,
+        in_specs=[vm] * 5 + [anyspec] * 11,
         out_specs=[vm] * 4,
         scratch_shapes=scratch,
         compiler_params=pltpu.CompilerParams(vmem_limit_bytes=62 * 2**20),
         name="block_backward",
-    )(tokens, keep, dy, vec, wqkv, wout, wup, wdown, *acts)
+    )(tokens, keep, dy, da, vec, wqkv, wout, wup, *acts)
+
+
+def split3(x):
+    hi = x.astype(BF)
+    r = x - hi.astype(F32)
+    mid = r.astype(BF)
+    lo = (r - mid.astype(F32)).astype(BF)
+    return hi, mid, lo
+
+
+NN = (((1,), (0,)), ((), ()))
+MESH = pl.DeviceIdType.MESH
+
+
+def mm3(x, w, dims=NN):
+    hi, mid, lo = split3(x)
+    return (mm(lo, w, dims) + mm(mid, w, dims)) + mm(hi, w, dims)
+
+
+def place(cz, cy):
+    row = lax.axis_index("row")
+    col = lax.axis_index("col")
+    return row, col // (2 * cy), lax.rem(col // 2, cy), lax.rem(col, 2)
+
+
+def head_kernel(
+    n_row, cz, cy, images, ff,
+    pooled_ref, texts_ref, apool_ref, pair_ref, scale_ref, wproj_ref, wdown_h,
+    loss_ref, dy_ref, da_ref, text_ref, proj_ref, down_ref,
+    pg, ax, ag, wdown, p_all, t_all, c_all, a_all, gproj, gdown,
+    in_sem, zs, zr, ps, pr, cs, cr,
+):
+    x, z, y, core = place(cz, cy)
+    load = pltpu.make_async_copy(wdown_h, wdown, in_sem.at[0])
+    load.start()
+    half = D // 2
+    plane = n_row * cy
+    spot = x * cy + y
+
+    def device(xx, zz, yy, cc):
+        return (xx, (zz * cy + yy) * 2 + cc)
+
+    z_peers = [lax.rem(z + k, cz) for k in range(1, cz)]
+    p_peers = [lax.rem(spot + k, plane) for k in range(1, plane)]
+    bar = pltpu.get_barrier_semaphore()
+    for zz in z_peers:
+        pl.semaphore_signal(bar, inc=1, device_id=device(x, zz, y, core), device_id_type=MESH)
+    for pp in p_peers:
+        pl.semaphore_signal(bar, inc=1, device_id=device(pp // cy, z, lax.rem(pp, cy), core), device_id_type=MESH)
+    pl.semaphore_signal(bar, inc=1, device_id=device(x, z, y, 1 - core), device_id_type=MESH)
+    mine = jnp.concatenate([
+        pooled_ref[0:images, 0:D],
+        jnp.concatenate([texts_ref[...].astype(F32), pooled_ref[0:images, D:], jnp.zeros((images, D - EMB - 128), F32)], axis=1),
+    ], axis=0)
+    pg[x, z, y, core] = mine
+    for g in range(cz):
+        ax[g, 0:images] = apool_ref[g, 0:images, 0:half]
+        ax[g, images:] = apool_ref[g, 0:images, half:]
+    ag[x, z, y, core] = ax[z]
+    pl.semaphore_wait(bar, cz - 1 + plane - 1 + 1)
+
+    def stage(src, dst, sems, slot, devs):
+        out = []
+        for k, (s, dev) in enumerate(zip(src, devs)):
+            c = pltpu.make_async_remote_copy(
+                s, dst, sems[0].at[slot, k], sems[1].at[slot, k], device_id=dev, device_id_type=MESH)
+            c.start()
+            out.append(c)
+        return out
+
+    z_devs = [device(x, zz, y, core) for zz in z_peers]
+    p_devs = [device(pp // cy, z, lax.rem(pp, cy), core) for pp in p_peers]
+    c_devs = [device(x, z, y, 1 - core)]
+    own = pg.at[x, z, y, core]
+    first = stage([own] * len(z_devs), own, (zs, zr), 0, z_devs)
+    first_a = stage([ax.at[zz] for zz in z_peers], ag.at[x, z, y, core], (zs, zr), 1, z_devs)
+    for c in first:
+        c.wait()
+    own = pg.at[x, :, y, core]
+    second = stage([own] * len(p_devs), own, (ps, pr), 0, p_devs)
+    for c in first_a:
+        c.wait()
+    own = ag.at[x, :, y, core]
+    second_a = stage([own] * len(p_devs), own, (ps, pr), 1, p_devs)
+    for c in second:
+        c.wait()
+    own = pg.at[:, :, :, core]
+    third = stage([own], own, (cs, cr), 0, c_devs)
+    for c in second_a:
+        c.wait()
+    own = ag.at[:, :, :, core]
+    third_a = stage([own], own, (cs, cr), 1, c_devs)
+    for c in third:
+        c.wait()
+    n_col = cz * cy * 2
+    n_img = n_row * n_col * images
+    for d in range(n_row * n_col):
+        rows = slice(d * images, (d + 1) * images)
+        at = (d // n_col, d % n_col // (2 * cy), d // 2 % cy, d % 2)
+        p_all[rows, :] = pg[at + (slice(0, images), slice(0, D))]
+        t_all[rows, :] = pg[at + (slice(images, 2 * images), slice(0, EMB))]
+        c_all[rows, :] = pg[at + (slice(images, 2 * images), slice(EMB, EMB + 128))]
+    scale = scale_ref[0]
+    pooled = p_all[...]
+    latent = mm3(pooled, wproj_ref[...])
+    norm = lax.rsqrt(jnp.sum(latent * latent, axis=1, keepdims=True) + 1e-6)
+    embeds = latent * norm
+    eb = embeds.astype(BF)
+    tb = t_all[...].astype(BF)
+    logits = scale * mm(eb, tb, NT)
+    row_max = jnp.max(logits, axis=1, keepdims=True)
+    row_exp = jnp.exp(logits - row_max)
+    row_sum = jnp.sum(row_exp, axis=1, keepdims=True)
+    col_max = jnp.max(logits, axis=0, keepdims=True)
+    col_exp = jnp.exp(logits - col_max)
+    col_sum = jnp.sum(col_exp, axis=0, keepdims=True)
+    ids = lax.broadcasted_iota(jnp.int32, (n_img, n_img), 0)
+    match = (ids == pair_ref[...]).astype(F32).T
+    grad = 0.5 * (row_exp / row_sum) + 0.5 * (col_exp / col_sum) - match
+    lse = jnp.sum(row_max + jnp.log(row_sum), axis=0, keepdims=True) + jnp.sum(
+        col_max + jnp.log(col_sum), axis=1, keepdims=True)
+    hits = jnp.sum(jnp.sum(logits * match, axis=1, keepdims=True), axis=0, keepdims=True)
+    loss_ref[...] = (0.5 * lse - hits) * (1.0 / n_img)
+    de = scale * mm3(grad, tb)
+    dz = norm * (de - embeds * jnp.sum(embeds * de, axis=1, keepdims=True))
+    image_grad = mm3(dz, wproj_ref[...], NT) / c_all[:, 0:1]
+    dev = x * n_col + (z * cy + y) * 2 + core
+    want = lax.broadcasted_iota(jnp.int32, (16, n_img), 0) + dev * images
+    have = lax.broadcasted_iota(jnp.int32, (16, n_img), 1)
+    pick = (want == have).astype(F32).astype(BF)
+    hi, mid, lo = split3(image_grad)
+    dy = (mm(pick, lo) + mm(pick, mid)) + mm(pick, hi)
+    dy_ref[...] = dy[0:8]
+    dyb = dy.astype(BF)
+    load.wait()
+
+    def spread(t, _):
+        col = pl.multiple_of(t * TILE, TILE)
+        da_ref[:, pl.ds(col, TILE)] = mm(dyb, wdown[pl.ds(col, TILE), :], NT)[0:8]
+        return 0
+
+    lax.fori_loop(0, ff // TILE, spread, 0)
+    g_hi, g_mid, g_lo = split3(grad)
+    own_grad = (mm(pick, g_lo, NT) + mm(pick, g_mid, NT)) + mm(pick, g_hi, NT)
+    text_ref[...] = (scale * mm3(own_grad, eb))[0:images]
+    p_hi, p_lo, _ = split3(pooled)
+    d_hi, d_lo, _ = split3(dz)
+    gproj[...] = (mm(p_lo, d_hi, TN) + mm(p_hi, d_lo, TN)) + mm(p_hi, d_hi, TN)
+    n_proj = D // n_col
+    at = pl.multiple_of(((z * cy + y) * 2 + core) * n_proj, 8)
+    proj_ref[...] = gproj[pl.ds(at, n_proj), :]
+    for c in third_a:
+        c.wait()
+    for d in range(n_row * n_col):
+        rows = slice(d * images, (d + 1) * images)
+        at = (d // n_col, d % n_col // (2 * cy), d // 2 % cy, d % 2)
+        a_all[rows, 0:half] = ag[at + (slice(0, images),)]
+        a_all[rows, half:] = ag[at + (slice(images, 2 * images),)]
+    acts = a_all[...]
+    a_hi = acts.astype(BF)
+    a_lo = (acts - a_hi.astype(F32)).astype(BF)
+    for n in range(D // TILE):
+        sl = slice(n * TILE, (n + 1) * TILE)
+        gdown[:, sl] = mm(a_lo, hi[:, sl], TN) + mm(a_hi, hi[:, sl], TN)
+    n_down = ff // n_col
+    at = pl.multiple_of((y * 2 + core) * n_down, 8)
+    down_ref[...] = gdown[pl.ds(at, n_down), :]
+
+
+def head_call(n_row, n_col, images, ff, pooled, texts, apool, pair, scale, wproj, wdown):
+    cz = ff // D
+    cy = n_col // (2 * cz)
+    n_img = n_row * n_col * images
+    vm = pl.BlockSpec(memory_space=pltpu.VMEM)
+    outs = [(1, 1), (8, D), (8, ff), (images, EMB), (D // n_col, EMB), (ff // n_col, D)]
+    plane = n_row * cy
+    grid = (n_row, cz, cy, 2, 2 * images)
+    scratch = [
+        pltpu.VMEM(grid + (D,), F32), pltpu.VMEM((cz, 2 * images, D // 2), F32), pltpu.VMEM(grid + (D // 2,), F32),
+        pltpu.VMEM((ff, D), BF), pltpu.VMEM((n_img, D), F32), pltpu.VMEM((n_img, EMB), F32),
+        pltpu.VMEM((n_img, 128), F32), pltpu.VMEM((n_img, D), F32), pltpu.VMEM((D, EMB), F32), pltpu.VMEM((D, D), F32),
+        pltpu.SemaphoreType.DMA((1,)), pltpu.SemaphoreType.DMA((2, cz)), pltpu.SemaphoreType.DMA((2, cz)),
+        pltpu.SemaphoreType.DMA((2, plane)), pltpu.SemaphoreType.DMA((2, plane)),
+        pltpu.SemaphoreType.DMA((2, 1)), pltpu.SemaphoreType.DMA((2, 1)),
+    ]
+    return pl.pallas_call(
+        functools.partial(head_kernel, n_row, cz, cy, images, ff),
+        out_shape=[jax.ShapeDtypeStruct(s, F32) for s in outs],
+        in_specs=[vm] * 4 + [pl.BlockSpec(memory_space=pltpu.SMEM), vm, pl.BlockSpec(memory_space=pl.ANY)],
+        out_specs=[vm] * len(outs),
+        scratch_shapes=scratch,
+        compiler_params=pltpu.CompilerParams(
+            vmem_limit_bytes=60 * 2**20, collective_id=0, has_side_effects=True),
+        name="contrastive_head",
+    )(pooled, texts, apool, pair, scale, wproj, wdown)
 
 
 def per_device(
@@ -442,57 +628,17 @@
     logit_scale,
 ):
     images = keep_mask.shape[0]
-    rows = tokens.shape[0]
-    total_images = pair_index.shape[0]
     ff = w_up.shape[1]
+    n_row, shards = lax.axis_size("row"), lax.axis_size("col")
+    mine = lax.axis_index("col")
     acts = forward_call(
         images, ff, tokens, keep_mask, w_qkv, w_out, w_up, w_down, vectors, up_bias.reshape(1, ff)
     )
-    activ_sum = acts[8].transpose(1, 0, 2).reshape(16, ff)[:images]
-    sent = acts[9][:images]
-    gathered = lax.all_gather(sent, ("row", "col"), axis=0, tiled=True)
-    all_texts = lax.all_gather(texts, ("row", "col"), axis=0, tiled=True).astype(jnp.float32)
-    pooled_all, counts_all = gathered[:, :D], gathered[:, D : D + 1]
-    proj_float = w_proj.astype(jnp.float32)
-    latent = jnp.dot(pooled_all, proj_float, precision=HIGH)
-    inv_norm = lax.rsqrt(jnp.sum(latent * latent, axis=-1, keepdims=True) + 1e-06)
-    embeds = latent * inv_norm
-    embeds_f = embeds.astype(jnp.bfloat16).astype(jnp.float32)
-    logit_mult = logit_scale[0]
-    first_image = lax.axis_index(("row", "col")) * images
-    all_ids = jnp.arange(total_images, dtype=jnp.int32)
-    match = (pair_index[:, None] == all_ids[None, :]).astype(jnp.float32)
-    logits = logit_mult * jnp.dot(
-        embeds_f.astype(jnp.bfloat16), all_texts.astype(jnp.bfloat16).T,
-        preferred_element_type=jnp.float32,
+    loss, dy, da, text_grad, grad_proj, grad_down = head_call(
+        n_row, shards, images, ff, acts[9], texts, acts[8], pair_index.reshape(1, -1), logit_scale, w_proj, w_down
     )
-    row_lse = jax.nn.logsumexp(logits, axis=1)
-    col_lse = jax.nn.logsumexp(logits, axis=0)
-    summed = 0.5 * (jnp.sum(row_lse) + jnp.sum(col_lse)) - jnp.sum(logits * match)
-    grad_logits = (
-        0.5 * jnp.exp(logits - row_lse[:, None]) + 0.5 * jnp.exp(logits - col_lse[None, :]) - match
-    )
-    embed_grad = logit_mult * jnp.dot(grad_logits, all_texts, precision=HIGH)
-    own_cols = lax.dynamic_slice_in_dim(grad_logits, first_image, images, axis=1)
-    text_grad = logit_mult * jnp.dot(own_cols.T, embeds_f, precision=HIGH)
-    grad_latent = inv_norm * (
-        embed_grad - embeds * jnp.sum(embeds * embed_grad, axis=-1, keepdims=True)
-    )
-    shards = lax.axis_size("col")
-    mine = lax.axis_index("col")
-    own_pooled = lax.dynamic_slice_in_dim(pooled_all, mine * (D // shards), D // shards, axis=1)
-    grad_proj = jnp.dot(own_pooled.T, grad_latent, precision=HIGH)
-    grad_pooled = jnp.dot(grad_latent, proj_float.T, precision=HIGH)
-    image_grads = (grad_pooled / counts_all).astype(jnp.bfloat16)
-    pieces = activ_sum.reshape(images, shards, ff // shards).transpose(1, 0, 2)
-    pieces = lax.all_to_all(pieces, "col", split_axis=0, concat_axis=0, tiled=True)
-    pieces = pieces.reshape(images * shards, ff // shards)
-    pieces = lax.all_gather(pieces, "row", axis=0, tiled=True)
-    grad_down = jnp.dot(pieces.T, image_grads.astype(jnp.float32), precision=HIGH)
-    own_grads = lax.dynamic_slice_in_dim(grad_pooled / counts_all, first_image, images)
-    dy = jnp.concatenate([own_grads, jnp.zeros((8 - images, D), jnp.float32)], axis=0)
     token_grad, grads, grad_vectors, grad_up_bias = backward_call(
-        images, ff, tokens, keep_mask, dy, vectors, w_qkv, w_out, w_up, w_down, acts[:8]
+        images, ff, tokens, keep_mask, dy, da, vectors, w_qkv, w_out, w_up, acts[:8]
     )
     part = lax.psum_scatter(grads, "col", scatter_dimension=1, tiled=True)
     part = lax.psum(part, "row").astype(jnp.float32)
@@ -505,9 +651,8 @@
     small = lax.psum(small, ("row", "col"))
     vec_share = lax.dynamic_slice_in_dim(small[:8], mine * (D // shards), D // shards, axis=1)
     bias_share = lax.dynamic_slice_in_dim(small[8:].reshape(ff), mine * (ff // shards), ff // shards)
-    loss = (summed / total_images).reshape(1)
     return (
-        loss,
+        loss.reshape(1),
         token_grad,
         qkv_share,
         out_share,

time: 345 us -> 297 us (0.86)
  blocking collectives: 128 us -> 40.7 us
  waiting for transfers between devices: 82.5 us -> 111 us
  Pallas kernels: 94.1 us -> 119 us
  matrix products: 5.37 us -> 0 us
  starting transfers between devices: 3.58 us -> 0.08 us
    all_gather x3 -> x0, blocking collectives: 86.8 us -> none  [the longest x1 43.8 us: per_device(): lax.all_gather(texts, ('row', 'col'), axis=0, tiled=True)]
    reduce_scatter x1, waiting for transfers between devices: 58 us -> 111 us  [per_device(): part = lax.psum_scatter(grads, 'col', scatter_dimension=1, tiled=True)]
    pallas_call x0 -> x1, Pallas kernels: none -> 26.4 us  [head_call(): pl.pallas_call(functools.partial(head_kernel, n_row, cz, cy, images, ff),...]
    psum x1, waiting for transfers between devices: 24.5 us -> 0.01 us  [per_device(): part = lax.psum(part, 'row').astype(jnp.float32)]
    dot_general x7 -> x0, matrix products: 5.37 us -> none  [the longest x1 1.26 us: per_device(): jnp.dot(pieces.T, image_grads.astype(jnp.float32), precision=HIGH)]
    all_to_all x1 -> x0, starting transfers between devices: 3.5 us -> none  [per_device(): lax.all_to_all(pieces, 'col', split_axis=0, concat_axis=0, tiled=True)]
  transfers between devices with their start and end apart: 3 -> 2, of which waited for: 2 -> 1; matrix products, arithmetic and copies ran while one was open for 2% -> 1% of each run, Pallas kernels for 0% -> 0%
where the time goes in v3:
time: 297 us
  Pallas kernels  119 us (40%)
  waiting for transfers between devices  111 us (37%)
  blocking collectives  40.7 us (14%)
  between operations  16.6 us (6%)
  local copies, waits for them, and re-layouts  7.14 us (2%)
    reduce_scatter x1, waiting for transfers between devices, per_device(): part = lax.psum_scatter(grads, 'col', scatter_dimension=1, tiled=True)  111 us
    pallas_call x1, Pallas kernels, backward_call(): pl.pallas_call(functools.partial(backward_kernel, images, ff), out_shape=...  53.9 us
    psum x1, blocking collectives, per_device(): small = lax.psum(small, ('row', 'col'))  40.7 us
    pallas_call x1, Pallas kernels, forward_call(): pl.pallas_call(functools.partial(forward_kernel, images, ff), out_shape=[...  38.9 us
    pallas_call x1, Pallas kernels, head_call(): pl.pallas_call(functools.partial(head_kernel, n_row, cz, cy, images, ff),...  26.4 us
  transfers between devices with their start and end apart: 2, of which 1 were waited for; matrix products, arithmetic and copies ran while one was open for 1% of the time, Pallas kernels for 0%

profile of v3, /device:TPU:0, one launch (start us, length us, event | category | flops | bytes accessed | tf_op | source)
XLA Modules:
  0.0 296.8 jit_solution(2766520975140776414)
XLA Ops:
  7.2 0.0 reduce-scatter.2.cloned.1.call-start
  7.9 38.9 %block_forward.1 = (bf16[832,768]{1,0:T(8,128)(2,1)}, bf16[9,880,256]{2,1,0:T(8,128)(2,1)}, bf16[12,832,256]{2,1,0:T(8,128)(2,1)}, bf16[3,832,256]{2,1,0:T(8,128...) custom-call(bf16[788,768]{1,0:T(8,128)(2,1)} %tok_ref.3, ...), custom_call_target="tpu_custom_call" | custom-call | tf_op jit(solution)/shard_map/block_forward/pallas_call | solution.py:203
  46.8 26.4 %contrastive_head.1 = (f32[1,1]{1,0:T(1,128)}, f32[8,768]{1,0:T(8,128)}, f32[8,3072]{1,0:T(8,128)}, f32[4,512]{1,0:T(4,128)}, f32[48,512]{1,0:T(8,128)}, /*index=5*/f32[192,768]{1,0:T(8,128)}) custom-call(f32[8,896]{1,0:T(8,128)} %get-tuple-element.30.pooled_ref, bf16[4,512]{1,0:T(4,128)(2,1)} %texts_ref.1, f32[4,8,768]{2,1,0:T(8,128)} %get-tuple-element.31.apool_ref, ...), custom_call_target="tpu_custom_call" | custom-call | tf_op jit(solution)/shard_map/contrastive_head/pallas_call | solution.py:604
  73.2 53.9 %block_backward.1 = (f32[788,768]{1,0:T(8,128)}, bf16[8,768,768]{2,1,0:T(8,128)(2,1)}, f32[8,768]{1,0:T(8,128)}, f32[1,3072]{1,0:T(1,128)}) custom-call(bf16[788,768]{1,0:T(8,128)(2,1)} %tok_ref.3, s32[4,197]{1,0:T(4,128)} %keep_ref.3, f32[8,768]{1,0:T(8,128)} %get-tuple-element.33.dy_ref, f32[8,3072]{1,0:T(8,128)} %get-tuple-element.34.da_s, ...), custom_call_target="tpu_custom_call" | custom-call | tf_op jit(solution)/shard_map/block_backward/pallas_call | solution.py:410
  127.1 0.0 copy-start.4
  127.1 0.0 copy-start.3
  127.2 0.0 reduce-scatter.2.cloned.1.call-update
  127.2 0.0 all-reduce.2.cloned.1.call-start
  127.2 111.2 %reduce-scatter.2.cloned.1.call-done = bf16[8,48,768]{2,1,0:T(8,128)(2,1)} async-done(((bf16[8,768,768]{2,1,0:T(8,128)(2,1)}), bf16[8,48,768]{2,1,0:T(8,128)(2,1)}) %reduce-scatter.2.cloned.1.call-update) | async-done | bytes 589840 | tf_op jit(solution)/shard_map/reduce_scatter | solution.py:643
  238.4 0.0 all-reduce.2.cloned.1.call-update
  238.4 0.5 broadcast.3
  238.9 0.0 copy-done.4
  238.9 0.7 reduce.3
  239.6 0.0 copy-done.3
  239.7 40.7 %psum.15 = f32[12,768]{1,0:T(8,128)S(1)} all-reduce(f32[12,768]{1,0:T(8,128)S(1)} %pad_maximum_fusion), channel_id=1, replica_groups=mesh['row'=2,'col'=16] {'row','col'}, use_global_device_ids=true, to_apply=%region_2.0 | all-reduce | flops 9216 | bytes 73728 | tf_op jit(solution)/shard_map/psum | solution.py:651
  280.4 0.6 dynamic_slice.7
  281.1 0.7 constant_dynamic-slice_fusion
  281.7 0.0 all-reduce.2.cloned.1.call-done
  281.7 1.2 convert_element_type.3
  282.9 0.0 copy-start
  282.9 0.7 slice_bitcast_fusion.1
  283.6 0.9 copy.25
  284.5 0.0 copy-done
  284.5 0.2 reshape.47
  284.8 0.0 copy-start.1
  284.8 0.3 copy.23
  285.1 0.0 copy-start.2
  285.1 0.0 copy-start.5
  285.1 1.1 reshape.48
  286.8 0.0 copy-done.1
  286.8 0.8 copy.33
  287.6 0.0 copy-done.2
  287.6 0.6 copy.34
  288.3 0.0 copy-done.5
  288.3 0.6 copy.35
  (7 shorter events, 0.1 us)
Async XLA Ops:
  7.2 231.2 %reduce-scatter.2.cloned.1.call-start = ((), (), s32[]{:S(2)}) async-start(), calls=%async_computation.1 | async-start | bytes 10027008 | tf_op jit(solution)/shard_map/reduce_scatter | solution.py:643
  127.1 111.8 %copy-start.4 = (f32[1,3072]{1,0:T(1,128)S(1)}, f32[1,3072]{1,0:T(1,128)}, u32[]{:S(2)}) copy-start(f32[1,3072]{1,0:T(1,128)} %get-tuple-element.47) | copy-start | bytes 36868
  127.1 112.5 %copy-start.3 = (f32[8,768]{1,0:T(8,128)S(1)}, f32[8,768]{1,0:T(8,128)}, u32[]{:S(2)}) copy-start(f32[8,768]{1,0:T(8,128)} %get-tuple-element.46) | copy-start | bytes 73732
  127.2 154.5 %all-reduce.2.cloned.1.call-start = ((), (), s32[]{:S(2)}) async-start(), calls=%async_computation.2 | async-start | bytes 1179648 | tf_op jit(solution)/shard_map/psum | solution.py:644
  282.9 1.6 copy-start
  284.8 2.0 copy-start.1
  285.1 2.5 copy-start.2
  285.1 3.2 %copy-start.5 = (f32[4,512]{1,0:T(4,128)S(1)}, f32[4,512]{1,0:T(4,128)}, u32[]{:S(2)}) copy-start(f32[4,512]{1,0:T(4,128)} %get-tuple-element.69) | copy-start | bytes 24580
Sparse Core Ops, SparseCore 0:
  127.3 111.0 reduce-scatter.1
  240.8 30.1 all-reduce.1

commit v4 on v3

--- a/solution.py
+++ b/solution.py
@@ -45,8 +45,9 @@
 def forward_kernel(
     images, ff,
     tok_ref, keep_ref, wqkv_h, wout_h, wup_h, wdown_h, vec_ref, upb_ref,
-    h1_h, qkv_h, p_h, o_h, h2_h, xh2_h, rstd_h, gk_h, apool_ref, pooled_ref,
-    wqkv, wout, wup, wdown, xs, h1, qkv, p_s, o_s, h2, xh2, rstd, gk, a_s, keep8, kmask, kcol, bias, acc,
+    h1t_h, qkv_h, p_h, ot_h, h2t_h, xh1_h, xh2_h, rstd1_h, rstd2_h, kcol_h, gk_h, apool_ref, pooled_ref,
+    wqkv, wout, wup, wdown, xs, h1t, qkv, p_s, ot, h2t, xh1, xh2, rstd1, rstd2, kcol, gk,
+    h1, o_s, h2, a_s, keep8, kmask, bias, acc,
     in_sem, out_sem,
 ):
     n_quads = D // TILE
@@ -77,6 +78,7 @@
         kmask[i] = jnp.where(rid == i, kb, 0.0).astype(BF)
         one = jnp.ones((kb.shape[0], 128), F32).astype(BF)
         kcol[i * ROWS:(i + 1) * ROWS, :] = mm(kmask[i], one, TN)[0:ROWS]
+    send(0, kcol, kcol_h)
     bias[0:1, 0:D] = vec_ref[2:3, :]
     bias[0:1, D:2 * D] = jnp.zeros((1, D), F32)
     bias[0:1, 2 * D:] = vec_ref[3:4, :]
@@ -84,8 +86,15 @@
         x = xs[i * SEQ:i * SEQ + ROWS, :]
         cen = x - jnp.mean(x, axis=1, keepdims=True)
         inv = lax.rsqrt(jnp.mean(cen * cen, axis=1, keepdims=True) + 1e-6)
-        h1[i * ROWS:(i + 1) * ROWS, :] = (cen * inv * vec_ref[0:1, :] + vec_ref[1:2, :]).astype(BF)
-    send(0, h1, h1_h)
+        xh = cen * inv
+        rows = slice(i * ROWS, (i + 1) * ROWS)
+        xh1[rows, :] = xh.astype(BF)
+        rstd1[rows, :] = jnp.broadcast_to(inv, (ROWS, 128))
+        h1[rows, :] = (xh * vec_ref[0:1, :] + vec_ref[1:2, :]).astype(BF)
+    send(8, xh1, xh1_h)
+    send(9, rstd1, rstd1_h)
+    h1t[...] = h1[...].T
+    send(10, h1t, h1t_h)
     loads[0].wait()
     span = images * ROWS
     pad = qkv.shape[1] - span
@@ -124,7 +133,9 @@
 
     lax.fori_loop(0, images * n_quads, attend, 0)
     send(2, p_s, p_h)
-    send(3, o_s, o_h)
+    for j in range(n_quads):
+        ot[j * TILE:(j + 1) * TILE, :] = o_s[j].T
+    send(3, ot, ot_h)
     loads[1].wait()
     pooled_ref[...] = jnp.zeros_like(pooled_ref)
     for i in range(images):
@@ -139,11 +150,12 @@
         inv = lax.rsqrt(jnp.mean(cen * cen, axis=1, keepdims=True) + 1e-6)
         xh = cen * inv
         xh2[rows, :] = xh.astype(BF)
-        rstd[rows, :] = jnp.broadcast_to(inv, (ROWS, 128))
+        rstd2[rows, :] = jnp.broadcast_to(inv, (ROWS, 128))
         h2[rows, :] = (xh * vec_ref[5:6, :] + vec_ref[6:7, :]).astype(BF)
-    send(4, h2, h2_h)
+    h2t[...] = h2[...].T
+    send(4, h2t, h2t_h)
     send(5, xh2, xh2_h)
-    send(6, rstd, rstd_h)
+    send(6, rstd2, rstd2_h)
     loads[2].wait()
     loads[3].wait()
     acc[...] = jnp.zeros_like(acc)
@@ -186,236 +198,30 @@
     nq = D // TILE
     wide = span + WIN - ROWS
     outs = [
-        ((span, D), BF), ((3 * nq, wide, TILE), BF), ((images * nq, 4 * ROWS, TILE), BF),
-        ((nq, span, TILE), BF), ((span, D), BF), ((span, D), BF), ((span, 128), F32),
-        ((ff // TILE, span, TILE), BF), ((ff // D, 8, D), F32), ((8, D + 128), F32),
+        ((D, span), BF), ((3 * nq, wide, TILE), BF), ((images * nq, 4 * ROWS, TILE), BF),
+        ((D, span), BF), ((D, span), BF), ((span, D), BF), ((span, D), BF), ((span, 128), F32), ((span, 128), F32),
+        ((span, 128), F32), ((ff // TILE, span, TILE), BF), ((ff // D, 8, D), F32), ((8, D + 128), F32),
     ]
     anyspec = pl.BlockSpec(memory_space=pl.ANY)
     vm = pl.BlockSpec(memory_space=pltpu.VMEM)
     scratch = [
         pltpu.VMEM((D, 3 * D), BF), pltpu.VMEM((D, D), BF), pltpu.VMEM((D, ff), BF), pltpu.VMEM((ff, D), BF),
         pltpu.VMEM(((images - 1) * SEQ + ROWS + 7 & -8, D), F32),
-    ] + [pltpu.VMEM(*o) for o in outs[:8]] + [
+    ] + [pltpu.VMEM(*o) for o in outs[:11]] + [
+        pltpu.VMEM((span, D), BF), pltpu.VMEM((nq, span, TILE), BF), pltpu.VMEM((span, D), BF),
         pltpu.VMEM((wide, TILE), BF), pltpu.VMEM((16, WIN), F32), pltpu.VMEM((images, 16, WIN), BF),
-        pltpu.VMEM((span, 128), F32), pltpu.VMEM((1, 3 * D), F32), pltpu.VMEM((16, D), F32),
-        pltpu.SemaphoreType.DMA((4,)), pltpu.SemaphoreType.DMA((8,)),
+        pltpu.VMEM((1, 3 * D), F32), pltpu.VMEM((16, D), F32),
+        pltpu.SemaphoreType.DMA((4,)), pltpu.SemaphoreType.DMA((11,)),
     ]
     return pl.pallas_call(
         functools.partial(forward_kernel, images, ff),
         out_shape=[jax.ShapeDtypeStruct(s, d) for s, d in outs],
         in_specs=[vm, vm] + [anyspec] * 4 + [vm, vm],
-        out_specs=[anyspec] * 8 + [vm, vm],
+        out_specs=[anyspec] * 11 + [vm, vm],
         scratch_shapes=scratch,
         compiler_params=pltpu.CompilerParams(vmem_limit_bytes=60 * 2**20),
         name="block_forward",
     )(tokens, keep, wqkv, wout, wup, wdown, vec, upb)
-
-
-def backward_kernel(
-    images, ff,
-    tok_ref, keep_ref, dy_ref, da_s, vec_ref,
-    wqkv_h, wout_h, wup_h, h1_h, qkv_h, p_h, o_h, h2_h, xh2_h, rstd_h, gk_h,
-    tg_ref, g_ref, vg_ref, ub_ref,
-    wqkv, wout, wup, h1, qkv, p_s, o_s, h2, xh2, rstd, du,
-    xs, dx, db, do_s, dp_s, h1t, h2t, keep8, kcol,
-    in_sem, gk_sem, p_sem,
-):
-    n_quads = D // TILE
-    n_ff = ff // TILE
-    span = images * ROWS
-    masks = head_masks()
-    loads = {}
-    for k, (name, src, dst) in enumerate((
-        ("h2", h2_h, h2), ("wup", wup_h, wup), ("xh2", xh2_h, xh2),
-        ("rstd", rstd_h, rstd), ("wout", wout_h, wout), ("o", o_h, o_s), ("qkv", qkv_h, qkv),
-        ("h1", h1_h, h1), ("wqkv", wqkv_h, wqkv),
-    )):
-        loads[name] = pltpu.make_async_copy(src, dst, in_sem.at[k])
-    for name in ("h2",):
-        loads[name].start()
-    gks = []
-    for t in range(n_ff):
-        c = pltpu.make_async_copy(gk_h.at[t], du.at[:, t * TILE:(t + 1) * TILE], gk_sem.at[t])
-        c.start()
-        gks.append(c)
-    for name in ("wup", "xh2", "rstd", "wout", "o", "qkv", "h1", "wqkv"):
-        loads[name].start()
-
-    def pcopy(i, j, slot):
-        return pltpu.make_async_copy(p_h.at[i * n_quads + j], p_s.at[slot], p_sem.at[slot])
-
-    pcopy(0, 0, 0).start()
-
-    total = images * SEQ
-    last = total // 16 * 16
-    xs[last:, :] = jnp.zeros_like(xs[last:, :])
-    xs[0:last, :] = tok_ref[0:last, :].astype(F32)
-    if last < total:
-        xs[last:total, :] = tok_ref[last:total, :].astype(F32)
-    keep8[...] = jnp.zeros_like(keep8)
-    keep8[0:images, 0:SEQ] = keep_ref[...].astype(F32)
-    kb = keep8[...]
-    rid = lax.broadcasted_iota(jnp.int32, kb.shape, 0)
-    one = jnp.ones((kb.shape[0], 128), F32).astype(BF)
-    for i in range(images):
-        km = jnp.where(rid == i, kb, 0.0).astype(BF)
-        kcol[i * ROWS:(i + 1) * ROWS, :] = mm(km, one, TN)[0:ROWS]
-
-    dy = dy_ref[...]
-    dyb = dy.astype(BF)
-    cnt = jnp.sum(kb, axis=1, keepdims=True)[0:8]
-    vg_ref[7:8, :] = jnp.sum(dyb.astype(F32) * cnt, axis=0, keepdims=True)
-    loads["h2"].wait()
-    h2t[...] = h2[...].T
-    for c in gks:
-        c.wait()
-
-    def expand(t, _):
-        col = pl.multiple_of(t * TILE, TILE)
-        ub = jnp.zeros((1, TILE), F32)
-        for i in range(images):
-            rows = slice(i * ROWS, (i + 1) * ROWS)
-            d = du[rows, pl.ds(col, TILE)].astype(F32) * da_s[i:i + 1, pl.ds(col, TILE)]
-            ub = ub + jnp.sum(d, axis=0, keepdims=True)
-            du[rows, pl.ds(col, TILE)] = d.astype(BF)
-        ub_ref[:, pl.ds(col, TILE)] = ub
-        part = mm(h2t[...], du[:, pl.ds(col, TILE)])
-        c3 = pl.multiple_of((t % 3) * TILE, TILE)
-        g_ref[t // 3, :, pl.ds(c3, TILE)] = part.astype(BF)
-        return 0
-
-    lax.fori_loop(0, n_ff, expand, 0)
-    loads["wup"].wait()
-
-    def down(n, _):
-        col = pl.multiple_of(n * TILE, TILE)
-        dx[:, pl.ds(col, TILE)] = mm(du[...], wup[pl.ds(col, TILE), :], NT)
-        return 0
-
-    lax.fori_loop(0, n_quads, down, 0)
-    for name in ("xh2", "rstd", "wout", "o"):
-        loads[name].wait()
-    g2 = jnp.zeros((1, D), F32)
-    b2 = jnp.zeros((1, D), F32)
-    bo = jnp.zeros((1, D), F32)
-    for i in range(images):
-        rows = slice(i * ROWS, (i + 1) * ROWS)
-        dh = dx[rows, :]
-        xh = xh2[rows, :].astype(F32)
-        g2 = g2 + jnp.sum(dh * xh, axis=0, keepdims=True)
-        b2 = b2 + jnp.sum(dh, axis=0, keepdims=True)
-        c = dh * vec_ref[5:6, :]
-        m1 = jnp.mean(c, axis=1, keepdims=True)
-        m2 = jnp.mean(c * xh, axis=1, keepdims=True)
-        r = dy[i:i + 1, :] * kcol[rows, 0:1] + rstd[rows, 0:1] * (c - m1 - xh * m2)
-        dx[rows, :] = r
-        rb = r.astype(BF)
-        db[rows, :] = rb
-        bo = bo + jnp.sum(rb.astype(F32), axis=0, keepdims=True)
-    vg_ref[5:6, :] = g2
-    vg_ref[6:7, :] = b2
-    vg_ref[4:5, :] = bo
-    for j in range(n_quads):
-        sl = slice(j * TILE, (j + 1) * TILE)
-        do_s[j] = mm(db[...], wout[sl, :], NT).astype(BF)
-        for n in range(n_quads):
-            g_ref[4, sl, n * TILE:(n + 1) * TILE] = mm(
-                o_s[j], db[:, n * TILE:(n + 1) * TILE], TN).astype(BF)
-    for name in ("qkv", "h1"):
-        loads[name].wait()
-    h1t[...] = h1[...].T
-
-    def quad(j, _):
-        def attend(i, _):
-            r0 = pl.multiple_of(i * ROWS, 16)
-            step = j * images + i
-            slot = step % 2
-            nxt = step + 1
-
-            @pl.when(nxt < n_quads * images)
-            def _():
-                pcopy(nxt % images, nxt // images, nxt % 2).start()
-
-            pcopy(i, j, slot).wait()
-            q4 = qkv[j, pl.ds(r0, ROWS), :]
-            k4 = qkv[n_quads + j, pl.ds(r0, WIN), :]
-            v4 = qkv[2 * n_quads + j, pl.ds(r0, WIN), :]
-            d4 = do_s[j, pl.ds(r0, ROWS), :]
-            dq = jnp.zeros((ROWS, TILE), F32)
-            dk = jnp.zeros((WIN, TILE), F32)
-            dv = jnp.zeros((WIN, TILE), F32)
-            for h, m in enumerate(masks):
-                pb = p_s[slot, h * ROWS:(h + 1) * ROWS, :]
-                dm = d4 * m
-                dv = dv + mm(pb, dm, TN)
-                dpr = mm(dm, v4, NT)
-                pf = pb.astype(F32)
-                ds = (pf * (dpr - jnp.sum(pf * dpr, axis=1, keepdims=True))).astype(BF)
-                dq = dq + mm(ds, k4 * m)
-                dk = dk + mm(ds, q4 * m, TN)
-            dq = dq * HEAD_DIM ** -0.5
-            for s, val in enumerate((dq, dk[0:ROWS], dv[0:ROWS])):
-                col = pl.multiple_of(s * D + j * TILE, TILE)
-                dp_s[pl.ds(r0, ROWS), pl.ds(col, TILE)] = val.astype(BF)
-            return 0
-
-        lax.fori_loop(0, images, attend, 0)
-        for s in range(3):
-            col = pl.multiple_of(s * D + j * TILE, TILE)
-            g_ref[5 + j, :, s * TILE:(s + 1) * TILE] = mm(h1t[...], dp_s[:, pl.ds(col, TILE)]).astype(BF)
-        return 0
-
-    lax.fori_loop(0, n_quads, quad, 0)
-    vg_ref[2:3, :] = jnp.sum(dp_s[:, 0:D].astype(F32), axis=0, keepdims=True)
-    vg_ref[3:4, :] = jnp.sum(dp_s[:, 2 * D:].astype(F32), axis=0, keepdims=True)
-    loads["wqkv"].wait()
-    g1 = jnp.zeros((1, D), F32)
-    b1 = jnp.zeros((1, D), F32)
-    for i in range(images):
-        rows = slice(i * ROWS, (i + 1) * ROWS)
-        dh = mm(dp_s[rows, :], wqkv[...], NT)
-        x = xs[i * SEQ:i * SEQ + ROWS, :]
-        cen = x - jnp.mean(x, axis=1, keepdims=True)
-        inv = lax.rsqrt(jnp.mean(cen * cen, axis=1, keepdims=True) + 1e-6)
-        xh = cen * inv
-        g1 = g1 + jnp.sum(dh * xh, axis=0, keepdims=True)
-        b1 = b1 + jnp.sum(dh, axis=0, keepdims=True)
-        c = dh * vec_ref[0:1, :]
-        m1 = jnp.mean(c, axis=1, keepdims=True)
-        m2 = jnp.mean(c * xh, axis=1, keepdims=True)
-        r = dx[rows, :] + inv * (c - m1 - xh * m2)
-        tg_ref[i * SEQ:(i + 1) * SEQ, :] = r[0:SEQ]
-    vg_ref[0:1, :] = g1
-    vg_ref[1:2, :] = b1
-
-
-def backward_call(images, ff, tokens, keep, dy, da, vec, wqkv, wout, wup, acts):
-    span = images * ROWS
-    nq = D // TILE
-    wide = span + WIN - ROWS
-    anyspec = pl.BlockSpec(memory_space=pl.ANY)
-    vm = pl.BlockSpec(memory_space=pltpu.VMEM)
-    outs = [((images * SEQ, D), F32), ((ff // D + 4, D, D), BF), ((8, D), F32), ((1, ff), F32)]
-    scratch = [
-        pltpu.VMEM((D, 3 * D), BF), pltpu.VMEM((D, D), BF), pltpu.VMEM((D, ff), BF),
-        pltpu.VMEM((span, D), BF), pltpu.VMEM((3 * nq, wide, TILE), BF), pltpu.VMEM((2, 4 * ROWS, TILE), BF),
-        pltpu.VMEM((nq, span, TILE), BF), pltpu.VMEM((span, D), BF), pltpu.VMEM((span, D), BF),
-        pltpu.VMEM((span, 128), F32), pltpu.VMEM((span, ff), BF),
-        pltpu.VMEM(((images - 1) * SEQ + ROWS + 7 & -8, D), F32), pltpu.VMEM((span, D), F32),
-        pltpu.VMEM((span, D), BF), pltpu.VMEM((nq, span, TILE), BF), pltpu.VMEM((span, 3 * D), BF),
-        pltpu.VMEM((D, span), BF), pltpu.VMEM((D, span), BF), pltpu.VMEM((16, WIN), F32),
-        pltpu.VMEM((span, 128), F32),
-        pltpu.SemaphoreType.DMA((10,)), pltpu.SemaphoreType.DMA((ff // TILE,)), pltpu.SemaphoreType.DMA((2,)),
-    ]
-    return pl.pallas_call(
-        functools.partial(backward_kernel, images, ff),
-        out_shape=[jax.ShapeDtypeStruct(s, d) for s, d in outs],
-        in_specs=[vm] * 5 + [anyspec] * 11,
-        out_specs=[vm] * 4,
-        scratch_shapes=scratch,
-        compiler_params=pltpu.CompilerParams(vmem_limit_bytes=62 * 2**20),
-        name="block_backward",
-    )(tokens, keep, dy, da, vec, wqkv, wout, wup, *acts)
 
 
 def split3(x):
@@ -613,6 +419,413 @@
     )(pooled, texts, apool, pair, scale, wproj, wdown)
 
 
+def backward_kernel(
+    n_row, cz, cy, images, ff, n_a,
+    dy_ref, da_ref, vec_ref,
+    wqkv_h, wout_h, wup_h, h1t_h, qkv_h, p_h, ot_h, h2t_h, xh1_h, xh2_h, rstd1_h, rstd2_h, kcol_h, gk_h,
+    tg_ref, qg_ref, og_ref, ug_ref, small_ref,
+    wqkv, wout, wup, h1t, qkv, ot, h2t, xh1, xh2, rstd1, rstd2, kcol, p_s, du, dx, db, do_s, dp_s,
+    g, r0, r1a, r1b, r2a, r2b, r3a, r3b, r4b, res, vc, vp, vz,
+    in_sem, gk_sem, p_sem, s_sem, r_sem, vs_sem, vr_sem,
+):
+    n_quads = D // TILE
+    n_ff = ff // TILE
+    n_up = ff // D
+    n_chunks = n_up + 1 + n_quads
+    masks = head_masks()
+    x, z, y, core = place(cz, cy)
+    two = n_a < D
+    n_h = (D - n_a) // 2
+    plane = n_row * cy
+    spot = x * cy + y
+
+    def device(xx, zz, yy, cc):
+        return (xx, (zz * cy + yy) * 2 + cc)
+
+    core_dev = device(x, z, y, 1 - core)
+    y_peers = [lax.rem(y + k, cy) for k in range(1, cy)]
+    z_peers = [lax.rem(z + k, cz) for k in range(1, cz)]
+    x_peers = [lax.rem(x + k, n_row) for k in range(1, n_row)]
+    p_peers = [lax.rem(spot + k, plane) for k in range(1, plane)]
+    z_devs = [device(x, zz, y, core) for zz in z_peers]
+    y_devs = [device(x, z, yy, core) for yy in y_peers]
+    x_devs = [device(xx, z, y, core) for xx in x_peers]
+    p_devs = [device(pp // cy, z, lax.rem(pp, cy), core) for pp in p_peers]
+
+    loads = {}
+    for k, (name, src, dst) in enumerate((
+        ("kcol", kcol_h, kcol), ("h2t", h2t_h, h2t), ("wup", wup_h, wup), ("xh2", xh2_h, xh2),
+        ("rstd2", rstd2_h, rstd2), ("wout", wout_h, wout), ("ot", ot_h, ot), ("qkv", qkv_h, qkv),
+        ("h1t", h1t_h, h1t), ("wqkv", wqkv_h, wqkv), ("xh1", xh1_h, xh1), ("rstd1", rstd1_h, rstd1),
+    )):
+        loads[name] = pltpu.make_async_copy(src, dst, in_sem.at[k])
+
+    def gcopy(t):
+        col = pl.multiple_of(t * TILE, TILE)
+        return pltpu.make_async_copy(gk_h.at[t], du.at[:, pl.ds(col, TILE)], gk_sem.at[t])
+
+    loads["h2t"].start()
+    for t in range(n_ff):
+        gcopy(t).start()
+    for name in ("kcol", "wup", "xh2", "rstd2", "wout", "ot", "qkv", "h1t", "wqkv", "xh1", "rstd1"):
+        loads[name].start()
+
+    def pcopy(step):
+        i = lax.rem(step, images)
+        j = step // images
+        slot = lax.rem(step, 2)
+        return pltpu.make_async_copy(p_h.at[i * n_quads + j], p_s.at[slot], p_sem.at[slot])
+
+    pcopy(0).start()
+    bar = pltpu.get_barrier_semaphore()
+    for dev in z_devs + p_devs + [core_dev]:
+        pl.semaphore_signal(bar, inc=1, device_id=dev, device_id_type=MESH)
+    pl.semaphore_wait(bar, len(z_devs) + len(p_devs) + 1)
+
+    half = lambda which: pl.ds(pl.multiple_of(n_a + which * n_h, 128), n_h)
+
+    def copies(p, c):
+        if p == 0:
+            out = [(g.at[lax.rem(c, 2), :, :, 1 - core], r0.at[c], core_dev)]
+        elif p == 1:
+            out = [(r0.at[c, :, yy, :, 0:n_a], r1a.at[c, k], dev) for k, (yy, dev) in enumerate(zip(y_peers, y_devs))]
+            if two:
+                out += [(r0.at[c, :, :, :, half(1 - x)], r1b.at[c], x_devs[0])]
+        elif p == 2:
+            out = [(r1a.at[c, 0, zz], r2a.at[c, k], dev) for k, (zz, dev) in enumerate(zip(z_peers, z_devs))]
+            if two:
+                out += [(r1b.at[c, :, yy], r2b.at[c, k], dev) for k, (yy, dev) in enumerate(zip(y_peers, y_devs))]
+        elif p == 3:
+            out = [(r3a.at[c, x], r3a.at[c, x], dev) for dev in x_devs]
+            if two:
+                out += [(r2b.at[c, 0, zz], r3b.at[c, k], dev) for k, (zz, dev) in enumerate(zip(z_peers, z_devs))]
+        else:
+            out = [(r3b.at[c, 0], r4b.at[c], x_devs[0])] if two else []
+        base = p * s_sem.shape[1] // 5
+        return [
+            pltpu.make_async_remote_copy(
+                src, dst, s_sem.at[c, base + k], r_sem.at[c, base + k], device_id=dev, device_id_type=MESH)
+            for k, (src, dst, dev) in enumerate(out)
+        ]
+
+    def finish(p, c):
+        up = lambda v: v.astype(F32)
+        if p == 0:
+            r0[c] = (up(r0[c]) + up(g[lax.rem(c, 2), :, :, core])).astype(BF)
+        elif p == 1:
+            v = up(r0[c, :, y, :, 0:n_a])
+            for k in range(cy - 1):
+                v = v + up(r1a[c, k])
+            r1a[c, 0] = v.astype(BF)
+            if two:
+                r1b[c] = (up(r1b[c]) + up(r0[c, :, :, :, half(x)])).astype(BF)
+        elif p == 2:
+            v = up(r1a[c, 0, z])
+            for k in range(cz - 1):
+                v = v + up(r2a[c, k])
+            r3a[c, x] = v.astype(BF)
+            if two:
+                v = up(r1b[c, :, y])
+                for k in range(cy - 1):
+                    v = v + up(r2b[c, k])
+                r2b[c, 0] = v.astype(BF)
+        elif p == 3:
+            v = up(r3a[c, 0])
+            for k in range(1, n_row):
+                v = v + up(r3a[c, k])
+            res[c, :, 0:n_a] = v
+            if two:
+                v = up(r2b[c, 0, z])
+                for k in range(cz - 1):
+                    v = v + up(r3b[c, k])
+                v = v.astype(BF)
+                r3b[c, 0] = v
+                res[c, :, half(x)] = up(v)
+        elif two:
+            res[c, :, half(1 - x)] = up(r4b[c])
+
+    def begin(p, c):
+        for d in copies(p, c):
+            d.start()
+
+    def advance(p, c):
+        for d in copies(p, c):
+            d.wait()
+        finish(p, c)
+        if p < 4:
+            begin(p + 1, c)
+
+    first = n_up + 2
+    last_unit = first + 2 * n_quads + images
+
+    def chunk_at(n):
+        odd = jnp.maximum((n - (n_up - 1)) // 2, 0)
+        return n - odd
+
+    def has_chunk(n):
+        return (n >= 0) & ((n < n_up) | ((lax.rem(n - n_up, 2) == 1) & (n < first + 2 * n_quads)))
+
+    def tick(n):
+        @pl.when(has_chunk(n))
+        def _():
+            begin(0, chunk_at(n))
+
+        for p in range(4, -1, -1):
+            m = n - 1 - p
+
+            @pl.when(has_chunk(m))
+            def _(p=p, m=m):
+                advance(p, chunk_at(m))
+
+    def put(c, tt, part):
+        col = pl.multiple_of(tt * TILE, TILE)
+        g[lax.rem(c, 2), :, :, :, :, pl.ds(col, TILE)] = part.reshape(g.shape[1:5] + (TILE,)).astype(BF)
+
+    def unit_up(n):
+        def expand(tt, _):
+            t = n * n_quads + tt
+            col = pl.multiple_of(t * TILE, TILE)
+            gcopy(t).wait()
+            ub = jnp.zeros((1, TILE), F32)
+            for i in range(images):
+                rows = slice(i * ROWS, (i + 1) * ROWS)
+                d = du[rows, pl.ds(col, TILE)].astype(F32) * da_ref[i:i + 1, pl.ds(col, TILE)]
+                ub = ub + jnp.sum(d, axis=0, keepdims=True)
+                du[rows, pl.ds(col, TILE)] = d.astype(BF)
+            scol = pl.multiple_of(tt * TILE, TILE)
+            small_ref[pl.ds(8 + n, 1), pl.ds(scol, TILE)] = ub
+            put(n, tt, mm(h2t[...], du[:, pl.ds(col, TILE)]))
+            return 0
+
+        lax.fori_loop(0, n_quads, expand, 0)
+
+    def unit_down():
+        loads["wup"].wait()
+
+        def down(n, _):
+            col = pl.multiple_of(n * TILE, TILE)
+            dx[:, pl.ds(col, TILE)] = mm(du[...], wup[pl.ds(col, TILE), :], NT)
+            return 0
+
+        lax.fori_loop(0, n_quads, down, 0)
+
+    def unit_mid():
+        for name in ("kcol", "xh2", "rstd2", "wout", "ot"):
+            loads[name].wait()
+        dy = dy_ref[...]
+        dyb = dy.astype(BF).astype(F32)
+        g2 = jnp.zeros((1, D), F32)
+        b2 = jnp.zeros((1, D), F32)
+        bo = jnp.zeros((1, D), F32)
+        bd = jnp.zeros((1, D), F32)
+        for i in range(images):
+            rows = slice(i * ROWS, (i + 1) * ROWS)
+            kc = kcol[rows, 0:1]
+            bd = bd + jnp.sum(kc, axis=0, keepdims=True) * dyb[i:i + 1, :]
+            dh = dx[rows, :]
+            xh = xh2[rows, :].astype(F32)
+            g2 = g2 + jnp.sum(dh * xh, axis=0, keepdims=True)
+            b2 = b2 + jnp.sum(dh, axis=0, keepdims=True)
+            c = dh * vec_ref[5:6, :]
+            m1 = jnp.mean(c, axis=1, keepdims=True)
+            m2 = jnp.mean(c * xh, axis=1, keepdims=True)
+            r = dy[i:i + 1, :] * kc + rstd2[rows, 0:1] * (c - m1 - xh * m2)
+            dx[rows, :] = r
+            rb = r.astype(BF)
+            db[rows, :] = rb
+            bo = bo + jnp.sum(rb.astype(F32), axis=0, keepdims=True)
+        small_ref[0:4, :] = jnp.zeros((4, D), F32)
+        small_ref[4:5, :] = bo
+        small_ref[5:6, :] = g2
+        small_ref[6:7, :] = b2
+        small_ref[7:8, :] = bd
+        for j in range(n_quads):
+            sl = slice(j * TILE, (j + 1) * TILE)
+            do_s[j] = mm(db[...], wout[sl, :], NT).astype(BF)
+            put(n_up, j, mm(ot[...], db[:, sl]))
+        for name in ("qkv", "h1t"):
+            loads[name].wait()
+
+    def unit_attend(m):
+        j = m // 2
+
+        def attend(ii, _):
+            i = lax.rem(m, 2) * (images // 2) + ii
+            r0_ = pl.multiple_of(i * ROWS, 16)
+            step = j * images + i
+            slot = lax.rem(step, 2)
+
+            @pl.when(step + 1 < n_quads * images)
+            def _():
+                pcopy(step + 1).start()
+
+            pcopy(step).wait()
+            q4 = qkv[j, pl.ds(r0_, ROWS), :]
+            k4 = qkv[n_quads + j, pl.ds(r0_, WIN), :]
+            v4 = qkv[2 * n_quads + j, pl.ds(r0_, WIN), :]
+            d4 = do_s[j, pl.ds(r0_, ROWS), :]
+            dq = jnp.zeros((ROWS, TILE), F32)
+            dk = jnp.zeros((WIN, TILE), F32)
+            dv = jnp.zeros((WIN, TILE), F32)
+            for h, mask in enumerate(masks):
+                pb = p_s[slot, h * ROWS:(h + 1) * ROWS, :]
+                dm = d4 * mask
+                dv = dv + mm(pb, dm, TN)
+                dpr = mm(dm, v4, NT)
+                pf = pb.astype(F32)
+                ds = (pf * (dpr - jnp.sum(pf * dpr, axis=1, keepdims=True))).astype(BF)
+                dq = dq + mm(ds, k4 * mask)
+                dk = dk + mm(ds, q4 * mask, TN)
+            dq = dq * HEAD_DIM ** -0.5
+            dv = dv[0:ROWS]
+            sl = pl.ds(pl.multiple_of(j * TILE, TILE), TILE)
+            small_ref[2:3, sl] += jnp.sum(dq, axis=0, keepdims=True)
+            small_ref[3:4, sl] += jnp.sum(dv, axis=0, keepdims=True)
+            for s, val in enumerate((dq, dk[0:ROWS], dv)):
+                col = pl.multiple_of(s * D + j * TILE, TILE)
+                dp_s[pl.ds(r0_, ROWS), pl.ds(col, TILE)] = val.astype(BF)
+            return 0
+
+        lax.fori_loop(0, images // 2, attend, 0)
+
+        @pl.when(lax.rem(m, 2) == 1)
+        def _():
+            for s in range(3):
+                col = pl.multiple_of(s * D + j * TILE, TILE)
+                put(n_up + 1 + j, s, mm(h1t[...], dp_s[:, pl.ds(col, TILE)]))
+
+    def unit_norm(i):
+        @pl.when(i == 0)
+        def _():
+            for name in ("wqkv", "xh1", "rstd1"):
+                loads[name].wait()
+
+        rows = pl.ds(pl.multiple_of(i * ROWS, 16), ROWS)
+        dh = mm(dp_s[rows, :], wqkv[...], NT)
+        xh = xh1[rows, :].astype(F32)
+        small_ref[0:1, :] += jnp.sum(dh * xh, axis=0, keepdims=True)
+        small_ref[1:2, :] += jnp.sum(dh, axis=0, keepdims=True)
+        c = dh * vec_ref[0:1, :]
+        m1 = jnp.mean(c, axis=1, keepdims=True)
+        m2 = jnp.mean(c * xh, axis=1, keepdims=True)
+        r = dx[rows, :] + rstd1[rows, 0:1] * (c - m1 - xh * m2)
+        for k in range(images):
+            @pl.when(i == k)
+            def _(k=k):
+                tg_ref[k * SEQ:(k + 1) * SEQ, :] = r[0:SEQ]
+
+    small_ref[...] = jnp.zeros_like(small_ref)
+    loads["h2t"].wait()
+
+    def unit(n, _):
+        @pl.when(n < n_up)
+        def _():
+            unit_up(n)
+
+        @pl.when(n == n_up)
+        def _():
+            unit_down()
+
+        @pl.when(n == n_up + 1)
+        def _():
+            unit_mid()
+
+        @pl.when((n >= first) & (n < first + 2 * n_quads))
+        def _():
+            unit_attend(n - first)
+
+        @pl.when(n >= first + 2 * n_quads)
+        def _():
+            unit_norm(n - first - 2 * n_quads)
+
+        tick(n)
+        return 0
+
+    lax.fori_loop(0, last_unit, unit, 0)
+
+    def spread(src, sems, slot, devs):
+        out = []
+        for k, dev in enumerate(devs):
+            d = pltpu.make_async_remote_copy(
+                src, src, vs_sem.at[slot, k], vr_sem.at[slot, k], device_id=dev, device_id_type=MESH)
+            d.start()
+            out.append(d)
+        return out
+
+    def total(ref, count):
+        v = ref[0]
+        for k in range(1, count):
+            v = v + ref[k]
+        return v
+
+    n = last_unit
+    last_start = first + 2 * n_quads - 1
+    vc[core] = small_ref[...]
+    going = spread(vc.at[core], None, 0, [core_dev])
+    for p in range(n - 1 - last_start, 5):
+        advance(p, n_chunks - 1)
+        for d in going:
+            d.wait()
+        going = []
+        if p == n - 1 - last_start:
+            vp[spot] = total(vc, 2)
+            going = spread(vp.at[spot], None, 1, p_devs)
+    for d in going:
+        d.wait()
+    vz[z] = total(vp, plane)
+    for d in spread(vz.at[z], None, 2, z_devs):
+        d.wait()
+    small_ref[...] = total(vz, cz)
+    for c in range(n_up):
+        ug_ref[:, c * D:(c + 1) * D] = res[c]
+    og_ref[...] = res[n_up]
+    for j in range(n_quads):
+        for s in range(3):
+            qg_ref[:, s * D + j * TILE:s * D + (j + 1) * TILE] = res[n_up + 1 + j, :, s * TILE:(s + 1) * TILE]
+
+
+def backward_call(n_row, n_col, images, ff, dy, da, vec, wqkv, wout, wup, acts):
+    span = images * ROWS
+    nq = D // TILE
+    wide = span + WIN - ROWS
+    cz = ff // D
+    cy = n_col // (2 * cz)
+    blk = D // n_col
+    n_a = 256 if n_row == 2 else D
+    n_h = max((D - n_a) // 2, 128)
+    n_ch = ff // D + 1 + nq
+    plane = n_row * cy
+    n_sem = 5 * (max(cy, cz, n_row) - 1 + max(cy, cz))
+    anyspec = pl.BlockSpec(memory_space=pl.ANY)
+    vm = pl.BlockSpec(memory_space=pltpu.VMEM)
+    outs = [(images * SEQ, D), (blk, 3 * D), (blk, D), (blk, ff), (16, D)]
+    B16 = lambda *s: pltpu.VMEM(s, BF)
+    B32 = lambda *s: pltpu.VMEM(s, F32)
+    scratch = [
+        B16(D, 3 * D), B16(D, D), B16(D, ff), B16(D, span), B16(3 * nq, wide, TILE), B16(D, span), B16(D, span),
+        B16(span, D), B16(span, D), B32(span, 128), B32(span, 128), B32(span, 128),
+        B16(2, 4 * ROWS, TILE), B16(span, ff), B32(span, D), B16(span, D), B16(nq, span, TILE), B16(span, 3 * D),
+        B16(2, cz, cy, 2, blk, D), B16(n_ch, cz, cy, blk, D),
+        B16(n_ch, cy - 1, cz, blk, n_a), B16(n_ch, cz, cy, blk, n_h),
+        B16(n_ch, cz - 1, blk, n_a), B16(n_ch, cy - 1, cz, blk, n_h),
+        B16(n_ch, n_row, blk, n_a), B16(n_ch, cz - 1, blk, n_h), B16(n_ch, blk, n_h), B32(n_ch, blk, D),
+        B32(2, 16, D), B32(plane, 16, D), B32(cz, 16, D),
+        pltpu.SemaphoreType.DMA((12,)), pltpu.SemaphoreType.DMA((ff // TILE,)), pltpu.SemaphoreType.DMA((2,)),
+        pltpu.SemaphoreType.DMA((n_ch, n_sem)), pltpu.SemaphoreType.DMA((n_ch, n_sem)),
+        pltpu.SemaphoreType.DMA((3, plane)), pltpu.SemaphoreType.DMA((3, plane)),
+    ]
+    return pl.pallas_call(
+        functools.partial(backward_kernel, n_row, cz, cy, images, ff, n_a),
+        out_shape=[jax.ShapeDtypeStruct(s, F32) for s in outs],
+        in_specs=[vm] * 3 + [anyspec] * 14,
+        out_specs=[vm] * len(outs),
+        scratch_shapes=scratch,
+        compiler_params=pltpu.CompilerParams(
+            vmem_limit_bytes=62 * 2**20, collective_id=1, has_side_effects=True),
+        name="block_backward",
+    )(dy, da, vec, wqkv, wout, wup, *acts)
+
+
 def per_device(
     tokens,
     keep_mask,
@@ -635,22 +848,13 @@
         images, ff, tokens, keep_mask, w_qkv, w_out, w_up, w_down, vectors, up_bias.reshape(1, ff)
     )
     loss, dy, da, text_grad, grad_proj, grad_down = head_call(
-        n_row, shards, images, ff, acts[9], texts, acts[8], pair_index.reshape(1, -1), logit_scale, w_proj, w_down
+        n_row, shards, images, ff, acts[12], texts, acts[11], pair_index.reshape(1, -1), logit_scale, w_proj, w_down
     )
-    token_grad, grads, grad_vectors, grad_up_bias = backward_call(
-        images, ff, tokens, keep_mask, dy, da, vectors, w_qkv, w_out, w_up, acts[:8]
+    token_grad, qkv_share, out_share, up_share, small = backward_call(
+        n_row, shards, images, ff, dy, da, vectors, w_qkv, w_out, w_up, acts[:11]
     )
-    part = lax.psum_scatter(grads, "col", scatter_dimension=1, tiled=True)
-    part = lax.psum(part, "row").astype(jnp.float32)
-    n_up = ff // D
-    up_share = part[:n_up].transpose(1, 0, 2).reshape(-1, ff)
-    out_share = part[n_up]
-    qkv_share = part[n_up + 1 :].reshape(D // TILE, -1, 3, TILE).transpose(1, 2, 0, 3)
-    qkv_share = qkv_share.reshape(-1, 3 * D)
-    small = jnp.concatenate([grad_vectors, grad_up_bias.reshape(ff // D, D)], axis=0)
-    small = lax.psum(small, ("row", "col"))
     vec_share = lax.dynamic_slice_in_dim(small[:8], mine * (D // shards), D // shards, axis=1)
-    bias_share = lax.dynamic_slice_in_dim(small[8:].reshape(ff), mine * (ff // shards), ff // shards)
+    bias_share = lax.dynamic_slice_in_dim(small[8 : 8 + ff // D].reshape(ff), mine * (ff // shards), ff // shards)
     return (
         loss.reshape(1),
         token_grad,

time: 297 us -> 177 us (0.60)
  waiting for transfers between devices: 111 us -> 0 us
  Pallas kernels: 119 us -> 163 us
  blocking collectives: 40.7 us -> 0 us
  between operations: 16.6 us -> 3.18 us
  local copies, waits for them, and re-layouts: 7.14 us -> 10.5 us
    reduce_scatter x1 -> x0, waiting for transfers between devices: 111 us -> none  [per_device(): part = lax.psum_scatter(grads, 'col', scatter_dimension=1, tiled=True)]
    pallas_call x1, Pallas kernels: 53.9 us -> 96.8 us  [backward_call(): pl.pallas_call(functools.partial(backward_kernel, n_row, cz, cy, images,...]
    psum x1 -> x0, blocking collectives: 40.7 us -> none  [per_device(): small = lax.psum(small, ('row', 'col'))]
    unnamed x16 -> x19, local copies, waits for them, and re-layouts: 2.13 us -> 7.71 us
  transfers between devices with their start and end apart: 2 -> 0, of which waited for: 1 -> 0; matrix products, arithmetic and copies ran while one was open for 1% -> 0% of each run, Pallas kernels for 0% -> 0%
where the time goes in v4:
time: 177 us
  Pallas kernels  163 us (92%)
  local copies, waits for them, and re-layouts  10.5 us (6%)
  between operations  3.18 us (2%)
    pallas_call x1, Pallas kernels, backward_call(): pl.pallas_call(functools.partial(backward_kernel, n_row, cz, cy, images,...  96.8 us
    pallas_call x1, Pallas kernels, forward_call(): pl.pallas_call(functools.partial(forward_kernel, images, ff), out_shape=[...  39.6 us
    pallas_call x1, Pallas kernels, head_call(): pl.pallas_call(functools.partial(head_kernel, n_row, cz, cy, images, ff),...  26.4 us
    unnamed x19, local copies, waits for them, and re-layouts  7.71 us

profile of v4, /device:TPU:0, one launch (start us, length us, event | category | flops | bytes accessed | tf_op | source)
XLA Modules:
  0.0 176.5 jit_solution(4417033150875179905)
XLA Ops:
  0.6 39.6 %block_forward.1 = (bf16[768,832]{1,0:T(8,128)(2,1)}, bf16[9,880,256]{2,1,0:T(8,128)(2,1)}, bf16[12,832,256]{2,1,0:T(8,128)(2,1)}, bf16[768,832]{1,0:T(8,128)(2,...) custom-call(bf16[788,768]{1,0:T(8,128)(2,1)} %tok_ref.1, ...), custom_call_target="tpu_custom_call" | custom-call | tf_op jit(solution)/shard_map/block_forward/pallas_call | solution.py:216
  40.9 26.4 %contrastive_head.1 = (f32[1,1]{1,0:T(1,128)}, f32[8,768]{1,0:T(8,128)}, f32[8,3072]{1,0:T(8,128)}, f32[4,512]{1,0:T(4,128)}, f32[48,512]{1,0:T(8,128)}, /*index=5*/f32[192,768]{1,0:T(8,128)}) custom-call(f32[8,896]{1,0:T(8,128)} %get-tuple-element.34.pooled_ref, bf16[4,512]{1,0:T(4,128)(2,1)} %texts_ref.1, f32[4,8,768]{2,1,0:T(8,128)} %get-tuple-element.35.apool_ref, ...), custom_call_target="tpu_custom_call" | custom-call | tf_op jit(solution)/shard_map/contrastive_head/pallas_call | solution.py:410
  67.4 96.8 %block_backward.1 = (f32[788,768]{1,0:T(8,128)}, f32[48,2304]{1,0:T(8,128)}, f32[48,768]{1,0:T(8,128)}, f32[48,3072]{1,0:T(8,128)}, f32[16,768]{1,0:T(8,128)}) custom-call(f32[8,768]{1,0:T(8,128)} %get-tuple-element.37.dy_ref, f32[8,3072]{1,0:T(8,128)} %get-tuple-element.38.da_ref, f32[8,768]{1,0:T(8,128)} %vec_ref.3, bf16[768,2304]{1,0:T(8,128)(2,1)} %wqkv_h.3, ...), custom_call_target="tpu_custom_call" | custom-call | tf_op jit(solution)/shard_map/block_backward/pallas_call | solution.py:817
  164.2 0.7 slice.6
  164.9 0.7 constant_dynamic-slice_fusion
  165.6 0.7 slice.7
  166.3 0.6 dynamic_slice.7
  167.6 0.0 copy-start.2
  167.7 0.0 copy-start.3
  167.7 0.0 copy-start.1
  167.7 0.0 copy-start
  167.7 3.4 %copy.32 = f32[788,768]{1,0:T(8,128)} copy(f32[788,768]{1,0:T(8,128)} %get-tuple-element.69) | data formatting | bytes 4841472
  171.1 0.0 copy-done.2
  171.1 0.0 copy-start.4
  171.1 0.0 copy-start.5
  171.1 0.8 copy.33
  171.9 0.0 copy-done.3
  171.9 0.7 copy.34
  172.5 0.0 copy-done.1
  172.5 0.8 copy.35
  173.3 0.0 copy-done
  173.3 0.8 copy.36
  174.2 0.0 copy-done.4
  174.2 0.6 copy.37
  174.8 0.0 copy-done.5
  174.8 0.6 copy.38
  (1 shorter events, 0.0 us)
Async XLA Ops:
  167.6 3.4 %copy-start.2 = (f32[48,2304]{1,0:T(8,128)S(1)}, f32[48,2304]{1,0:T(8,128)}, u32[]{:S(2)}) copy-start(f32[48,2304]{1,0:T(8,128)} %get-tuple-element.70) | copy-start | bytes 1327108
  167.7 4.2 %copy-start.3 = (f32[48,768]{1,0:T(8,128)S(1)}, f32[48,768]{1,0:T(8,128)}, u32[]{:S(2)}) copy-start(f32[48,768]{1,0:T(8,128)} %get-tuple-element.71) | copy-start | bytes 442372
  167.7 4.9 %copy-start.1 = (f32[48,3072]{1,0:T(8,128)S(1)}, f32[48,3072]{1,0:T(8,128)}, u32[]{:S(2)}) copy-start(f32[48,3072]{1,0:T(8,128)} %get-tuple-element.72) | copy-start | bytes 1769476
  167.7 5.7 %copy-start = (f32[192,768]{1,0:T(8,128)S(1)}, f32[192,768]{1,0:T(8,128)}, u32[]{:S(2)}) copy-start(f32[192,768]{1,0:T(8,128)} %get-tuple-element.73) | copy-start | bytes 1769476
  171.1 3.1 %copy-start.4 = (f32[48,512]{1,0:T(8,128)S(1)}, f32[48,512]{1,0:T(8,128)}, u32[]{:S(2)}) copy-start(f32[48,512]{1,0:T(8,128)} %get-tuple-element.76) | copy-start | bytes 294916
  171.1 3.7 %copy-start.5 = (f32[4,512]{1,0:T(4,128)S(1)}, f32[4,512]{1,0:T(4,128)}, u32[]{:S(2)}) copy-start(f32[4,512]{1,0:T(4,128)} %get-tuple-element.77) | copy-start | bytes 24580

commit v5 on v4

--- a/solution.py
+++ b/solution.py
@@ -419,13 +419,18 @@
     )(pooled, texts, apool, pair, scale, wproj, wdown)
 
 
+READY = [2, 5, 8, 11, 18, 23, 28, 33]
+WAITS = [[(7, 0), (9, 1), (12, 2), (13, 3), (20, 4), (25, 5), (30, 6), (35, 7)], [(14, 0), (17, 1), (21, 2), (24, 3), (27, 4), (31, 5), (35, 6)], [(19, 0), (21, 1), (26, 2), (27, 3), (32, 4), (35, 5)], [(24, 0), (27, 1), (31, 2), (32, 3), (36, 4)], [(28, 0), (31, 1), (35, 2), (36, 3)]]
+TAIL = [(3, 5), (2, 6), (1, 7), (4, 4), (4, 5), (3, 6), (4, 6), (2, 7), (3, 7), (4, 7)]
+
+
 def backward_kernel(
     n_row, cz, cy, images, ff, n_a,
     dy_ref, da_ref, vec_ref,
     wqkv_h, wout_h, wup_h, h1t_h, qkv_h, p_h, ot_h, h2t_h, xh1_h, xh2_h, rstd1_h, rstd2_h, kcol_h, gk_h,
     tg_ref, qg_ref, og_ref, ug_ref, small_ref,
     wqkv, wout, wup, h1t, qkv, ot, h2t, xh1, xh2, rstd1, rstd2, kcol, p_s, du, dx, db, do_s, dp_s,
-    g, r0, r1a, r1b, r2a, r2b, r3a, r3b, r4b, res, vc, vp, vz,
+    g, r0, r1a, r1b, r2a, r2b, r3a, r3b, r4b, res, vc, vp, vz, sv, small_s,
     in_sem, gk_sem, p_sem, s_sem, r_sem, vs_sem, vr_sem,
 ):
     n_quads = D // TILE
@@ -480,13 +485,11 @@
     bar = pltpu.get_barrier_semaphore()
     for dev in z_devs + p_devs + [core_dev]:
         pl.semaphore_signal(bar, inc=1, device_id=dev, device_id_type=MESH)
-    pl.semaphore_wait(bar, len(z_devs) + len(p_devs) + 1)
-
     half = lambda which: pl.ds(pl.multiple_of(n_a + which * n_h, 128), n_h)
 
     def copies(p, c):
         if p == 0:
-            out = [(g.at[lax.rem(c, 2), :, :, 1 - core], r0.at[c], core_dev)]
+            out = [(g.at[lax.rem(c, 4), :, :, 1 - core], r0.at[c], core_dev)]
         elif p == 1:
             out = [(r0.at[c, :, yy, :, 0:n_a], r1a.at[c, k], dev) for k, (yy, dev) in enumerate(zip(y_peers, y_devs))]
             if two:
@@ -501,24 +504,24 @@
                 out += [(r2b.at[c, 0, zz], r3b.at[c, k], dev) for k, (zz, dev) in enumerate(zip(z_peers, z_devs))]
         else:
             out = [(r3b.at[c, 0], r4b.at[c], x_devs[0])] if two else []
-        base = p * s_sem.shape[1] // 5
+        base = (0, 1, 1 + cy, cz + 2 * cy - 1, 2 * cz + 2 * cy + n_row - 3)[p]
         return [
             pltpu.make_async_remote_copy(
-                src, dst, s_sem.at[c, base + k], r_sem.at[c, base + k], device_id=dev, device_id_type=MESH)
+                src, dst, s_sem.at[lax.rem(c, 4), base + k], r_sem.at[c, base + k], device_id=dev, device_id_type=MESH)
             for k, (src, dst, dev) in enumerate(out)
         ]
 
     def finish(p, c):
         up = lambda v: v.astype(F32)
         if p == 0:
-            r0[c] = (up(r0[c]) + up(g[lax.rem(c, 2), :, :, core])).astype(BF)
+            r0[c] = r0[c] + g[lax.rem(c, 4), :, :, core]
         elif p == 1:
             v = up(r0[c, :, y, :, 0:n_a])
             for k in range(cy - 1):
                 v = v + up(r1a[c, k])
             r1a[c, 0] = v.astype(BF)
             if two:
-                r1b[c] = (up(r1b[c]) + up(r0[c, :, :, :, half(x)])).astype(BF)
+                r1b[c] = r1b[c] + r0[c, :, :, :, half(x)]
         elif p == 2:
             v = up(r1a[c, 0, z])
             for k in range(cz - 1):
@@ -555,59 +558,59 @@
         if p < 4:
             begin(p + 1, c)
 
-    first = n_up + 2
-    last_unit = first + 2 * n_quads + images
-
-    def chunk_at(n):
-        odd = jnp.maximum((n - (n_up - 1)) // 2, 0)
-        return n - odd
-
-    def has_chunk(n):
-        return (n >= 0) & ((n < n_up) | ((lax.rem(n - n_up, 2) == 1) & (n < first + 2 * n_quads)))
+    def lookup(n, events):
+        hit = n < 0
+        c = jnp.int32(0)
+        for at, chunk in events:
+            same = n == at
+            hit = hit | same
+            c = jnp.where(same, chunk, c)
+        return hit, c
 
     def tick(n):
-        @pl.when(has_chunk(n))
-        def _():
-            begin(0, chunk_at(n))
+        @pl.when(n == READY[0])
+        def _():
+            pl.semaphore_wait(bar, len(z_devs) + len(p_devs) + 1)
+
+        hit, c = lookup(n, [(at, k) for k, at in enumerate(READY)])
+
+        @pl.when(hit)
+        def _():
+            begin(0, c)
 
         for p in range(4, -1, -1):
-            m = n - 1 - p
-
-            @pl.when(has_chunk(m))
-            def _(p=p, m=m):
-                advance(p, chunk_at(m))
+            hit, c = lookup(n, WAITS[p])
+
+            @pl.when(hit)
+            def _(p=p, c=c):
+                advance(p, c)
 
     def put(c, tt, part):
         col = pl.multiple_of(tt * TILE, TILE)
-        g[lax.rem(c, 2), :, :, :, :, pl.ds(col, TILE)] = part.reshape(g.shape[1:5] + (TILE,)).astype(BF)
-
-    def unit_up(n):
-        def expand(tt, _):
-            t = n * n_quads + tt
-            col = pl.multiple_of(t * TILE, TILE)
-            gcopy(t).wait()
-            ub = jnp.zeros((1, TILE), F32)
-            for i in range(images):
-                rows = slice(i * ROWS, (i + 1) * ROWS)
-                d = du[rows, pl.ds(col, TILE)].astype(F32) * da_ref[i:i + 1, pl.ds(col, TILE)]
-                ub = ub + jnp.sum(d, axis=0, keepdims=True)
-                du[rows, pl.ds(col, TILE)] = d.astype(BF)
-            scol = pl.multiple_of(tt * TILE, TILE)
-            small_ref[pl.ds(8 + n, 1), pl.ds(scol, TILE)] = ub
-            put(n, tt, mm(h2t[...], du[:, pl.ds(col, TILE)]))
-            return 0
-
-        lax.fori_loop(0, n_quads, expand, 0)
-
-    def unit_down():
-        loads["wup"].wait()
-
-        def down(n, _):
-            col = pl.multiple_of(n * TILE, TILE)
-            dx[:, pl.ds(col, TILE)] = mm(du[...], wup[pl.ds(col, TILE), :], NT)
-            return 0
-
-        lax.fori_loop(0, n_quads, down, 0)
+        g[lax.rem(c, 4), :, :, :, :, pl.ds(col, TILE)] = part.reshape(g.shape[1:5] + (TILE,)).astype(BF)
+
+    def unit_up(t):
+        n = t // n_quads
+        tt = lax.rem(t, n_quads)
+        col = pl.multiple_of(t * TILE, TILE)
+        gcopy(t).wait()
+        ub = jnp.zeros((1, TILE), F32)
+        for i in range(images):
+            rows = slice(i * ROWS, (i + 1) * ROWS)
+            d = du[rows, pl.ds(col, TILE)].astype(F32) * da_ref[i:i + 1, pl.ds(col, TILE)]
+            ub = ub + jnp.sum(d, axis=0, keepdims=True)
+            du[rows, pl.ds(col, TILE)] = d.astype(BF)
+        scol = pl.multiple_of(tt * TILE, TILE)
+        small_s[pl.ds(8 + n, 1), pl.ds(scol, TILE)] = ub
+        put(n, tt, mm(h2t[...], du[:, pl.ds(col, TILE)]))
+
+    def unit_down(n):
+        @pl.when(n == 0)
+        def _():
+            loads["wup"].wait()
+
+        col = pl.multiple_of(n * TILE, TILE)
+        dx[:, pl.ds(col, TILE)] = mm(du[...], wup[pl.ds(col, TILE), :], NT)
 
     def unit_mid():
         for name in ("kcol", "xh2", "rstd2", "wout", "ot"):
@@ -634,65 +637,58 @@
             rb = r.astype(BF)
             db[rows, :] = rb
             bo = bo + jnp.sum(rb.astype(F32), axis=0, keepdims=True)
-        small_ref[0:4, :] = jnp.zeros((4, D), F32)
-        small_ref[4:5, :] = bo
-        small_ref[5:6, :] = g2
-        small_ref[6:7, :] = b2
-        small_ref[7:8, :] = bd
-        for j in range(n_quads):
-            sl = slice(j * TILE, (j + 1) * TILE)
-            do_s[j] = mm(db[...], wout[sl, :], NT).astype(BF)
-            put(n_up, j, mm(ot[...], db[:, sl]))
+        small_s[0:4, :] = jnp.zeros((4, D), F32)
+        small_s[4:5, :] = bo
+        small_s[5:6, :] = g2
+        small_s[6:7, :] = b2
+        small_s[7:8, :] = bd
         for name in ("qkv", "h1t"):
             loads[name].wait()
 
-    def unit_attend(m):
-        j = m // 2
-
-        def attend(ii, _):
-            i = lax.rem(m, 2) * (images // 2) + ii
-            r0_ = pl.multiple_of(i * ROWS, 16)
-            step = j * images + i
-            slot = lax.rem(step, 2)
-
-            @pl.when(step + 1 < n_quads * images)
-            def _():
-                pcopy(step + 1).start()
-
-            pcopy(step).wait()
-            q4 = qkv[j, pl.ds(r0_, ROWS), :]
-            k4 = qkv[n_quads + j, pl.ds(r0_, WIN), :]
-            v4 = qkv[2 * n_quads + j, pl.ds(r0_, WIN), :]
-            d4 = do_s[j, pl.ds(r0_, ROWS), :]
-            dq = jnp.zeros((ROWS, TILE), F32)
-            dk = jnp.zeros((WIN, TILE), F32)
-            dv = jnp.zeros((WIN, TILE), F32)
-            for h, mask in enumerate(masks):
-                pb = p_s[slot, h * ROWS:(h + 1) * ROWS, :]
-                dm = d4 * mask
-                dv = dv + mm(pb, dm, TN)
-                dpr = mm(dm, v4, NT)
-                pf = pb.astype(F32)
-                ds = (pf * (dpr - jnp.sum(pf * dpr, axis=1, keepdims=True))).astype(BF)
-                dq = dq + mm(ds, k4 * mask)
-                dk = dk + mm(ds, q4 * mask, TN)
-            dq = dq * HEAD_DIM ** -0.5
-            dv = dv[0:ROWS]
-            sl = pl.ds(pl.multiple_of(j * TILE, TILE), TILE)
-            small_ref[2:3, sl] += jnp.sum(dq, axis=0, keepdims=True)
-            small_ref[3:4, sl] += jnp.sum(dv, axis=0, keepdims=True)
-            for s, val in enumerate((dq, dk[0:ROWS], dv)):
-                col = pl.multiple_of(s * D + j * TILE, TILE)
-                dp_s[pl.ds(r0_, ROWS), pl.ds(col, TILE)] = val.astype(BF)
-            return 0
-
-        lax.fori_loop(0, images // 2, attend, 0)
-
-        @pl.when(lax.rem(m, 2) == 1)
-        def _():
-            for s in range(3):
-                col = pl.multiple_of(s * D + j * TILE, TILE)
-                put(n_up + 1 + j, s, mm(h1t[...], dp_s[:, pl.ds(col, TILE)]))
+    def unit_out(j):
+        col = pl.multiple_of(j * TILE, TILE)
+        do_s[j] = mm(db[...], wout[pl.ds(col, TILE), :], NT).astype(BF)
+        put(n_up, j, mm(ot[...], db[:, pl.ds(col, TILE)]))
+
+    def unit_attend(j, i):
+        r0_ = pl.multiple_of(i * ROWS, 16)
+        step = j * images + i
+        slot = lax.rem(step, 2)
+
+        @pl.when(step + 1 < n_quads * images)
+        def _():
+            pcopy(step + 1).start()
+
+        pcopy(step).wait()
+        q4 = qkv[j, pl.ds(r0_, ROWS), :]
+        k4 = qkv[n_quads + j, pl.ds(r0_, WIN), :]
+        v4 = qkv[2 * n_quads + j, pl.ds(r0_, WIN), :]
+        d4 = do_s[j, pl.ds(r0_, ROWS), :]
+        dq = jnp.zeros((ROWS, TILE), F32)
+        dk = jnp.zeros((WIN, TILE), F32)
+        dv = jnp.zeros((WIN, TILE), F32)
+        for h, mask in enumerate(masks):
+            pb = p_s[slot, h * ROWS:(h + 1) * ROWS, :]
+            dm = d4 * mask
+            dv = dv + mm(pb, dm, TN)
+            dpr = mm(dm, v4, NT)
+            pf = pb.astype(F32)
+            ds = (pf * (dpr - jnp.sum(pf * dpr, axis=1, keepdims=True))).astype(BF)
+            dq = dq + mm(ds, k4 * mask)
+            dk = dk + mm(ds, q4 * mask, TN)
+        dq = dq * HEAD_DIM ** -0.5
+        dv = dv[0:ROWS]
+        sl = pl.ds(pl.multiple_of(j * TILE, TILE), TILE)
+        small_s[2:3, sl] += jnp.sum(dq, axis=0, keepdims=True)
+        small_s[3:4, sl] += jnp.sum(dv, axis=0, keepdims=True)
+        for s, val in enumerate((dq, dk[0:ROWS], dv)):
+            col = pl.multiple_of(s * D + j * TILE, TILE)
+            dp_s[pl.ds(r0_, ROWS), pl.ds(col, TILE)] = val.astype(BF)
+
+    def unit_weight(j):
+        for s in range(3):
+            col = pl.multiple_of(s * D + j * TILE, TILE)
+            put(n_up + 1 + j, s, mm(h1t[...], dp_s[:, pl.ds(col, TILE)]))
 
     def unit_norm(i):
         @pl.when(i == 0)
@@ -703,8 +699,8 @@
         rows = pl.ds(pl.multiple_of(i * ROWS, 16), ROWS)
         dh = mm(dp_s[rows, :], wqkv[...], NT)
         xh = xh1[rows, :].astype(F32)
-        small_ref[0:1, :] += jnp.sum(dh * xh, axis=0, keepdims=True)
-        small_ref[1:2, :] += jnp.sum(dh, axis=0, keepdims=True)
+        small_s[0:1, :] += jnp.sum(dh * xh, axis=0, keepdims=True)
+        small_s[1:2, :] += jnp.sum(dh, axis=0, keepdims=True)
         c = dh * vec_ref[0:1, :]
         m1 = jnp.mean(c, axis=1, keepdims=True)
         m2 = jnp.mean(c * xh, axis=1, keepdims=True)
@@ -714,40 +710,56 @@
             def _(k=k):
                 tg_ref[k * SEQ:(k + 1) * SEQ, :] = r[0:SEQ]
 
-    small_ref[...] = jnp.zeros_like(small_ref)
+    small_s[...] = jnp.zeros_like(small_s)
     loads["h2t"].wait()
+    t_down = n_ff
+    t_mid = t_down + n_quads
+    t_out = t_mid + 1
+    t_attend = t_out + n_quads
+    t_norm = t_attend + n_quads * (images + 1)
 
     def unit(n, _):
-        @pl.when(n < n_up)
+        @pl.when(n < t_down)
         def _():
             unit_up(n)
 
-        @pl.when(n == n_up)
-        def _():
-            unit_down()
-
-        @pl.when(n == n_up + 1)
+        @pl.when((n >= t_down) & (n < t_mid))
+        def _():
+            unit_down(n - t_down)
+
+        @pl.when(n == t_mid)
         def _():
             unit_mid()
 
-        @pl.when((n >= first) & (n < first + 2 * n_quads))
-        def _():
-            unit_attend(n - first)
-
-        @pl.when(n >= first + 2 * n_quads)
-        def _():
-            unit_norm(n - first - 2 * n_quads)
+        @pl.when((n >= t_out) & (n < t_attend))
+        def _():
+            unit_out(n - t_out)
+
+        m = n - t_attend
+        inner = lax.rem(m, images + 1)
+
+        @pl.when((m >= 0) & (n < t_norm) & (inner < images))
+        def _():
+            unit_attend(m // (images + 1), inner)
+
+        @pl.when((m >= 0) & (n < t_norm) & (inner == images))
+        def _():
+            unit_weight(m // (images + 1))
+
+        @pl.when(n >= t_norm)
+        def _():
+            unit_norm(n - t_norm)
 
         tick(n)
         return 0
 
-    lax.fori_loop(0, last_unit, unit, 0)
-
-    def spread(src, sems, slot, devs):
+    lax.fori_loop(0, t_norm + images, unit, 0)
+
+    def spread(src, dst, slot, devs):
         out = []
         for k, dev in enumerate(devs):
             d = pltpu.make_async_remote_copy(
-                src, src, vs_sem.at[slot, k], vr_sem.at[slot, k], device_id=dev, device_id_type=MESH)
+                src[k], dst, vs_sem.at[slot, k], vr_sem.at[slot, k], device_id=dev, device_id_type=MESH)
             d.start()
             out.append(d)
         return out
@@ -758,24 +770,28 @@
             v = v + ref[k]
         return v
 
-    n = last_unit
-    last_start = first + 2 * n_quads - 1
-    vc[core] = small_ref[...]
-    going = spread(vc.at[core], None, 0, [core_dev])
-    for p in range(n - 1 - last_start, 5):
-        advance(p, n_chunks - 1)
-        for d in going:
-            d.wait()
-        going = []
-        if p == n - 1 - last_start:
-            vp[spot] = total(vc, 2)
-            going = spread(vp.at[spot], None, 1, p_devs)
+    part = D // cz
+    for zz in range(cz):
+        sv[zz, 0:8, 0:part] = small_s[0:8, zz * part:(zz + 1) * part]
+        for k in range(D // part):
+            sv[zz, 8 + k:9 + k, 0:part] = small_s[8 + zz:9 + zz, k * part:(k + 1) * part]
+    vz[z] = sv[z]
+    going = spread([sv.at[zz] for zz in z_peers], vz.at[z], 0, z_devs)
+    for e, (p, c) in enumerate(TAIL):
+        advance(p, c)
+        if e == len(TAIL) // 3:
+            for d in going:
+                d.wait()
+            vp[spot] = total(vz, cz)
+            going = spread([vp.at[spot]] * len(p_devs), vp.at[spot], 1, p_devs)
+        if e == 2 * len(TAIL) // 3:
+            for d in going:
+                d.wait()
+            vc[core] = total(vp, plane)
+            going = spread([vc.at[core]], vc.at[core], 2, [core_dev])
     for d in going:
         d.wait()
-    vz[z] = total(vp, plane)
-    for d in spread(vz.at[z], None, 2, z_devs):
-        d.wait()
-    small_ref[...] = total(vz, cz)
+    small_ref[...] = total(vc, 2)
     for c in range(n_up):
         ug_ref[:, c * D:(c + 1) * D] = res[c]
     og_ref[...] = res[n_up]
@@ -795,23 +811,23 @@
     n_h = max((D - n_a) // 2, 128)
     n_ch = ff // D + 1 + nq
     plane = n_row * cy
-    n_sem = 5 * (max(cy, cz, n_row) - 1 + max(cy, cz))
+    n_sem = 2 * cz + 2 * cy + n_row - 2
     anyspec = pl.BlockSpec(memory_space=pl.ANY)
     vm = pl.BlockSpec(memory_space=pltpu.VMEM)
-    outs = [(images * SEQ, D), (blk, 3 * D), (blk, D), (blk, ff), (16, D)]
+    outs = [(images * SEQ, D), (blk, 3 * D), (blk, D), (blk, ff), (16, 256)]
     B16 = lambda *s: pltpu.VMEM(s, BF)
     B32 = lambda *s: pltpu.VMEM(s, F32)
     scratch = [
         B16(D, 3 * D), B16(D, D), B16(D, ff), B16(D, span), B16(3 * nq, wide, TILE), B16(D, span), B16(D, span),
         B16(span, D), B16(span, D), B32(span, 128), B32(span, 128), B32(span, 128),
         B16(2, 4 * ROWS, TILE), B16(span, ff), B32(span, D), B16(span, D), B16(nq, span, TILE), B16(span, 3 * D),
-        B16(2, cz, cy, 2, blk, D), B16(n_ch, cz, cy, blk, D),
+        B16(4, cz, cy, 2, blk, D), B16(n_ch, cz, cy, blk, D),
         B16(n_ch, cy - 1, cz, blk, n_a), B16(n_ch, cz, cy, blk, n_h),
         B16(n_ch, cz - 1, blk, n_a), B16(n_ch, cy - 1, cz, blk, n_h),
         B16(n_ch, n_row, blk, n_a), B16(n_ch, cz - 1, blk, n_h), B16(n_ch, blk, n_h), B32(n_ch, blk, D),
-        B32(2, 16, D), B32(plane, 16, D), B32(cz, 16, D),
+        B32(2, 16, 256), B32(plane, 16, 256), B32(cz, 16, 256), B32(cz, 16, 256), B32(16, D),
         pltpu.SemaphoreType.DMA((12,)), pltpu.SemaphoreType.DMA((ff // TILE,)), pltpu.SemaphoreType.DMA((2,)),
-        pltpu.SemaphoreType.DMA((n_ch, n_sem)), pltpu.SemaphoreType.DMA((n_ch, n_sem)),
+        pltpu.SemaphoreType.DMA((4, n_sem)), pltpu.SemaphoreType.DMA((n_ch, n_sem)),
         pltpu.SemaphoreType.DMA((3, plane)), pltpu.SemaphoreType.DMA((3, plane)),
     ]
     return pl.pallas_call(
@@ -824,6 +840,56 @@
             vmem_limit_bytes=62 * 2**20, collective_id=1, has_side_effects=True),
         name="block_backward",
     )(dy, da, vec, wqkv, wout, wup, *acts)
+
+
+def finish_kernel(n_col, cz, images, ff, small_ref, *refs):
+    n_big = (len(refs) - 4) // 3
+    big, vec_ref, ub_ref, outs = refs[:n_big], refs[n_big], refs[n_big + 1], refs[n_big + 2:2 * n_big + 2]
+    held, in_sem, out_sem = refs[2 * n_big + 2:-2], refs[-2], refs[-1]
+    moves = []
+    for src, mid, dst in zip(big, held, outs):
+        rows = src.shape[0]
+        step = rows if rows < 400 else 200
+        for at in range(0, rows, step):
+            sl = pl.ds(at, min(step, rows - at))
+            k = len(moves)
+            c = pltpu.make_async_copy(src.at[sl], mid.at[sl], in_sem.at[k])
+            c.start()
+            moves.append((c, pltpu.make_async_copy(mid.at[sl], dst.at[sl], out_sem.at[k])))
+    for c, d in moves:
+        c.wait()
+        d.start()
+    member = lax.rem(lax.axis_index("col"), n_col // cz)
+    part = D // cz
+    values = small_ref[...]
+    src = lax.broadcasted_iota(jnp.int32, (256, 256), 0)
+    lane = lax.broadcasted_iota(jnp.int32, (256, 256), 1)
+    width = D // n_col
+    pick = (src == lane + member * width).astype(F32).astype(BF)
+    vec_ref[...] = mm3(values[0:8], pick)[:, 0:width]
+    n_ub = ff // n_col
+    row = lax.broadcasted_iota(jnp.int32, values.shape, 0)
+    line = jnp.sum(jnp.where(row == 8 + member * n_ub // part, values, 0.0), axis=0, keepdims=True)
+    pick = (src == lane + lax.rem(member * n_ub, part)).astype(F32).astype(BF)
+    ub_ref[...] = mm3(jnp.broadcast_to(line, (8, 256)), pick)[0:1, 0:n_ub]
+    for c, d in moves:
+        d.wait()
+
+
+def finish_call(n_col, images, ff, small, *big):
+    vm = pl.BlockSpec(memory_space=pltpu.VMEM)
+    anyspec = pl.BlockSpec(memory_space=pl.ANY)
+    shapes = [jax.ShapeDtypeStruct((8, D // n_col), F32), jax.ShapeDtypeStruct((1, ff // n_col), F32)]
+    shapes += [jax.ShapeDtypeStruct(b.shape, b.dtype) for b in big]
+    return pl.pallas_call(
+        functools.partial(finish_kernel, n_col, ff // D, images, ff),
+        out_shape=shapes,
+        in_specs=[vm] + [anyspec] * len(big),
+        out_specs=[vm, vm] + [anyspec] * len(big),
+        scratch_shapes=[pltpu.VMEM(b.shape, b.dtype) for b in big] + [pltpu.SemaphoreType.DMA((12,))] * 2,
+        compiler_params=pltpu.CompilerParams(vmem_limit_bytes=62 * 2**20),
+        name="results",
+    )(small, *big)
 
 
 def per_device(
@@ -843,7 +909,6 @@
     images = keep_mask.shape[0]
     ff = w_up.shape[1]
     n_row, shards = lax.axis_size("row"), lax.axis_size("col")
-    mine = lax.axis_index("col")
     acts = forward_call(
         images, ff, tokens, keep_mask, w_qkv, w_out, w_up, w_down, vectors, up_bias.reshape(1, ff)
     )
@@ -853,8 +918,9 @@
     token_grad, qkv_share, out_share, up_share, small = backward_call(
         n_row, shards, images, ff, dy, da, vectors, w_qkv, w_out, w_up, acts[:11]
     )
-    vec_share = lax.dynamic_slice_in_dim(small[:8], mine * (D // shards), D // shards, axis=1)
-    bias_share = lax.dynamic_slice_in_dim(small[8 : 8 + ff // D].reshape(ff), mine * (ff // shards), ff // shards)
+    vec_share, bias_share, token_grad, qkv_share, out_share, up_share, grad_down, grad_proj, text_grad = finish_call(
+        shards, images, ff, small, token_grad, qkv_share, out_share, up_share, grad_down, grad_proj, text_grad
+    )
     return (
         loss.reshape(1),
         token_grad,
@@ -863,7 +929,7 @@
         up_share,
         grad_down,
         vec_share,
-        bias_share,
+        bias_share.reshape(-1),
         grad_proj,
         text_grad,
     )

time: 177 us -> 149 us (0.84)
  Pallas kernels: 163 us -> 146 us
  local copies, waits for them, and re-layouts: 10.5 us -> 0 us
    pallas_call x1, Pallas kernels: 96.8 us -> 74.6 us  [backward_call(): pl.pallas_call(functools.partial(backward_kernel, n_row, cz, cy, images,...]
    unnamed x19 -> x0, local copies, waits for them, and re-layouts: 7.71 us -> none
    pallas_call x0 -> x1, Pallas kernels: none -> 4.94 us  [finish_call(): pl.pallas_call(functools.partial(finish_kernel, n_col, ff // D, images, f...]
where the time goes in v5:
time: 149 us
  Pallas kernels  146 us (98%)
  between operations  3.13 us (2%)
    pallas_call x1, Pallas kernels, backward_call(): pl.pallas_call(functools.partial(backward_kernel, n_row, cz, cy, images,...  74.6 us
    pallas_call x1, Pallas kernels, forward_call(): pl.pallas_call(functools.partial(forward_kernel, images, ff), out_shape=[...  39.7 us
    pallas_call x1, Pallas kernels, head_call(): pl.pallas_call(functools.partial(head_kernel, n_row, cz, cy, images, ff),...  26.4 us
    pallas_call x1, Pallas kernels, finish_call(): pl.pallas_call(functools.partial(finish_kernel, n_col, ff // D, images, f...  4.94 us

profile of v5, /device:TPU:0, one launch (start us, length us, event | category | flops | bytes accessed | tf_op | source)
XLA Modules:
  0.0 148.7 jit_solution(10359331073009547166)
XLA Ops:
  1.3 39.7 %block_forward.1 = (bf16[768,832]{1,0:T(8,128)(2,1)}, bf16[9,880,256]{2,1,0:T(8,128)(2,1)}, bf16[12,832,256]{2,1,0:T(8,128)(2,1)}, bf16[768,832]{1,0:T(8,128)(2,...) custom-call(bf16[788,768]{1,0:T(8,128)(2,1)} %tok_ref.1, ...), custom_call_target="tpu_custom_call" | custom-call | tf_op jit(solution)/shard_map/block_forward/pallas_call | solution.py:216
  41.0 26.4 %contrastive_head.1 = (f32[1,1]{1,0:T(1,128)}, f32[8,768]{1,0:T(8,128)}, f32[8,3072]{1,0:T(8,128)}, f32[4,512]{1,0:T(4,128)}, f32[48,512]{1,0:T(8,128)}, /*index=5*/f32[192,768]{1,0:T(8,128)}) custom-call(f32[8,896]{1,0:T(8,128)} %get-tuple-element.43.pooled_ref, bf16[4,512]{1,0:T(4,128)(2,1)} %texts_ref.1, f32[4,8,768]{2,1,0:T(8,128)} %get-tuple-element.44.apool_ref, ...), custom_call_target="tpu_custom_call" | custom-call | tf_op jit(solution)/shard_map/contrastive_head/pallas_call | solution.py:410
  67.4 74.6 %block_backward.1 = (f32[788,768]{1,0:T(8,128)}, f32[48,2304]{1,0:T(8,128)}, f32[48,768]{1,0:T(8,128)}, f32[48,3072]{1,0:T(8,128)}, f32[16,256]{1,0:T(8,128)}) custom-call(f32[8,768]{1,0:T(8,128)} %get-tuple-element.46.dy_ref, f32[8,3072]{1,0:T(8,128)} %get-tuple-element.47.da_ref, f32[8,768]{1,0:T(8,128)} %vec_ref.3, bf16[768,2304]{1,0:T(8,128)(2,1)} %wqkv_h.3, ...), custom_call_target="tpu_custom_call" | custom-call | tf_op jit(solution)/shard_map/block_backward/pallas_call | solution.py:833
  142.0 4.9 %results.1 = (f32[8,48]{1,0:T(8,128)}, f32[1,192]{1,0:T(1,128)}, f32[788,768]{1,0:T(8,128)}, f32[48,2304]{1,0:T(8,128)}, f32[48,768]{1,0:T(8,128)}, /*index=5*/f...) custom-call(f32[16,256]{1,0:T(8,128)} %get-tuple-element.59.small_ref, ...), custom_call_target="tpu_custom_call" | custom-call | tf_op jit(solution)/shard_map/results/pallas_call | solution.py:884

commit v6 on v5

--- a/solution.py
+++ b/solution.py
@@ -47,7 +47,7 @@
     tok_ref, keep_ref, wqkv_h, wout_h, wup_h, wdown_h, vec_ref, upb_ref,
     h1t_h, qkv_h, p_h, ot_h, h2t_h, xh1_h, xh2_h, rstd1_h, rstd2_h, kcol_h, gk_h, apool_ref, pooled_ref,
     wqkv, wout, wup, wdown, xs, h1t, qkv, p_s, ot, h2t, xh1, xh2, rstd1, rstd2, kcol, gk,
-    h1, o_s, h2, a_s, keep8, kmask, bias, acc,
+    h1, o_s, h2, a_s, a_t, u_a, u_b, keep8, kmask, bias, acc,
     in_sem, out_sem,
 ):
     n_quads = D // TILE
@@ -108,7 +108,7 @@
         qkv[t, 0:span, :] = r.astype(BF)
         return 0
 
-    lax.fori_loop(0, 3 * n_quads, proj, 0)
+    lax.fori_loop(0, 3 * n_quads, proj, 0, unroll=3)
     send(1, qkv, qkv_h)
     masks = head_masks()
 
@@ -131,7 +131,7 @@
         o_s[j, pl.ds(r0, ROWS), :] = out.astype(BF)
         return 0
 
-    lax.fori_loop(0, images * n_quads, attend, 0)
+    lax.fori_loop(0, images * n_quads, attend, 0, unroll=2)
     send(2, p_s, p_h)
     for j in range(n_quads):
         ot[j * TILE:(j + 1) * TILE, :] = o_s[j].T
@@ -160,16 +160,10 @@
     loads[3].wait()
     acc[...] = jnp.zeros_like(acc)
     a_s[span:, :] = jnp.zeros((a_s.shape[0] - span, TILE), BF)
-
-    def feed(t, _):
-        col = pl.multiple_of(t * TILE, TILE)
-        ub = upb_ref[0:1, pl.ds(col, TILE)]
-        for i in range(images):
-            rows = slice(i * ROWS, (i + 1) * ROWS)
-            u = mm(h2[rows, :], wup[:, pl.ds(col, TILE)]) + ub
-            a, g = gelu_pair(u)
-            a_s[rows, :] = a.astype(BF)
-            gk[t, rows, :] = (g * kcol[rows, 0:1]).astype(BF)
+    a_t[span:, :] = jnp.zeros((a_s.shape[0] - span, TILE), BF)
+
+
+    def pool(t, a_s):
         ap = jnp.zeros((kmask.shape[1], TILE), F32)
         for i in range(images):
             ap = ap + mm(kmask[i], a_s[i * ROWS:i * ROWS + WIN, :])
@@ -177,12 +171,34 @@
         apool_ref[t // n_quads, :, pl.ds(at, TILE)] = ap[0:8]
         hi = ap.astype(BF)
         lo = (ap - hi.astype(F32)).astype(BF)
-        w = wdown[pl.ds(col, TILE), :]
-        acc[...] += mm(hi, w) + mm(lo, w)
+        both = mm(jnp.concatenate([hi, lo], axis=0), wdown[pl.ds(pl.multiple_of(t * TILE, TILE), TILE), :])
+        acc[...] += both[0:16] + both[16:32]
+
+    def lift(t, u_s):
+        col = pl.multiple_of(t * TILE, TILE)
+        u_s[...] = mm(h2[...], wup[:, pl.ds(col, TILE)]) + upb_ref[0:1, pl.ds(col, TILE)]
+
+    def bend(t, u_s, a_s):
+        for i in range(images):
+            rows = slice(i * ROWS, (i + 1) * ROWS)
+            a, g = gelu_pair(u_s[rows, :])
+            a_s[rows, :] = a.astype(BF)
+            gk[t, rows, :] = (g * kcol[rows, 0:1]).astype(BF)
         pltpu.make_async_copy(gk.at[t], gk_h.at[t], out_sem.at[7]).start()
+
+    lift(0, u_a)
+
+    def feed(r, _):
+        t = 2 * r
+        lift(t + 1, u_b)
+        bend(t, u_a, a_s)
+        pool(t, a_s)
+        lift(jnp.minimum(t + 2, n_ff - 1), u_a)
+        bend(t + 1, u_b, a_t)
+        pool(t + 1, a_t)
         return 0
 
-    lax.fori_loop(0, n_ff, feed, 0)
+    lax.fori_loop(0, n_ff // 2, feed, 0)
     cnt = jnp.sum(kb, axis=1, keepdims=True)[0:8]
     inv = 1.0 / jnp.maximum(cnt, 1.0)
     pooled_ref[:, 0:D] = (pooled_ref[:, 0:D] + acc[0:8, :]) * inv + vec_ref[7:8, :]
@@ -209,7 +225,7 @@
         pltpu.VMEM(((images - 1) * SEQ + ROWS + 7 & -8, D), F32),
     ] + [pltpu.VMEM(*o) for o in outs[:11]] + [
         pltpu.VMEM((span, D), BF), pltpu.VMEM((nq, span, TILE), BF), pltpu.VMEM((span, D), BF),
-        pltpu.VMEM((wide, TILE), BF), pltpu.VMEM((16, WIN), F32), pltpu.VMEM((images, 16, WIN), BF),
+        pltpu.VMEM((wide, TILE), BF), pltpu.VMEM((wide, TILE), BF), pltpu.VMEM((span, TILE), F32), pltpu.VMEM((span, TILE), F32), pltpu.VMEM((16, WIN), F32), pltpu.VMEM((images, 16, WIN), BF),
         pltpu.VMEM((1, 3 * D), F32), pltpu.VMEM((16, D), F32),
         pltpu.SemaphoreType.DMA((4,)), pltpu.SemaphoreType.DMA((11,)),
     ]
@@ -420,8 +436,8 @@
 
 
 READY = [2, 5, 8, 11, 18, 23, 28, 33]
-WAITS = [[(7, 0), (9, 1), (12, 2), (13, 3), (20, 4), (25, 5), (30, 6), (35, 7)], [(14, 0), (17, 1), (21, 2), (24, 3), (27, 4), (31, 5), (35, 6)], [(19, 0), (21, 1), (26, 2), (27, 3), (32, 4), (35, 5)], [(24, 0), (27, 1), (31, 2), (32, 3), (36, 4)], [(28, 0), (31, 1), (35, 2), (36, 3)]]
-TAIL = [(3, 5), (2, 6), (1, 7), (4, 4), (4, 5), (3, 6), (4, 6), (2, 7), (3, 7), (4, 7)]
+WAITS = [[(6, 0), (9, 1), (12, 2), (13, 3), (20, 4), (25, 5), (30, 6), (35, 7)], [(13, 0), (15, 1), (20, 2), (23, 3), (27, 4), (32, 5), (36, 6)], [(16, 0), (20, 1), (25, 2), (27, 3), (32, 4), (36, 5)], [(24, 0), (25, 1), (29, 2), (33, 3), (36, 4)], [(28, 0), (29, 1), (33, 2), (37, 3)]]
+TAIL = [(1, 7), (4, 4), (3, 5), (2, 6), (4, 5), (2, 7), (3, 6), (4, 6), (3, 7), (4, 7)]
 
 
 def backward_kernel(
@@ -664,18 +680,23 @@
         k4 = qkv[n_quads + j, pl.ds(r0_, WIN), :]
         v4 = qkv[2 * n_quads + j, pl.ds(r0_, WIN), :]
         d4 = do_s[j, pl.ds(r0_, ROWS), :]
+        dp = mm(jnp.concatenate([d4 * mask for mask in masks], axis=0), v4, NT)
+        pb = p_s[slot]
+        pf = pb.astype(F32)
+        ds = (pf * (dp - jnp.sum(pf * dp, axis=1, keepdims=True))).astype(BF)
         dq = jnp.zeros((ROWS, TILE), F32)
-        dk = jnp.zeros((WIN, TILE), F32)
-        dv = jnp.zeros((WIN, TILE), F32)
+        dt = d4.T
+        qt = q4.T
+        dv = []
+        dk = []
         for h, mask in enumerate(masks):
-            pb = p_s[slot, h * ROWS:(h + 1) * ROWS, :]
-            dm = d4 * mask
-            dv = dv + mm(pb, dm, TN)
-            dpr = mm(dm, v4, NT)
-            pf = pb.astype(F32)
-            ds = (pf * (dpr - jnp.sum(pf * dpr, axis=1, keepdims=True))).astype(BF)
-            dq = dq + mm(ds, k4 * mask)
-            dk = dk + mm(ds, q4 * mask, TN)
+            rows = slice(h * ROWS, (h + 1) * ROWS)
+            cut = slice(h * HEAD_DIM, (h + 1) * HEAD_DIM)
+            dq = dq + mm(ds[rows], k4 * mask)
+            dv.append(mm(dt[cut], pb[rows]))
+            dk.append(mm(qt[cut], ds[rows]))
+        dv = jnp.concatenate(dv, axis=0).T
+        dk = jnp.concatenate(dk, axis=0).T
         dq = dq * HEAD_DIM ** -0.5
         dv = dv[0:ROWS]
         sl = pl.ds(pl.multiple_of(j * TILE, TILE), TILE)

time: 149 us -> 136 us (0.913)
  Pallas kernels: 146 us -> 133 us
    pallas_call x1, Pallas kernels: 39.7 us -> 33.1 us  [forward_call(): pl.pallas_call(functools.partial(forward_kernel, images, ff), out_shape=[...]
    pallas_call x1, Pallas kernels: 74.6 us -> 68.4 us  [backward_call(): pl.pallas_call(functools.partial(backward_kernel, n_row, cz, cy, images,...]
where the time goes in v6:
time: 136 us
  Pallas kernels  133 us (98%)
  between operations  3.13 us (2%)
    pallas_call x1, Pallas kernels, backward_call(): pl.pallas_call(functools.partial(backward_kernel, n_row, cz, cy, images,...  68.4 us
    pallas_call x1, Pallas kernels, forward_call(): pl.pallas_call(functools.partial(forward_kernel, images, ff), out_shape=[...  33.1 us
    pallas_call x1, Pallas kernels, head_call(): pl.pallas_call(functools.partial(head_kernel, n_row, cz, cy, images, ff),...  26.4 us
    pallas_call x1, Pallas kernels, finish_call(): pl.pallas_call(functools.partial(finish_kernel, n_col, ff // D, images, f...  4.94 us

profile of v6, /device:TPU:0, one launch (start us, length us, event | category | flops | bytes accessed | tf_op | source)
XLA Modules:
  0.0 136.0 jit_solution(6772993276722603024)
XLA Ops:
  1.3 33.1 %block_forward.1 = (bf16[768,832]{1,0:T(8,128)(2,1)}, bf16[9,880,256]{2,1,0:T(8,128)(2,1)}, bf16[12,832,256]{2,1,0:T(8,128)(2,1)}, bf16[768,832]{1,0:T(8,128)(2,...) custom-call(bf16[788,768]{1,0:T(8,128)(2,1)} %tok_ref.1, ...), custom_call_target="tpu_custom_call" | custom-call | tf_op jit(solution)/shard_map/block_forward/pallas_call | solution.py:232
  34.4 26.4 %contrastive_head.1 = (f32[1,1]{1,0:T(1,128)}, f32[8,768]{1,0:T(8,128)}, f32[8,3072]{1,0:T(8,128)}, f32[4,512]{1,0:T(4,128)}, f32[48,512]{1,0:T(8,128)}, /*index=5*/f32[192,768]{1,0:T(8,128)}) custom-call(f32[8,896]{1,0:T(8,128)} %get-tuple-element.43.pooled_ref, bf16[4,512]{1,0:T(4,128)(2,1)} %texts_ref.1, f32[4,8,768]{2,1,0:T(8,128)} %get-tuple-element.44.apool_ref, ...), custom_call_target="tpu_custom_call" | custom-call | tf_op jit(solution)/shard_map/contrastive_head/pallas_call | solution.py:426
  60.8 68.4 %block_backward.1 = (f32[788,768]{1,0:T(8,128)}, f32[48,2304]{1,0:T(8,128)}, f32[48,768]{1,0:T(8,128)}, f32[48,3072]{1,0:T(8,128)}, f32[16,256]{1,0:T(8,128)}) custom-call(f32[8,768]{1,0:T(8,128)} %get-tuple-element.46.dy_ref, f32[8,3072]{1,0:T(8,128)} %get-tuple-element.47.da_ref, f32[8,768]{1,0:T(8,128)} %vec_ref.3, bf16[768,2304]{1,0:T(8,128)(2,1)} %wqkv_h.3, ...), custom_call_target="tpu_custom_call" | custom-call | tf_op jit(solution)/shard_map/block_backward/pallas_call | solution.py:854
  129.2 4.9 %results.1 = (f32[8,48]{1,0:T(8,128)}, f32[1,192]{1,0:T(1,128)}, f32[788,768]{1,0:T(8,128)}, f32[48,2304]{1,0:T(8,128)}, f32[48,768]{1,0:T(8,128)}, /*index=5*/f...) custom-call(f32[16,256]{1,0:T(8,128)} %get-tuple-element.59.small_ref, ...), custom_call_target="tpu_custom_call" | custom-call | tf_op jit(solution)/shard_map/results/pallas_call | solution.py:905

commit v7 on v6

--- a/solution.py
+++ b/solution.py
@@ -267,7 +267,7 @@
     n_row, cz, cy, images, ff,
     pooled_ref, texts_ref, apool_ref, pair_ref, scale_ref, wproj_ref, wdown_h,
     loss_ref, dy_ref, da_ref, text_ref, proj_ref, down_ref,
-    pg, ax, ag, wdown, p_all, t_all, c_all, a_all, gproj, gdown,
+    pg, tg, ax, ag, wdown, p_all, t_all, c_all, a_all, gproj, gdown,
     in_sem, zs, zr, ps, pr, cs, cr,
 ):
     x, z, y, core = place(cz, cy)
@@ -288,14 +288,14 @@
     for pp in p_peers:
         pl.semaphore_signal(bar, inc=1, device_id=device(pp // cy, z, lax.rem(pp, cy), core), device_id_type=MESH)
     pl.semaphore_signal(bar, inc=1, device_id=device(x, z, y, 1 - core), device_id_type=MESH)
-    mine = jnp.concatenate([
-        pooled_ref[0:images, 0:D],
-        jnp.concatenate([texts_ref[...].astype(F32), pooled_ref[0:images, D:], jnp.zeros((images, D - EMB - 128), F32)], axis=1),
-    ], axis=0)
-    pg[x, z, y, core] = mine
+    pg[x, z, y, core] = jnp.concatenate([pooled_ref[0:images, 0:half], pooled_ref[0:images, half:D]], axis=0)
+    text = texts_ref[...].astype(F32)
+    tg[x, z, y, core] = jnp.concatenate([text[:, k * 128:(k + 1) * 128] for k in range(EMB // 128)], axis=0).astype(BF)
     for g in range(cz):
-        ax[g, 0:images] = apool_ref[g, 0:images, 0:half]
-        ax[g, images:] = apool_ref[g, 0:images, half:]
+        ax[g, 0:images, 0:half] = apool_ref[g, 0:images, 0:half]
+        ax[g, images:, 0:half] = apool_ref[g, 0:images, half:]
+        ax[g, 0:images, half:] = pooled_ref[0:images, D:]
+        ax[g, images:, half:] = pooled_ref[0:images, D:]
     ag[x, z, y, core] = ax[z]
     pl.semaphore_wait(bar, cz - 1 + plane - 1 + 1)
 
@@ -312,24 +312,30 @@
     p_devs = [device(pp // cy, z, lax.rem(pp, cy), core) for pp in p_peers]
     c_devs = [device(x, z, y, 1 - core)]
     own = pg.at[x, z, y, core]
+    own_t = tg.at[x, z, y, core]
     first = stage([own] * len(z_devs), own, (zs, zr), 0, z_devs)
-    first_a = stage([ax.at[zz] for zz in z_peers], ag.at[x, z, y, core], (zs, zr), 1, z_devs)
+    first_t = stage([own_t] * len(z_devs), own_t, (zs, zr), 2, z_devs)
     for c in first:
         c.wait()
     own = pg.at[x, :, y, core]
     second = stage([own] * len(p_devs), own, (ps, pr), 0, p_devs)
+    for c in first_t:
+        c.wait()
+    own_t = tg.at[x, :, y, core]
+    second_t = stage([own_t] * len(p_devs), own_t, (ps, pr), 2, p_devs)
+    first_a = stage([ax.at[zz] for zz in z_peers], ag.at[x, z, y, core], (zs, zr), 1, z_devs)
+    for c in second:
+        c.wait()
+    own = pg.at[:, :, :, core]
+    third = stage([own], own, (cs, cr), 0, c_devs)
+    for c in second_t:
+        c.wait()
+    own_t = tg.at[:, :, :, core]
+    third_t = stage([own_t], own_t, (cs, cr), 2, c_devs)
     for c in first_a:
         c.wait()
     own = ag.at[x, :, y, core]
     second_a = stage([own] * len(p_devs), own, (ps, pr), 1, p_devs)
-    for c in second:
-        c.wait()
-    own = pg.at[:, :, :, core]
-    third = stage([own], own, (cs, cr), 0, c_devs)
-    for c in second_a:
-        c.wait()
-    own = ag.at[:, :, :, core]
-    third_a = stage([own], own, (cs, cr), 1, c_devs)
     for c in third:
         c.wait()
     n_col = cz * cy * 2
@@ -337,15 +343,21 @@
     for d in range(n_row * n_col):
         rows = slice(d * images, (d + 1) * images)
         at = (d // n_col, d % n_col // (2 * cy), d // 2 % cy, d % 2)
-        p_all[rows, :] = pg[at + (slice(0, images), slice(0, D))]
-        t_all[rows, :] = pg[at + (slice(images, 2 * images), slice(0, EMB))]
-        c_all[rows, :] = pg[at + (slice(images, 2 * images), slice(EMB, EMB + 128))]
+        p_all[rows, 0:half] = pg[at + (slice(0, images),)]
+        p_all[rows, half:] = pg[at + (slice(images, 2 * images),)]
     scale = scale_ref[0]
     pooled = p_all[...]
     latent = mm3(pooled, wproj_ref[...])
     norm = lax.rsqrt(jnp.sum(latent * latent, axis=1, keepdims=True) + 1e-6)
     embeds = latent * norm
     eb = embeds.astype(BF)
+    for c in third_t:
+        c.wait()
+    for d in range(n_row * n_col):
+        rows = slice(d * images, (d + 1) * images)
+        text = tg[d // n_col, d % n_col // (2 * cy), d // 2 % cy, d % 2].astype(F32)
+        for k in range(EMB // 128):
+            t_all[rows, k * 128:(k + 1) * 128] = text[k * images:(k + 1) * images]
     tb = t_all[...].astype(BF)
     logits = scale * mm(eb, tb, NT)
     row_max = jnp.max(logits, axis=1, keepdims=True)
@@ -363,23 +375,25 @@
     loss_ref[...] = (0.5 * lse - hits) * (1.0 / n_img)
     de = scale * mm3(grad, tb)
     dz = norm * (de - embeds * jnp.sum(embeds * de, axis=1, keepdims=True))
-    image_grad = mm3(dz, wproj_ref[...], NT) / c_all[:, 0:1]
+    pooled_grad = mm3(dz, wproj_ref[...], NT)
     dev = x * n_col + (z * cy + y) * 2 + core
     want = lax.broadcasted_iota(jnp.int32, (16, n_img), 0) + dev * images
     have = lax.broadcasted_iota(jnp.int32, (16, n_img), 1)
     pick = (want == have).astype(F32).astype(BF)
-    hi, mid, lo = split3(image_grad)
+    hi, mid, lo = split3(pooled_grad)
     dy = (mm(pick, lo) + mm(pick, mid)) + mm(pick, hi)
-    dy_ref[...] = dy[0:8]
-    dyb = dy.astype(BF)
+    dy = dy[0:8] / jnp.maximum(pooled_ref[:, D:D + 1], 1.0)
+    dy_ref[...] = dy
+    dyb = jnp.concatenate([dy, jnp.zeros_like(dy)], axis=0).astype(BF)
+    for c in second_a:
+        c.wait()
+    own = ag.at[:, :, :, core]
+    third_a = stage([own], own, (cs, cr), 1, c_devs)
     load.wait()
 
-    def spread(t, _):
-        col = pl.multiple_of(t * TILE, TILE)
-        da_ref[:, pl.ds(col, TILE)] = mm(dyb, wdown[pl.ds(col, TILE), :], NT)[0:8]
-        return 0
-
-    lax.fori_loop(0, ff // TILE, spread, 0)
+    for t in range(ff // TILE):
+        sl = slice(t * TILE, (t + 1) * TILE)
+        da_ref[:, sl] = mm(dyb, wdown[sl, :], NT)[0:8]
     g_hi, g_mid, g_lo = split3(grad)
     own_grad = (mm(pick, g_lo, NT) + mm(pick, g_mid, NT)) + mm(pick, g_hi, NT)
     text_ref[...] = (scale * mm3(own_grad, eb))[0:images]
@@ -394,8 +408,10 @@
     for d in range(n_row * n_col):
         rows = slice(d * images, (d + 1) * images)
         at = (d // n_col, d % n_col // (2 * cy), d // 2 % cy, d % 2)
-        a_all[rows, 0:half] = ag[at + (slice(0, images),)]
-        a_all[rows, half:] = ag[at + (slice(images, 2 * images),)]
+        a_all[rows, 0:half] = ag[at + (slice(0, images), slice(0, half))]
+        a_all[rows, half:] = ag[at + (slice(images, 2 * images), slice(0, half))]
+        c_all[rows, :] = ag[at + (slice(0, images), slice(half, half + 128))]
+    hi = (pooled_grad / c_all[:, 0:1]).astype(BF)
     acts = a_all[...]
     a_hi = acts.astype(BF)
     a_lo = (acts - a_hi.astype(F32)).astype(BF)
@@ -416,12 +432,13 @@
     plane = n_row * cy
     grid = (n_row, cz, cy, 2, 2 * images)
     scratch = [
-        pltpu.VMEM(grid + (D,), F32), pltpu.VMEM((cz, 2 * images, D // 2), F32), pltpu.VMEM(grid + (D // 2,), F32),
+        pltpu.VMEM(grid + (D // 2,), F32), pltpu.VMEM(grid[:4] + (images * EMB // 128, 128), BF),
+        pltpu.VMEM((cz, 2 * images, D // 2 + 128), F32), pltpu.VMEM(grid + (D // 2 + 128,), F32),
         pltpu.VMEM((ff, D), BF), pltpu.VMEM((n_img, D), F32), pltpu.VMEM((n_img, EMB), F32),
         pltpu.VMEM((n_img, 128), F32), pltpu.VMEM((n_img, D), F32), pltpu.VMEM((D, EMB), F32), pltpu.VMEM((D, D), F32),
-        pltpu.SemaphoreType.DMA((1,)), pltpu.SemaphoreType.DMA((2, cz)), pltpu.SemaphoreType.DMA((2, cz)),
-        pltpu.SemaphoreType.DMA((2, plane)), pltpu.SemaphoreType.DMA((2, plane)),
-        pltpu.SemaphoreType.DMA((2, 1)), pltpu.SemaphoreType.DMA((2, 1)),
+        pltpu.SemaphoreType.DMA((1,)), pltpu.SemaphoreType.DMA((3, cz - 1)), pltpu.SemaphoreType.DMA((3, cz - 1)),
+        pltpu.SemaphoreType.DMA((3, plane - 1)), pltpu.SemaphoreType.DMA((3, plane - 1)),
+        pltpu.SemaphoreType.DMA((3, 1)), pltpu.SemaphoreType.DMA((3, 1)),
     ]
     return pl.pallas_call(
         functools.partial(head_kernel, n_row, cz, cy, images, ff),
@@ -444,8 +461,8 @@
     n_row, cz, cy, images, ff, n_a,
     dy_ref, da_ref, vec_ref,
     wqkv_h, wout_h, wup_h, h1t_h, qkv_h, p_h, ot_h, h2t_h, xh1_h, xh2_h, rstd1_h, rstd2_h, kcol_h, gk_h,
-    tg_ref, qg_ref, og_ref, ug_ref, small_ref,
-    wqkv, wout, wup, h1t, qkv, ot, h2t, xh1, xh2, rstd1, rstd2, kcol, p_s, du, dx, db, do_s, dp_s,
+    tg_h, qg_ref, og_ref, ug_ref, small_ref,
+    tg_ref, wqkv, wout, wup, h1t, qkv, ot, h2t, xh1, xh2, rstd1, rstd2, kcol, p_s, du, dx, db, do_s, dp_s,
     g, r0, r1a, r1b, r2a, r2b, r3a, r3b, r4b, res, vc, vp, vz, sv, small_s,
     in_sem, gk_sem, p_sem, s_sem, r_sem, vs_sem, vr_sem,
 ):
@@ -775,6 +792,8 @@
         return 0
 
     lax.fori_loop(0, t_norm + images, unit, 0)
+    leave = pltpu.make_async_copy(tg_ref, tg_h, in_sem.at[12])
+    leave.start()
 
     def spread(src, dst, slot, devs):
         out = []
@@ -813,6 +832,7 @@
     for d in going:
         d.wait()
     small_ref[...] = total(vc, 2)
+    leave.wait()
     for c in range(n_up):
         ug_ref[:, c * D:(c + 1) * D] = res[c]
     og_ref[...] = res[n_up]
@@ -839,7 +859,7 @@
     B16 = lambda *s: pltpu.VMEM(s, BF)
     B32 = lambda *s: pltpu.VMEM(s, F32)
     scratch = [
-        B16(D, 3 * D), B16(D, D), B16(D, ff), B16(D, span), B16(3 * nq, wide, TILE), B16(D, span), B16(D, span),
+        B32(images * SEQ, D), B16(D, 3 * D), B16(D, D), B16(D, ff), B16(D, span), B16(3 * nq, wide, TILE), B16(D, span), B16(D, span),
         B16(span, D), B16(span, D), B32(span, 128), B32(span, 128), B32(span, 128),
         B16(2, 4 * ROWS, TILE), B16(span, ff), B32(span, D), B16(span, D), B16(nq, span, TILE), B16(span, 3 * D),
         B16(4, cz, cy, 2, blk, D), B16(n_ch, cz, cy, blk, D),
@@ -847,7 +867,7 @@
         B16(n_ch, cz - 1, blk, n_a), B16(n_ch, cy - 1, cz, blk, n_h),
         B16(n_ch, n_row, blk, n_a), B16(n_ch, cz - 1, blk, n_h), B16(n_ch, blk, n_h), B32(n_ch, blk, D),
         B32(2, 16, 256), B32(plane, 16, 256), B32(cz, 16, 256), B32(cz, 16, 256), B32(16, D),
-        pltpu.SemaphoreType.DMA((12,)), pltpu.SemaphoreType.DMA((ff // TILE,)), pltpu.SemaphoreType.DMA((2,)),
+        pltpu.SemaphoreType.DMA((13,)), pltpu.SemaphoreType.DMA((ff // TILE,)), pltpu.SemaphoreType.DMA((2,)),
         pltpu.SemaphoreType.DMA((4, n_sem)), pltpu.SemaphoreType.DMA((n_ch, n_sem)),
         pltpu.SemaphoreType.DMA((3, plane)), pltpu.SemaphoreType.DMA((3, plane)),
     ]
@@ -855,7 +875,7 @@
         functools.partial(backward_kernel, n_row, cz, cy, images, ff, n_a),
         out_shape=[jax.ShapeDtypeStruct(s, F32) for s in outs],
         in_specs=[vm] * 3 + [anyspec] * 14,
-        out_specs=[vm] * len(outs),
+        out_specs=[anyspec] + [vm] * (len(outs) - 1),
         scratch_shapes=scratch,
         compiler_params=pltpu.CompilerParams(
             vmem_limit_bytes=62 * 2**20, collective_id=1, has_side_effects=True),

time: 136 us -> 133 us (0.978)
  Pallas kernels: 133 us -> 129 us
    pallas_call x1, Pallas kernels: 26.4 us -> 23.9 us  [head_call(): pl.pallas_call(functools.partial(head_kernel, n_row, cz, cy, images, ff),...]
where the time goes in v7:
time: 133 us; the launch traced here: 132 us
  Pallas kernels  129 us (97%)
  between operations  3.13 us (2%)
    pallas_call x1, Pallas kernels, backward_call(): pl.pallas_call(functools.partial(backward_kernel, n_row, cz, cy, images,...  67.3 us
    pallas_call x1, Pallas kernels, forward_call(): pl.pallas_call(functools.partial(forward_kernel, images, ff), out_shape=[...  33.1 us
    pallas_call x1, Pallas kernels, head_call(): pl.pallas_call(functools.partial(head_kernel, n_row, cz, cy, images, ff),...  23.9 us
    pallas_call x1, Pallas kernels, finish_call(): pl.pallas_call(functools.partial(finish_kernel, n_col, ff // D, images, f...  4.94 us

profile of v7, /device:TPU:0, one launch (start us, length us, event | category | flops | bytes accessed | tf_op | source)
XLA Modules:
  0.0 132.4 jit_solution(4426940274755641514)
XLA Ops:
  1.3 33.1 %block_forward.1 = (bf16[768,832]{1,0:T(8,128)(2,1)}, bf16[9,880,256]{2,1,0:T(8,128)(2,1)}, bf16[12,832,256]{2,1,0:T(8,128)(2,1)}, bf16[768,832]{1,0:T(8,128)(2,...) custom-call(bf16[788,768]{1,0:T(8,128)(2,1)} %tok_ref.1, ...), custom_call_target="tpu_custom_call" | custom-call | tf_op jit(solution)/shard_map/block_forward/pallas_call | solution.py:232
  34.4 23.9 %contrastive_head.1 = (f32[1,1]{1,0:T(1,128)}, f32[8,768]{1,0:T(8,128)}, f32[8,3072]{1,0:T(8,128)}, f32[4,512]{1,0:T(4,128)}, f32[48,512]{1,0:T(8,128)}, /*index=5*/f32[192,768]{1,0:T(8,128)}) custom-call(f32[8,896]{1,0:T(8,128)} %get-tuple-element.43.pooled_ref, bf16[4,512]{1,0:T(4,128)(2,1)} %texts_ref.1, f32[4,8,768]{2,1,0:T(8,128)} %get-tuple-element.44.apool_ref, ...), custom_call_target="tpu_custom_call" | custom-call | tf_op jit(solution)/shard_map/contrastive_head/pallas_call | solution.py:443
  58.3 67.3 %block_backward.1 = (f32[788,768]{1,0:T(8,128)}, f32[48,2304]{1,0:T(8,128)}, f32[48,768]{1,0:T(8,128)}, f32[48,3072]{1,0:T(8,128)}, f32[16,256]{1,0:T(8,128)}) custom-call(f32[8,768]{1,0:T(8,128)} %get-tuple-element.46.dy_ref, f32[8,3072]{1,0:T(8,128)} %get-tuple-element.47.da_ref, f32[8,768]{1,0:T(8,128)} %vec_ref.3, bf16[768,2304]{1,0:T(8,128)(2,1)} %wqkv_h.3, ...), custom_call_target="tpu_custom_call" | custom-call | tf_op jit(solution)/shard_map/block_backward/pallas_call | solution.py:874
  125.6 4.9 %results.1 = (f32[8,48]{1,0:T(8,128)}, f32[1,192]{1,0:T(1,128)}, f32[788,768]{1,0:T(8,128)}, f32[48,2304]{1,0:T(8,128)}, f32[48,768]{1,0:T(8,128)}, /*index=5*/f...) custom-call(f32[16,256]{1,0:T(8,128)} %get-tuple-element.59.small_ref, ...), custom_call_target="tpu_custom_call" | custom-call | tf_op jit(solution)/shard_map/results/pallas_call | solution.py:925

commit v8 on v7

--- a/solution.py
+++ b/solution.py
@@ -33,7 +33,7 @@
 def gelu_pair(u):
     z = jnp.abs(u)
     t = 1.0 / (1.0 + (0.3275911 * 0.7071067811865476) * z)
-    e = jnp.exp(-0.5 * (u * u))
+    e = jnp.exp2((-0.5 * 1.4426950408889634) * (u * u))
     poly = 0.5 * 1.061405429
     for c in (-1.453152027, 1.421413741, -0.284496736, 0.254829592):
         poly = poly * t + 0.5 * c
@@ -47,7 +47,7 @@
     tok_ref, keep_ref, wqkv_h, wout_h, wup_h, wdown_h, vec_ref, upb_ref,
     h1t_h, qkv_h, p_h, ot_h, h2t_h, xh1_h, xh2_h, rstd1_h, rstd2_h, kcol_h, gk_h, apool_ref, pooled_ref,
     wqkv, wout, wup, wdown, xs, h1t, qkv, p_s, ot, h2t, xh1, xh2, rstd1, rstd2, kcol, gk,
-    h1, o_s, h2, a_s, a_t, u_a, u_b, keep8, kmask, bias, acc,
+    h1, o_s, y_s, h2, a_s, a_t, u_a, u_b, keep8, kmask, bias, acc,
     in_sem, out_sem,
 ):
     n_quads = D // TILE
@@ -128,22 +128,22 @@
             pb = (e * (1.0 / jnp.sum(e, axis=1, keepdims=True))).astype(BF)
             p_s[it, h * ROWS:(h + 1) * ROWS, :] = pb
             out = out + mm(pb, v4 * m)
-        o_s[j, pl.ds(r0, ROWS), :] = out.astype(BF)
+        o_s[pl.ds(r0, ROWS), pl.ds(pl.multiple_of(j * TILE, TILE), TILE)] = out.astype(BF)
         return 0
 
     lax.fori_loop(0, images * n_quads, attend, 0, unroll=2)
     send(2, p_s, p_h)
+    loads[1].wait()
     for j in range(n_quads):
-        ot[j * TILE:(j + 1) * TILE, :] = o_s[j].T
+        sl = slice(j * TILE, (j + 1) * TILE)
+        y_s[:, sl] = mm(o_s[...], wout[:, sl])
+    ot[...] = o_s[...].T
     send(3, ot, ot_h)
-    loads[1].wait()
     pooled_ref[...] = jnp.zeros_like(pooled_ref)
     for i in range(images):
         rows = slice(i * ROWS, (i + 1) * ROWS)
         x = xs[i * SEQ:i * SEQ + ROWS, :]
-        y = x + vec_ref[4:5, :]
-        for j in range(n_quads):
-            y = y + mm(o_s[j, rows, :], wout[j * TILE:(j + 1) * TILE, :])
+        y = x + vec_ref[4:5, :] + y_s[rows, :]
         kc = kcol[rows, 0:1]
         pooled_ref[i:i + 1, 0:D] = jnp.sum(y * kc, axis=0, keepdims=True)
         cen = y - jnp.mean(y, axis=1, keepdims=True)
@@ -224,7 +224,7 @@
         pltpu.VMEM((D, 3 * D), BF), pltpu.VMEM((D, D), BF), pltpu.VMEM((D, ff), BF), pltpu.VMEM((ff, D), BF),
         pltpu.VMEM(((images - 1) * SEQ + ROWS + 7 & -8, D), F32),
     ] + [pltpu.VMEM(*o) for o in outs[:11]] + [
-        pltpu.VMEM((span, D), BF), pltpu.VMEM((nq, span, TILE), BF), pltpu.VMEM((span, D), BF),
+        pltpu.VMEM((span, D), BF), pltpu.VMEM((span, D), BF), pltpu.VMEM((span, D), F32), pltpu.VMEM((span, D), BF),
         pltpu.VMEM((wide, TILE), BF), pltpu.VMEM((wide, TILE), BF), pltpu.VMEM((span, TILE), F32), pltpu.VMEM((span, TILE), F32), pltpu.VMEM((16, WIN), F32), pltpu.VMEM((images, 16, WIN), BF),
         pltpu.VMEM((1, 3 * D), F32), pltpu.VMEM((16, D), F32),
         pltpu.SemaphoreType.DMA((4,)), pltpu.SemaphoreType.DMA((11,)),
@@ -453,8 +453,8 @@
 
 
 READY = [2, 5, 8, 11, 18, 23, 28, 33]
-WAITS = [[(6, 0), (9, 1), (12, 2), (13, 3), (20, 4), (25, 5), (30, 6), (35, 7)], [(13, 0), (15, 1), (20, 2), (23, 3), (27, 4), (32, 5), (36, 6)], [(16, 0), (20, 1), (25, 2), (27, 3), (32, 4), (36, 5)], [(24, 0), (25, 1), (29, 2), (33, 3), (36, 4)], [(28, 0), (29, 1), (33, 2), (37, 3)]]
-TAIL = [(1, 7), (4, 4), (3, 5), (2, 6), (4, 5), (2, 7), (3, 6), (4, 6), (3, 7), (4, 7)]
+WAITS = [[(7, 0), (9, 1), (12, 2), (13, 3), (21, 4), (26, 5), (31, 6), (35, 7)], [(13, 0), (16, 1), (20, 2), (24, 3), (28, 4), (33, 5), (36, 6)], [(16, 0), (22, 1), (24, 2), (29, 3), (32, 4), (36, 5)], [(24, 0), (28, 1), (29, 2), (34, 3), (37, 4)], [(29, 0), (33, 1), (34, 2), (37, 3)]]
+TAIL = [(1, 7), (3, 5), (2, 6), (4, 4), (4, 5), (2, 7), (3, 6), (3, 7), (4, 6), (4, 7)]
 
 
 def backward_kernel(

time: 133 us -> 130 us (0.977)
  Pallas kernels: 129 us -> 126 us
    pallas_call x1, Pallas kernels: 67.3 us -> 65.2 us  [backward_call(): pl.pallas_call(functools.partial(backward_kernel, n_row, cz, cy, images,...]
where the time goes in v8:
time: 130 us
  Pallas kernels  126 us (97%)
  between operations  3.13 us (2%)
    pallas_call x1, Pallas kernels, backward_call(): pl.pallas_call(functools.partial(backward_kernel, n_row, cz, cy, images,...  65.2 us
    pallas_call x1, Pallas kernels, forward_call(): pl.pallas_call(functools.partial(forward_kernel, images, ff), out_shape=[...  32.4 us
    pallas_call x1, Pallas kernels, head_call(): pl.pallas_call(functools.partial(head_kernel, n_row, cz, cy, images, ff),...  23.9 us
    pallas_call x1, Pallas kernels, finish_call(): pl.pallas_call(functools.partial(finish_kernel, n_col, ff // D, images, f...  4.94 us

profile of v8, /device:TPU:0, one launch (start us, length us, event | category | flops | bytes accessed | tf_op | source)
XLA Modules:
  0.0 129.6 jit_solution(7972285570243246666)
XLA Ops:
  1.3 32.4 %block_forward.1 = (bf16[768,832]{1,0:T(8,128)(2,1)}, bf16[9,880,256]{2,1,0:T(8,128)(2,1)}, bf16[12,832,256]{2,1,0:T(8,128)(2,1)}, bf16[768,832]{1,0:T(8,128)(2,...) custom-call(bf16[788,768]{1,0:T(8,128)(2,1)} %tok_ref.1, ...), custom_call_target="tpu_custom_call" | custom-call | tf_op jit(solution)/shard_map/block_forward/pallas_call | solution.py:232
  33.7 23.9 %contrastive_head.1 = (f32[1,1]{1,0:T(1,128)}, f32[8,768]{1,0:T(8,128)}, f32[8,3072]{1,0:T(8,128)}, f32[4,512]{1,0:T(4,128)}, f32[48,512]{1,0:T(8,128)}, /*index=5*/f32[192,768]{1,0:T(8,128)}) custom-call(f32[8,896]{1,0:T(8,128)} %get-tuple-element.43.pooled_ref, bf16[4,512]{1,0:T(4,128)(2,1)} %texts_ref.1, f32[4,8,768]{2,1,0:T(8,128)} %get-tuple-element.44.apool_ref, ...), custom_call_target="tpu_custom_call" | custom-call | tf_op jit(solution)/shard_map/contrastive_head/pallas_call | solution.py:443
  57.6 65.2 %block_backward.1 = (f32[788,768]{1,0:T(8,128)}, f32[48,2304]{1,0:T(8,128)}, f32[48,768]{1,0:T(8,128)}, f32[48,3072]{1,0:T(8,128)}, f32[16,256]{1,0:T(8,128)}) custom-call(f32[8,768]{1,0:T(8,128)} %get-tuple-element.46.dy_ref, f32[8,3072]{1,0:T(8,128)} %get-tuple-element.47.da_ref, f32[8,768]{1,0:T(8,128)} %vec_ref.3, bf16[768,2304]{1,0:T(8,128)(2,1)} %wqkv_h.3, ...), custom_call_target="tpu_custom_call" | custom-call | tf_op jit(solution)/shard_map/block_backward/pallas_call | solution.py:874
  122.8 4.9 %results.1 = (f32[8,48]{1,0:T(8,128)}, f32[1,192]{1,0:T(1,128)}, f32[788,768]{1,0:T(8,128)}, f32[48,2304]{1,0:T(8,128)}, f32[48,768]{1,0:T(8,128)}, /*index=5*/f...) custom-call(f32[16,256]{1,0:T(8,128)} %get-tuple-element.59.small_ref, ...), custom_call_target="tpu_custom_call" | custom-call | tf_op jit(solution)/shard_map/results/pallas_call | solution.py:925
